TPU v7x, 512 devices: a whole 4x4x16 slice. The times are simulated.
512 devices in a mesh: gx: 16 (over x, y), gy: 32 (over z, core).
Axes of the slice: x: 4, y: 4, z: 16, core: 2. Of those that a mesh axis runs over, the one named last changes fastest.
Arguments:
- displacement: float32 [3, 192, 256, 128], P(None, 'gx', 'gy'), may hold values from -6 to 6
- adjoint_load: float32 [3, 192, 256, 128], P(None, 'gx', 'gy'), may hold values from -24 to 24
- density: float32 [192, 256, 128], P('gx', 'gy'), may hold values from 0.1 to 1
- fixed_mask: int32 [192, 256, 128], P('gx', 'gy'), may hold values 0 or 1
- load_nodes: int32 [3, 2048], replicated, may hold values from 0 to 255, as said below
- load_forces: float32 [3, 2048], replicated, may hold values from -16 to 16
Outputs:
- adjoint: float32 [3, 192, 256, 128], P(None, 'gx', 'gy')
- sensitivity: float32 [192, 256, 128], P('gx', 'gy')
Inputs may be any that keep to these rules, and one draw needn't show every extreme that they name: `load_nodes`: row 0 holds x coordinates below 192, row 1 y coordinates below 256, row 2 z coordinates below 128; loads may share a node, and then add.
All inputs are finite; a program needn't handle non-finite values. No bound on the sum of `fixed_mask` on one device may be relied on, other than what follows from the above.
Results may differ from a plain program's by a relative error of at most 0.0003.
Values sent between devices are 32-bit elements; how exact they have to be, the bound alone decides.
No kernel may reach another device: no remote copies, remote signals or barrier semaphores. Data moves between devices by JAX's collectives and lax.ppermute only.
A program may use at most 64 MiB of HBM per device.

v0:
```python
import jax
import jax.numpy as jnp
import numpy as np
from jax import lax
from jax.sharding import PartitionSpec as P

ITERS = 3


POISSON = 0.3
PENALTY = 3.0
SOFT = 0.001
CORNERS = [(a, b, c) for c in (0, 1) for b in (0, 1) for a in (0, 1)]


def with_halo(cells, sides, width):
    for axis, dim in sides:
        count = lax.axis_size(axis)
        ends = count - 1
        head = lax.slice_in_dim(cells, 0, width, axis=dim)
        tail = lax.slice_in_dim(cells, cells.shape[dim] - width, cells.shape[dim], axis=dim)
        cells = jnp.concatenate(
            [
                lax.ppermute(tail, axis, [(i, (i + 1) % count) for i in range(ends)]),
                cells,
                lax.ppermute(head, axis, [((i + 1) % count, i) for i in range(ends)]),
            ],
            axis=dim,
        )
    return cells


def shifted(block, axis, distance):
    devices = range(lax.axis_size(axis))
    route = [(i - distance, i) for i in devices if i - distance in devices]
    return lax.ppermute(block, axis, route)


def element_stiffness():
    lame_first = POISSON / ((1.0 + POISSON) * (1.0 - 2.0 * POISSON))
    shear_mod = 1.0 / (2.0 * (1.0 + POISSON))
    elastic = np.zeros((6, 6))
    elastic[:3, :3] = lame_first
    for axis_number in range(3):
        elastic[axis_number, axis_number] = lame_first + 2.0 * shear_mod
        elastic[axis_number + 3, axis_number + 3] = shear_mod
    points = [0.5 - 0.5 / np.sqrt(3.0), 0.5 + 0.5 / np.sqrt(3.0)]
    matrix = np.zeros((24, 24))
    for point_x in points:
        for point_y in points:
            for point_z in points:
                coords = (point_x, point_y, point_z)
                strain = np.zeros((6, 24))
                for number, corner in enumerate(CORNERS):
                    factors = [coords[d] if corner[d] else 1.0 - coords[d] for d in range(3)]
                    slopes = [1.0 if corner[d] else -1.0 for d in range(3)]
                    derivs = [
                        slopes[0] * factors[1] * factors[2],
                        factors[0] * slopes[1] * factors[2],
                        factors[0] * factors[1] * slopes[2],
                    ]
                    column = 3 * number
                    strain[0, column] = derivs[0]
                    strain[1, column + 1] = derivs[1]
                    strain[2, column + 2] = derivs[2]
                    strain[3, column] = derivs[1]
                    strain[3, column + 1] = derivs[0]
                    strain[4, column + 1] = derivs[2]
                    strain[4, column + 2] = derivs[1]
                    strain[5, column] = derivs[2]
                    strain[5, column + 2] = derivs[0]
                matrix += strain.T @ elastic @ strain / 8.0
    return matrix


def filter_table():
    entries = []
    for offset_x in (-1, 0, 1):
        for offset_y in (-1, 0, 1):
            for offset_z in (-1, 0, 1):
                distance = float(np.sqrt(offset_x**2 + offset_y**2 + offset_z**2))
                result = 1.5 - distance
                if result > 0:
                    entries.append(((offset_x, offset_y, offset_z), result))
    return entries


def smooth(padded, out_x, out_y):
    layers = padded.shape[2]
    deeper = jnp.pad(padded, ((0, 0), (0, 0), (1, 1)))
    summed = jnp.zeros((out_x, out_y, layers), jnp.float32)
    for offset, weight in filter_table():
        summed = (
            summed
            + weight
            * deeper[
                1 + offset[0] : 1 + offset[0] + out_x,
                1 + offset[1] : 1 + offset[1] + out_y,
                1 + offset[2] : 1 + offset[2] + layers,
            ]
        )
    return summed


def domain_mask(first_x, first_y, count_x, count_y, extent_x, extent_y, layers):
    places_x = first_x + jnp.arange(count_x)
    places_y = first_y + jnp.arange(count_y)
    inside_x = (places_x >= 0) & (places_x < extent_x)
    inside_y = (places_y >= 0) & (places_y < extent_y)
    inside = (inside_x[:, None] & inside_y[None, :]).astype(jnp.float32)
    return jnp.broadcast_to(inside[:, :, None], (count_x, count_y, layers))


def corner_stack(padded, span_x, span_y):
    layers = padded.shape[3] - 1
    portions = [padded[:, a : a + span_x, b : b + span_y, c : c + layers] for a, b, c in CORNERS]
    return jnp.concatenate(portions, axis=0)


def element_forces(stiffness, stacked):
    return jnp.dot(stiffness, stacked.reshape(24, -1), precision=lax.Precision.HIGHEST).reshape(
        stacked.shape
    )


def collect_nodes(forces, rows_x, rows_y):
    layers = forces.shape[3]
    summed = jnp.zeros((3, rows_x, rows_y, layers), jnp.float32)
    for number, (a, b, c) in enumerate(CORNERS):
        portion = forces[
            3 * number : 3 * number + 3, 1 - a : 1 - a + rows_x, 1 - b : 1 - b + rows_y, :
        ]
        if c == 1:
            portion = jnp.pad(portion, ((0, 0), (0, 0), (0, 0), (1, 0)))[..., :layers]
        summed = summed + portion
    return summed


def precond_sum(residual, scaled):
    return lax.psum(jnp.sum(residual * scaled), ("gx", "gy"))


def shards(displacement, adjoint_load, density, fixed_mask, load_nodes, load_forces):
    stiffness = jnp.asarray(element_stiffness(), dtype=jnp.float32)
    corner_diag = jnp.diagonal(stiffness)
    rows_x, rows_y, layers = density.shape
    anchor_x = lax.axis_index("gx") * rows_x
    anchor_y = lax.axis_index("gy") * rows_y
    extent_x = rows_x * lax.axis_size("gx")
    extent_y = rows_y * lax.axis_size("gy")
    margin = 2
    padded_rho = with_halo(density, (("gx", 0), ("gy", 1)), 2)
    inside = domain_mask(
        anchor_x - margin,
        anchor_y - margin,
        rows_x + 2 * margin,
        rows_y + 2 * margin,
        extent_x,
        extent_y,
        layers,
    )
    span_x = rows_x + 2 * margin - 2
    span_y = rows_y + 2 * margin - 2
    weights = smooth(inside, span_x, span_y)
    inner_inside = inside[1:-1, 1:-1]
    physical = smooth(padded_rho, span_x, span_y) / (weights + 1.0 - inner_inside)
    modulus = inner_inside * (SOFT + (1.0 - SOFT) * physical**3)
    trim_size = margin - 1
    own_physical = physical[trim_size : trim_size + rows_x, trim_size : trim_size + rows_y]
    own_weights = weights[trim_size : trim_size + rows_x, trim_size : trim_size + rows_y]
    modulus_ext = modulus[: rows_x + 1, : rows_y + 1]
    diag_nodes = collect_nodes(corner_diag[:, None, None, None] * modulus_ext[None], rows_x, rows_y)
    free_nodes = (1 - fixed_mask).astype(jnp.float32)[None]
    diagonal = free_nodes * diag_nodes + (1.0 - free_nodes)
    local_x = load_nodes[0] - anchor_x
    local_y = load_nodes[1] - anchor_y
    is_owned = (local_x >= 0) & (local_x < rows_x) & (local_y >= 0) & (local_y < rows_y)
    safe_x = jnp.where(is_owned, local_x, 0)
    safe_y = jnp.where(is_owned, local_y, 0)
    placed = (
        jnp.zeros((3, rows_x, rows_y, layers), jnp.float32)
        .at[:, safe_x, safe_y, load_nodes[2]]
        .add(load_forces * is_owned.astype(jnp.float32)[None])
    )
    right_side = free_nodes * (adjoint_load + placed)
    adjoint = jnp.zeros_like(right_side)
    residual = right_side
    scaled = residual / diagonal
    direction = scaled
    norm_now = precond_sum(residual, scaled)
    for iteration in range(ITERS):
        padded = with_halo(free_nodes * direction, (("gx", 1), ("gy", 2)), 1)
        padded = jnp.pad(padded, ((0, 0), (0, 0), (0, 0), (0, 1)))
        stacked = corner_stack(padded, rows_x + 1, rows_y + 1)
        product_field = (
            free_nodes
            * collect_nodes(element_forces(stiffness, stacked) * modulus_ext[None], rows_x, rows_y)
            + (1.0 - free_nodes) * direction
        )
        step_size = norm_now / lax.psum(jnp.sum(direction * product_field), ("gx", "gy"))
        adjoint = adjoint + step_size * direction
        if iteration + 1 < ITERS:
            residual = residual - step_size * product_field
            scaled = residual / diagonal
            norm_next = precond_sum(residual, scaled)
            direction = scaled + norm_next / norm_now * direction
            norm_now = norm_next
    both_fields = jnp.concatenate([displacement, adjoint], axis=0)
    column = shifted(both_fields[:, :, :1, :], "gy", -1)
    widened = jnp.concatenate([both_fields, column], axis=2)
    plane_x = shifted(widened[:, :1], "gx", -1)
    extended = jnp.pad(
        jnp.concatenate([widened, plane_x], axis=1), ((0, 0), (0, 0), (0, 0), (0, 1))
    )
    disp_elem = corner_stack(extended[:3], rows_x, rows_y)
    adj_elem = corner_stack(extended[3:], rows_x, rows_y)
    energy = jnp.sum(disp_elem * element_forces(stiffness, adj_elem), axis=0)
    derived = PENALTY * (1.0 - SOFT) * own_physical**2 * energy / own_weights
    padded_sens = with_halo(derived, (("gx", 0), ("gy", 1)), 1)
    sensitivity = smooth(padded_sens, rows_x, rows_y)
    return (adjoint, sensitivity)


def solution(mesh):
    in_specs = (
        P(None, "gx", "gy", None),
        P(None, "gx", "gy", None),
        P("gx", "gy", None),
        P("gx", "gy", None),
        P(),
        P(),
    )
    out_specs = (P(None, "gx", "gy", None), P("gx", "gy", None))
    return jax.shard_map(shards, mesh=mesh, in_specs=in_specs, out_specs=out_specs, check_vma=False)
```

profile of v0, /device:TPU:1, one launch (start us, length us, event | category | flops | bytes accessed | tf_op | source)
XLA Modules:
  0.0 698.7 jit_solution(3124512963751322482)
XLA Ops:
  1.3 4.0 collective-permute-start
  5.4 1.3 collective-permute-start.1
  14.3 6.0 collective-permute-start.3
  20.4 1.9 collective-permute-start.2
  22.4 4.8 copy.12
  27.5 15.8 %scatter_fusion = f32[3,12288]{0,1:T(8,128)} fusion(f32[3,12288]{0,1:T(8,128)} %bitcast.76, s32[2048]{0:T(1024)S(1)} %broadcast_select_fusion, f32[2048,3]{1,0:T(8,128)S(1)} %copy.13), kind=kCustom, calls=%fused_computation.1 | custom fusion | flops 6144 | bytes 81920
  43.2 4.4 copy.14
  48.7 1.0 fusion.53
  50.6 1.3 collective-permute-start.5
  51.9 4.9 collective-permute-start.4
  57.6 3.3 collective-permute-start.7
  60.9 2.3 collective-permute-start.6
  63.2 0.9 collective-permute-done.6
  67.2 0.9 slice_dynamic-update-slice_fusion.19
  68.1 0.9 slice_dynamic-update-slice_fusion.18
  69.0 0.9 slice_dynamic-update-slice_fusion.17
  69.9 0.9 slice_dynamic-update-slice_fusion.16
  70.7 1.8 reshape.187
  72.5 2.4 fusion.149
  75.0 1.5 reshape.188
  76.7 0.9 multiply_reduce_fusion.3
  77.6 113.4 %all-reduce.23 = (f32[]{:T(128)}, f32[]{:T(128)}) all-reduce(f32[]{:T(128)} %get-tuple-element.3, f32[]{:T(128)} %get-tuple-element.2), channel_id=1, replica_groups=mesh['gx'=16,'gy'=32] {'gx','gy'}, use_global_device_ids=true, to_apply=%region_2.3 | all-reduce | flops 2 | bytes 16 | tf_op jit(solution)/shard_map/psum | solution.py:140
  192.9 100.6 %psum.44 = f32[]{:T(128)} all-reduce(f32[]{:T(128)} %get-tuple-element.14), channel_id=1, replica_groups=mesh['gx'=16,'gy'=32] {'gx','gy'}, use_global_device_ids=true, to_apply=%region_6.7 | all-reduce | flops 1 | bytes 8 | tf_op jit(solution)/shard_map/psum | solution.py:140
  294.8 1.3 collective-permute-start.9
  296.1 4.0 collective-permute-start.8
  300.9 3.7 collective-permute-start.11
  304.7 2.7 collective-permute-start.10
  311.2 0.9 slice_dynamic-update-slice_fusion.11
  312.1 0.9 slice_dynamic-update-slice_fusion.10
  313.0 0.9 slice_dynamic-update-slice_fusion.9
  313.9 0.9 slice_dynamic-update-slice_fusion.8
  314.7 1.8 reshape.189
  316.5 2.4 fusion.150
  319.0 1.5 reshape.190
  320.7 0.9 multiply_reduce_fusion.1
  321.6 104.0 %psum.45 = f32[]{:T(128)} all-reduce(f32[]{:T(128)} %get-tuple-element.10), channel_id=1, replica_groups=mesh['gx'=16,'gy'=32] {'gx','gy'}, use_global_device_ids=true, to_apply=%region_8.9 | all-reduce | flops 1 | bytes 8 | tf_op jit(solution)/shard_map/psum | solution.py:200
  427.6 100.4 %psum.46 = f32[]{:T(128)} all-reduce(f32[]{:T(128)} %multiply_reduce_fusion), channel_id=1, replica_groups=mesh['gx'=16,'gy'=32] {'gx','gy'}, use_global_device_ids=true, to_apply=%region_10.11 | all-reduce | flops 1 | bytes 8 | tf_op jit(solution)/shard_map/psum | solution.py:140
  529.4 1.3 collective-permute-start.13
  530.7 4.0 collective-permute-start.12
  535.6 3.7 collective-permute-start.15
  539.3 1.9 collective-permute-start.14
  541.2 1.1 collective-permute-done.14
  546.4 0.9 slice_dynamic-update-slice_fusion.2
  547.3 0.9 slice_dynamic-update-slice_fusion.1
  548.1 0.9 slice_dynamic-update-slice_fusion
  549.0 1.8 reshape.191
  550.8 2.4 fusion.151
  553.2 1.5 reshape.192
  555.9 104.2 %psum.47 = f32[]{:T(128)} all-reduce(f32[]{:T(128)} %fusion.43), channel_id=1, replica_groups=mesh['gx'=16,'gy'=32] {'gx','gy'}, use_global_device_ids=true, to_apply=%region_12.13 | all-reduce | flops 1 | bytes 8 | tf_op jit(solution)/shard_map/psum | solution.py:200
  661.6 2.6 collective-permute-start.16
  664.1 3.7 collective-permute-done.16
  667.9 1.5 collective-permute-start.17
  669.5 1.3 fusion.106
  670.8 1.9 collective-permute-done.17
  673.8 0.9 copy_bitcast_fusion.2
  674.7 1.0 copy_bitcast_fusion
  675.6 3.7 concatenate.160
  679.3 1.8 fusion
  681.1 1.0 slice_divide_fusion
  682.1 1.3 collective-permute-start.19
  683.4 4.0 collective-permute-start.18
  688.1 4.6 collective-permute-start.20
  692.8 1.9 collective-permute-start.21
  694.7 3.0 collective-permute-done.21
  (128 shorter events, 29.9 us)
Async XLA Ops:
  1.3 12.1 %collective-permute-start = (f32[2,8,128]{2,1,0:T(8,128)S(1)}, f32[2,8,128]{2,1,0:T(8,128)S(1)}, u32[]{:S(2)}, u32[]{:S(2)}) collective-permute-start(f32[2,8,128]{2,1,0:T(8,128)S(1)} %get-tuple-element.75), channel_id=1, source_target_pairs={{0,32},{32,64},{64,96},{96,128},{128,160},{160,192},{192,224},{224... | collective-permute-start | bytes 24584 | tf_op jit(solution)/shard_map/ppermute | solution.py:24
  5.4 8.9 %collective-permute-start.1 = (f32[2,8,128]{2,1,0:T(8,128)S(1)}, f32[2,8,128]{2,1,0:T(8,128)S(1)}, u32[]{:S(2)}, u32[]{:S(2)}) collective-permute-start(f32[2,8,128]{2,1,0:T(8,128)S(1)} %get-tuple-element.74), channel_id=1, source_target_pairs={{32,0},{64,32},{96,64},{128,96},{160,128},{192,160},{224,192},{256... | collective-permute-start | bytes 24584 | tf_op jit(solution)/shard_map/ppermute | solution.py:26
  12.6 36.0 %copy-start.6 = (f32[14,10]{1,0:T(8,128)}, f32[14,10]{1,0:T(8,128)S(1)}, u32[]{:S(2)}) copy-start(f32[14,10]{1,0:T(8,128)S(1)} %get-tuple-element.83) | copy-start | bytes 1684
  12.6 36.0 %copy-start.8 = (f32[14,10]{1,0:T(8,128)}, f32[14,10]{1,0:T(8,128)S(1)}, u32[]{:S(2)}) copy-start(f32[14,10]{1,0:T(8,128)S(1)} %get-tuple-element.84) | copy-start | bytes 1684
  12.6 36.0 %copy-start.10 = (f32[14,10]{1,0:T(8,128)}, f32[14,10]{1,0:T(8,128)S(1)}, u32[]{:S(2)}) copy-start(f32[14,10]{1,0:T(8,128)S(1)} %get-tuple-element.85) | copy-start | bytes 1684
  12.6 36.0 %copy-start.12 = (f32[14,10]{1,0:T(8,128)}, f32[14,10]{1,0:T(8,128)S(1)}, u32[]{:S(2)}) copy-start(f32[14,10]{1,0:T(8,128)S(1)} %get-tuple-element.86) | copy-start | bytes 1684
  14.3 34.2 %collective-permute-start.3 = (f32[16,2,128]{2,1,0:T(2,128)S(1)}, f32[16,2,128]{2,1,0:T(2,128)S(1)}, u32[]{:S(2)}, u32[]{:S(2)}) collective-permute-start(f32[16,2,128]{2,1,0:T(2,128)S(1)} %get-tuple-element.67), channel_id=1, source_target_pairs={{1,0},{2,1},{3,2},{4,3},{5,4},{6,5},{7,6},{8,7},{9,8},{10,9},{11,1... | collective-permute-start | bytes 49160 | tf_op jit(solution)/shard_map/ppermute | solution.py:26
  20.4 28.1 %collective-permute-start.2 = (f32[16,2,128]{2,1,0:T(2,128)S(1)}, f32[16,2,128]{2,1,0:T(2,128)S(1)}, u32[]{:S(2)}, u32[]{:S(2)}) collective-permute-start(f32[16,2,128]{2,1,0:T(2,128)S(1)} %get-tuple-element.66), channel_id=1, source_target_pairs={{0,1},{1,2},{2,3},{3,4},{4,5},{5,6},{6,7},{7,8},{8,9},{9,10},{10,1... | collective-permute-start | bytes 49160 | tf_op jit(solution)/shard_map/ppermute | solution.py:24
  43.2 4.4 copy-start
  48.6 1.4 copy-start.3
  49.7 0.6 copy-start.5
  50.6 6.2 collective-permute-start.5
  51.9 5.7 collective-permute-start.4
  57.6 5.6 collective-permute-start.7
  60.9 3.2 collective-permute-start.6
  294.8 5.3 collective-permute-start.9
  296.1 4.8 collective-permute-start.8
  300.9 6.4 collective-permute-start.11
  304.7 3.4 collective-permute-start.10
  529.4 5.3 collective-permute-start.13
  530.7 4.8 collective-permute-start.12
  535.6 5.6 collective-permute-start.15
  539.3 3.1 collective-permute-start.14
  554.9 106.6 %copy-start.2 = (f32[3,12,8,128]{3,2,1,0:T(8,128)S(1)}, f32[3,12,8,128]{3,2,1,0:T(8,128)}, u32[]{:S(2)}) copy-start(f32[3,12,8,128]{3,2,1,0:T(8,128)} %param.7) | copy-start | bytes 442372
  554.9 114.5 %copy-start.4 = (f32[16,12,128]{2,1,0:T(8,128)S(1)}, f32[16,12,128]{2,1,0:T(8,128)}, u32[]{:S(2)}) copy-start(f32[16,12,128]{2,1,0:T(8,128)} %copy-done.3) | copy-start | bytes 294916
  554.9 114.5 %copy-start.7 = (f32[14,10]{1,0:T(8,128)S(1)}, f32[14,10]{1,0:T(8,128)}, u32[]{:S(2)}) copy-start(f32[14,10]{1,0:T(8,128)} %copy-done.6) | copy-start | bytes 1684
  555.0 114.5 %copy-start.9 = (f32[14,10]{1,0:T(8,128)S(1)}, f32[14,10]{1,0:T(8,128)}, u32[]{:S(2)}) copy-start(f32[14,10]{1,0:T(8,128)} %copy-done.8) | copy-start | bytes 1684
  555.0 114.5 %copy-start.11 = (f32[14,10]{1,0:T(8,128)S(1)}, f32[14,10]{1,0:T(8,128)}, u32[]{:S(2)}) copy-start(f32[14,10]{1,0:T(8,128)} %copy-done.10) | copy-start | bytes 1684
  555.0 114.5 %copy-start.13 = (f32[14,10]{1,0:T(8,128)S(1)}, f32[14,10]{1,0:T(8,128)}, u32[]{:S(2)}) copy-start(f32[14,10]{1,0:T(8,128)} %copy-done.12) | copy-start | bytes 1684
  661.5 11.6 %copy-start.1 = (f32[3,12,8,128]{3,2,1,0:T(8,128)}, f32[3,12,8,128]{3,2,1,0:T(8,128)S(1)}, u32[]{:S(2)}) copy-start(f32[3,12,8,128]{3,2,1,0:T(8,128)S(1)} %get-tuple-element.7) | copy-start | bytes 442372
  661.6 6.3 collective-permute-start.16
  667.9 4.8 collective-permute-start.17
  682.1 5.3 collective-permute-start.19
  683.4 4.7 collective-permute-start.18
  688.1 6.5 collective-permute-start.20
  692.8 5.0 collective-permute-start.21
where the time goes:
time: 705 us; the launch traced here: 699 us
  blocking collectives  523 us (74%)
  starting transfers between devices  63.5 us (9%)
  local copies, waits for them, and re-layouts  48.4 us (7%)
  other arithmetic  32.6 us (5%)
  waiting for transfers between devices  14.5 us (2%)
  matrix products  9.08 us (1%)
  between operations  8.05 us (1%)
    psum x3, blocking collectives, precond_sum(): return lax.psum(jnp.sum(residual * scaled), ('gx', 'gy'))  314 us
    psum x2, blocking collectives, shards(): lax.psum(jnp.sum(direction * product_field), ('gx', 'gy'))  208 us
    ppermute x10, starting transfers between devices, with_halo(): lax.ppermute(tail, axis, [(i, (i + 1) % count) for i in range(ends)])  34.3 us
    ppermute x10, starting transfers between devices, with_halo(): lax.ppermute(head, axis, [((i + 1) % count, i) for i in range(ends)])  25.1 us
    unnamed x59, local copies, waits for them, and re-layouts  23.2 us
    unnamed x6, other arithmetic  17.4 us
  transfers between devices with their start and end apart: 22, of which 10 were waited for; matrix products, arithmetic and copies ran while one was open for 5% of the time, Pallas kernels for 0%

commit v1 on v0

v1 whole, which is shorter than its diff:
```python
import functools

import jax
import jax.numpy as jnp
import numpy as np
from jax import lax
from jax.experimental import pallas as pl
from jax.experimental.pallas import tpu as pltpu
from jax.sharding import Mesh, PartitionSpec as P

POISSON = 0.3
PENALTY = 3.0
SOFT = 0.001
CORNERS = [(a, b, c) for c in (0, 1) for b in (0, 1) for a in (0, 1)]
EDGE = float(1.5 - np.sqrt(2.0))

RX, RY, NZ = 12, 8, 128
NI = RX + 8
NJ = 16
LOW_X, UP_X = 20, 27
BLOCKS = 128
F32 = jnp.float32


def element_stiffness():
    lame_first = POISSON / ((1.0 + POISSON) * (1.0 - 2.0 * POISSON))
    shear_mod = 1.0 / (2.0 * (1.0 + POISSON))
    elastic = np.zeros((6, 6))
    elastic[:3, :3] = lame_first
    for axis_number in range(3):
        elastic[axis_number, axis_number] = lame_first + 2.0 * shear_mod
        elastic[axis_number + 3, axis_number + 3] = shear_mod
    points = [0.5 - 0.5 / np.sqrt(3.0), 0.5 + 0.5 / np.sqrt(3.0)]
    matrix = np.zeros((24, 24))
    for point_x in points:
        for point_y in points:
            for point_z in points:
                coords = (point_x, point_y, point_z)
                strain = np.zeros((6, 24))
                for number, corner in enumerate(CORNERS):
                    factors = [coords[d] if corner[d] else 1.0 - coords[d] for d in range(3)]
                    slopes = [1.0 if corner[d] else -1.0 for d in range(3)]
                    derivs = [
                        slopes[0] * factors[1] * factors[2],
                        factors[0] * slopes[1] * factors[2],
                        factors[0] * factors[1] * slopes[2],
                    ]
                    column = 3 * number
                    strain[0, column] = derivs[0]
                    strain[1, column + 1] = derivs[1]
                    strain[2, column + 2] = derivs[2]
                    strain[3, column] = derivs[1]
                    strain[3, column + 1] = derivs[0]
                    strain[4, column + 1] = derivs[2]
                    strain[4, column + 2] = derivs[1]
                    strain[5, column] = derivs[2]
                    strain[5, column + 2] = derivs[0]
                matrix += strain.T @ elastic @ strain / 8.0
    return matrix


def modal_stiffness():
    one = np.array([[1.0, 1.0], [-1.0, 1.0]])
    change = np.zeros((8, 8))
    for row, (a, b, c) in enumerate(CORNERS):
        for column, (p, q, r) in enumerate(CORNERS):
            change[row, column] = one[a, p] * one[b, q] * one[c, r]
    inverse = np.linalg.inv(np.kron(change, np.eye(3)))
    modal = inverse.T @ element_stiffness() @ inverse
    modes = [corner + (d,) for corner in CORNERS for d in range(3)]
    rows = {}
    for i, row in enumerate(modes):
        terms = [(modes[j], float(modal[i, j])) for j in range(24) if abs(modal[i, j]) > 1e-12]
        if terms:
            rows[row] = terms
    return rows


MODAL = modal_stiffness()
CORNER_DIAG = float(element_stiffness()[0, 0])


def pack_x_kernel(load, disp, dens, mask, low, up):
    for c in range(3):
        low[3 * c : 3 * c + 3] = load[c, RX - 3 : RX]
        up[4 * c : 4 * c + 4] = load[c, 0:4]
        low[17 + c] = disp[c, RX - 1]
        up[21 + 2 * c : 23 + 2 * c] = disp[c, 0:2]
    low[9:12] = (1 - mask[RX - 3 : RX]).astype(F32)
    up[12:16] = (1 - mask[0:4]).astype(F32)
    low[12:17] = dens[RX - 5 : RX]
    up[16:21] = dens[0:5]


def loads_kernel(nodes, forces, out):
    first_x = (lax.axis_index("x") * lax.axis_size("y") + lax.axis_index("y")) * RX - 3
    first_y = (lax.axis_index("z") * lax.axis_size("c") + lax.axis_index("c")) * RY
    count = (NI - 1) * RY
    chunk = 256
    place = lax.broadcasted_iota(jnp.int32, (count, chunk), 0)
    depth = lax.broadcasted_iota(jnp.int32, (NZ, chunk), 0)
    total = jnp.zeros((9 * count, NZ), F32)
    for start in range(0, nodes.shape[1], chunk):
        cols = slice(start, start + chunk)
        local_x = nodes[0:1, cols] - first_x
        local_y = nodes[1:2, cols] - first_y
        inside = (local_x >= 0) & (local_x < NI - 1) & (local_y >= 0) & (local_y < RY)
        spot = jnp.where(inside, local_x * RY + local_y, -1)
        hit = place == spot
        layer = jnp.where(depth == nodes[2:3, cols], 1.0, 0.0).astype(jnp.bfloat16)
        parts = []
        for c in range(3):
            rest = forces[c : c + 1, cols]
            for _ in range(3):
                head = rest.astype(jnp.bfloat16).astype(F32)
                rest = rest - head
                parts.append(jnp.where(hit, head, 0.0).astype(jnp.bfloat16))
        total = total + lax.dot_general(
            jnp.concatenate(parts, axis=0),
            layer,
            (((1,), (1,)), ((), ())),
            preferred_element_type=F32,
        )
    for c in range(3):
        base = 3 * c * count
        summed = (
            total[base : base + count]
            + total[base + count : base + 2 * count]
            + total[base + 2 * count : base + 3 * count]
        )
        out[c] = summed.reshape(NI - 1, RY, NZ)


def pack_y_kernel(load, disp, dens, mask, placed, low, up, ld, fr, dn, di, first, second):
    for c in range(3):
        ld[c, 0:3] = low[3 * c : 3 * c + 3] + placed[c, 0:3]
        ld[c, 3 : 3 + RX] = load[c] + placed[c, 3 : 3 + RX]
        ld[c, 3 + RX : 7 + RX] = up[4 * c : 4 * c + 4] + placed[c, 3 + RX : 7 + RX]
        di[c, 0] = low[17 + c]
        di[c, 1 : 1 + RX] = disp[c]
        di[c, 1 + RX : 3 + RX] = up[21 + 2 * c : 23 + 2 * c]
    fr[0:3] = low[9:12]
    fr[3 : 3 + RX] = (1 - mask[...]).astype(F32)
    fr[3 + RX : 7 + RX] = up[12:16]
    dn[0:5] = low[12:17]
    dn[5 : 5 + RX] = dens[...]
    dn[5 + RX : 10 + RX] = up[16:21]
    even = lax.axis_index("c") == 0

    def rows_for_upper(out):
        for c in range(3):
            out[19 * c : 19 * c + 19] = ld[c, :, 4:8]
        out[57:76] = fr[:, 4:8]
        out[76:98] = dn[:, 4:8]
        for p in range(22):
            out[98 + p // 4, p % 4 : p % 4 + 1] = dn[p, 3:4]
        for n in range(45):
            out[104 + n // 4, n % 4 : n % 4 + 1] = di[n // 15, n % 15, 7:8]

    def rows_for_lower(out):
        for c in range(3):
            out[19 * c : 19 * c + 19] = ld[c, :, 0:4]
        out[57:76] = fr[:, 0:4]
        out[76:98] = dn[:, 0:4]
        for p in range(22):
            out[98 + p // 4, p % 4 : p % 4 + 1] = dn[p, 4:5]
        for n in range(45):
            out[104 + n // 2, 2 * (n % 2) : 2 * (n % 2) + 2] = di[n // 15, n % 15, 0:2]

    @pl.when(even)
    def _():
        rows_for_upper(first)
        rows_for_lower(second)

    @pl.when(jnp.logical_not(even))
    def _():
        rows_for_lower(first)
        rows_for_upper(second)


def up_z(v, lane):
    return jnp.where(lane < NZ - 1, pltpu.roll(v, NZ - 1, 1), 0.0)


def down_z(v, lane):
    return jnp.where(lane > 0, pltpu.roll(v, 1, 1), 0.0)


def up_y(v):
    return pltpu.roll(v, NJ - 1, 0)


def down_y(v):
    return pltpu.roll(v, 1, 0)


def gather_yz(v, lane):
    above = up_z(v, lane)
    result = {}
    for c, part in ((0, v + above), (1, above - v)):
        higher = up_y(part)
        result[0, c] = part + higher
        result[1, c] = higher - part
    return result


YZ = [(b, c) for b in (0, 1) for c in (0, 1)]


def main_kernel(ld, fr, dn, di, first, second, basis, senses, sums, LD, FR, DN, DI, MOD, SC, W, Z, G, N, F, DV, HP):
    gx = lax.axis_index("x") * lax.axis_size("y") + lax.axis_index("y")
    gy = lax.axis_index("z") * lax.axis_size("c") + lax.axis_index("c")
    extent_x = RX * lax.axis_size("x") * lax.axis_size("y")
    extent_y = RY * lax.axis_size("z") * lax.axis_size("c")
    lane = lax.broadcasted_iota(jnp.int32, (NJ, NZ), 1)
    row = lax.broadcasted_iota(jnp.int32, (NJ, NZ), 0)

    LD[:, :, 4:12] = ld[...]
    FR[:, 4:12] = fr[...]
    DN[:, 8:16] = dn[...]
    DI[:, :, 4:12] = di[...]
    DI[:, :, 0:4] = jnp.zeros((3, 15, 4, NZ), F32)
    DI[:, :, 12:16] = jnp.zeros((3, 15, 4, NZ), F32)

    def fill(below, above):
        for c in range(3):
            LD[c, :, 0:4] = below[19 * c : 19 * c + 19]
            LD[c, :, 12:16] = above[19 * c : 19 * c + 19]
        FR[:, 0:4] = below[57:76]
        FR[:, 12:16] = above[57:76]
        DN[:, 4:8] = below[76:98]
        DN[:, 16:20] = above[76:98]
        for p in range(22):
            DN[p, 3:4] = below[98 + p // 4, p % 4 : p % 4 + 1]
            DN[p, 20:21] = above[98 + p // 4, p % 4 : p % 4 + 1]
        for n in range(45):
            DI[n // 15, n % 15, 3:4] = below[104 + n // 4, n % 4 : n % 4 + 1]
            DI[n // 15, n % 15, 12:14] = above[104 + n // 2, 2 * (n % 2) : 2 * (n % 2) + 2]

    even = lax.axis_index("c") == 0

    @pl.when(even)
    def _():
        fill(second, first)

    @pl.when(jnp.logical_not(even))
    def _():
        fill(first, second)

    place_y = gy * RY - 4 + row
    inside_y = jnp.where((place_y >= 0) & (place_y < extent_y), 1.0, 0.0)
    near_y = 2.0 - jnp.where(place_y == 0, 1.0, 0.0) - jnp.where(place_y == extent_y - 1, 1.0, 0.0)
    near_z = 2.0 - jnp.where(lane == 0, 1.0, 0.0) - jnp.where(lane == NZ - 1, 1.0, 0.0)
    part_a = 1.5 + 0.5 * (near_y + near_z) + EDGE * near_y * near_z
    part_b = 0.5 + EDGE * (near_y + near_z)

    def filter_parts(p, _):
        cells = DN[p, 4:20]
        beside = DN[p, 3:19] + DN[p, 5:21]
        deep = up_z(cells, lane) + down_z(cells, lane)
        deep_beside = up_z(beside, lane) + down_z(beside, lane)
        N[0, p] = 1.5 * cells + 0.5 * (deep + beside) + EDGE * deep_beside
        N[1, p] = 0.5 * cells + EDGE * (deep + beside)
        return 0

    lax.fori_loop(0, NI + 2, filter_parts, 0)

    def modulus(i, _):
        place_x = gx * RX - 4 + i
        inside_x = jnp.where((place_x >= 0) & (place_x < extent_x), 1.0, 0.0)
        near_x = 2.0 - jnp.where(place_x == 0, 1.0, 0.0) - jnp.where(place_x == extent_x - 1, 1.0, 0.0)
        weights = part_a + near_x * part_b
        physical = (N[0, i + 1] + N[1, i] + N[1, i + 2]) / weights
        squared = physical * physical
        inside = inside_y * inside_x
        mod = inside * (SOFT + (1.0 - SOFT) * squared * physical)
        MOD[i] = mod
        SC[i] = inside * (PENALTY * (1.0 - SOFT)) * squared / weights
        deep = mod + down_z(mod, lane)
        HP[i] = deep + down_y(deep)
        return 0

    lax.fori_loop(0, NI, modulus, 0)

    owned_row = (row >= 4) & (row < 12)
    zero = jnp.zeros((NJ, NZ), F32)

    def store_gather(c, i, v):
        for (b, s), value in gather_yz(v, lane).items():
            G[4 * c + 2 * b + s, i] = value

    def start(i, total):
        diagonal = CORNER_DIAG * (HP[i] + HP[i - 1])
        inverse = jnp.where(FR[i - 1] > 0.5, 1.0 / diagonal, 0.0)
        W[i] = inverse
        own = (i >= 4) & (i < 4 + RX)
        part = zero
        for c in range(3):
            load = LD[c, i - 1]
            z = inverse * load
            Z[0, c, i] = z
            part = part + z * load
            store_gather(c, i, z)
        return total + jnp.where(own, part, 0.0)

    bz = lax.fori_loop(1, NI, start, zero)

    def modes_of(low_plane, high_plane):
        result = {}
        for c in range(3):
            for b, s in YZ:
                near, far = low_plane[c, b, s], high_plane[c, b, s]
                result[0, b, s, c] = near + far
                result[1, b, s, c] = far - near
        return result

    def stiff(modes):
        forces = {}
        for mode, terms in MODAL.items():
            value = None
            for other, factor in terms:
                term = modes[other] * factor
                value = term if value is None else value + term
            forces[mode] = value
        return forces

    def planes_of(ref, i, rows):
        return {(c, b, s): ref[4 * c + 2 * b + s, i, rows] for c in range(3) for b, s in YZ}

    def gather_disp(p, _):
        for c in range(3):
            for (b, s), value in gather_yz(DI[c, p], lane).items():
                N[4 * c + 2 * b + s, p] = value
        return 0

    lax.fori_loop(0, 15, gather_disp, 0)
    numbers = {mode: n for n, mode in enumerate(MODAL)}

    for tile in range(2):
        rows = slice(8 * tile, 8 * tile + 8)

        def disp_forces(p, _, rows=rows):
            forces = stiff(modes_of(planes_of(N, p, rows), planes_of(N, p + 1, rows)))
            for mode, value in forces.items():
                F[numbers[mode], p, rows] = value
            return 0

        lax.fori_loop(0, 14, disp_forces, 0)

    def apply(k):
        begin, end = 1 + k, NI - 1 - k
        for tile in range(2):
            rows = slice(8 * tile, 8 * tile + 8)
            blank = jnp.zeros((8, NZ), F32)

            def elements(i, carry, rows=rows):
                passed = carry
                modes = modes_of(planes_of(G, i, rows), planes_of(G, i + 1, rows))
                young = MOD[i, rows]
                forces = stiff(modes)
                energy = blank
                for mode, n in numbers.items():
                    energy = energy + modes[mode] * F[n, jnp.clip(i - 3, 0, 13), rows]
                DV[k, i, rows] = energy * SC[i, rows]
                following = []
                for c in range(3):
                    for b, s in YZ:
                        slope = forces[1, b, s, c] * young
                        if (0, b, s, c) in forces:
                            level = forces[0, b, s, c] * young
                            low, high = level - slope, level + slope
                        else:
                            low, high = -slope, slope
                        N[4 * c + 2 * b + s, i, rows] = passed[len(following)] + low
                        following.append(high)
                return tuple(following)

            lax.fori_loop(begin, end, elements, (blank,) * 12)

    def image(c, i):
        levels = []
        for b in (0, 1):
            level, slope = N[4 * c + 2 * b, i], N[4 * c + 2 * b + 1, i]
            levels.append(level - slope + down_z(level + slope, lane))
        return levels[0] - levels[1] + down_y(levels[0] + levels[1])

    apply(0)

    def first_image(i, totals):
        own = (i >= 4) & (i < 4 + RX)
        inverse = W[i]
        parts = [zero, zero, zero]
        for c in range(3):
            q = image(c, i)
            z = Z[0, c, i]
            y = inverse * q - z
            Z[1, c, i] = y
            parts = [parts[0] + z * q, parts[1] + y * LD[c, i - 1], parts[2] + y * q]
            store_gather(c, i, y)
        return tuple(t + jnp.where(own, p, 0.0) for t, p in zip(totals, parts))

    h00, b1, h01 = lax.fori_loop(2, NI - 1, first_image, (zero,) * 3)
    apply(1)

    def second_image(i, totals):
        own = (i >= 4) & (i < 4 + RX)
        inverse = W[i]
        parts = [zero, zero, zero]
        for c in range(3):
            q = image(c, i)
            z = Z[1, c, i]
            y = inverse * q - z
            Z[2, c, i] = y
            parts = [parts[0] + z * q, parts[1] + y * LD[c, i - 1], parts[2] + y * q]
            store_gather(c, i, y)
        return tuple(t + jnp.where(own, p, 0.0) for t, p in zip(totals, parts))

    h11, b2, h12 = lax.fori_loop(3, NI - 2, second_image, (zero,) * 3)
    apply(2)

    def third_image(i, totals):
        parts = [zero, zero]
        for c in range(3):
            q = image(c, i)
            parts = [parts[0] + Z[2, c, i] * q, parts[1] + Z[0, c, i] * q]
        return tuple(t + p for t, p in zip(totals, parts))

    h22, h02 = lax.fori_loop(4, 4 + RX, third_image, (zero,) * 2)

    lanes = lax.broadcasted_iota(jnp.int32, (1, NZ), 1)
    line = jnp.zeros((1, NZ), F32)
    for n, value in enumerate((bz, b1, b2, h00, h01, h02, h11, h12, h22)):
        whole = jnp.sum(jnp.where(owned_row, value, 0.0), axis=0, keepdims=True)
        whole = jnp.sum(whole, axis=1, keepdims=True)
        line = line + jnp.where(lanes == n, whole, 0.0)
    for n in range(sums.shape[0]):
        sums[n] = line

    lane8 = lax.broadcasted_iota(jnp.int32, (RY, NZ), 1)
    for k in range(3):

        def sense_parts(i, _, k=k):
            cells = DV[k, i, 4:12]
            beside = DV[k, i, 3:11] + DV[k, i, 5:13]
            deep = up_z(cells, lane8) + down_z(cells, lane8)
            deep_beside = up_z(beside, lane8) + down_z(beside, lane8)
            N[0, i, 0:8] = 1.5 * cells + 0.5 * (deep + beside) + EDGE * deep_beside
            N[1, i, 0:8] = 0.5 * cells + EDGE * (deep + beside)
            return 0

        lax.fori_loop(3, NI - 3, sense_parts, 0)
        for i in range(4, 4 + RX):
            senses[k, i - 4] = N[0, i, 0:8] + N[1, i - 1, 0:8] + N[1, i + 1, 0:8]
    basis[...] = Z[:, :, 4 : 4 + RX, 4:12]


def final_kernel(gathered, basis, senses, adjoint, sensitivity):
    total = jnp.sum(gathered[...], axis=0)

    def value(n):
        return jnp.broadcast_to(total[:, n : n + 1], (1, NZ))

    b0, b1, b2, h00, h01, h02, h11, h12, h22 = [value(n) for n in range(9)]
    l1, l2 = h01 / h00, h02 / h00
    d1 = h11 - l1 * h01
    e = h12 - l1 * h02
    fine1 = d1 > 0.0
    l3 = jnp.where(fine1, e / d1, 0.0)
    d2 = h22 - l2 * h02 - l3 * e
    t1 = b1 - l1 * b0
    t2 = b2 - l2 * b0 - l3 * t1
    c2 = jnp.where(d2 > 0.0, t2 / d2, 0.0)
    c1 = jnp.where(fine1, t1 / d1, 0.0) - l3 * c2
    c0 = b0 / h00 - l1 * c1 - l2 * c2
    adjoint[...] = c0 * basis[0] + c1 * basis[1] + c2 * basis[2]
    sensitivity[...] = c0 * senses[0] + c1 * senses[1] + c2 * senses[2]


VMEM = pl.BlockSpec(memory_space=pltpu.VMEM)


def call(kernel, inputs, outs, scratch=(), limit=None):
    single = not isinstance(outs, list)
    shapes = [outs] if single else outs
    result = pl.pallas_call(
        kernel,
        out_shape=[jax.ShapeDtypeStruct(s, F32) for s in shapes],
        in_specs=[VMEM] * len(inputs),
        out_specs=[VMEM] * len(shapes),
        scratch_shapes=[pltpu.VMEM(s, F32) for s in scratch],
        compiler_params=pltpu.CompilerParams(vmem_limit_bytes=limit or 32 * 1024 * 1024),
    )(*inputs)
    return result[0] if single else result


def shards(displacement, adjoint_load, density, fixed_mask, load_nodes, load_forces):
    gx, gy = ("x", "y"), ("z", "c")
    count_x = lax.axis_size("x") * lax.axis_size("y")
    count_y = lax.axis_size("z") * lax.axis_size("c")
    own = (adjoint_load, displacement, density, fixed_mask)
    low, up = call(pack_x_kernel, own, [(LOW_X, RY, NZ), (UP_X, RY, NZ)])
    low = lax.ppermute(low, gx, [(i, i + 1) for i in range(count_x - 1)])
    up = lax.ppermute(up, gx, [(i + 1, i) for i in range(count_x - 1)])
    placed = call(loads_kernel, (load_nodes, load_forces), (3, NI - 1, RY, NZ))
    ld, fr, dn, di, first, second = call(
        pack_y_kernel,
        own + (placed, low, up),
        [
            (3, NI - 1, RY, NZ),
            (NI - 1, RY, NZ),
            (NI + 2, RY, NZ),
            (3, RX + 3, RY, NZ),
            (BLOCKS, 4, NZ),
            (BLOCKS, 4, NZ),
        ],
    )
    first = lax.ppermute(first, "c", [(0, 1), (1, 0)])
    pairs = [(i, i + 1) for i in range(1, count_y - 1, 2)]
    second = lax.ppermute(second, gy, pairs + [(j, i) for i, j in pairs])
    near = lax.axis_size("c") * count_x
    far = lax.axis_size("z")
    basis, senses, sums = call(
        main_kernel,
        (ld, fr, dn, di, first, second),
        [(3, 3, RX, RY, NZ), (3, RX, RY, NZ), (near, 1, NZ)],
        [
            (3, NI - 1, NJ, NZ),
            (NI - 1, NJ, NZ),
            (NI + 2, 24, NZ),
            (3, RX + 3, NJ, NZ),
            (NI, NJ, NZ),
            (NI, NJ, NZ),
            (NI, NJ, NZ),
            (3, 3, NI, NJ, NZ),
            (12, NI, NJ, NZ),
            (12, NI + 2, NJ, NZ),
            (len(MODAL), 14, NJ, NZ),
            (3, NI, NJ, NZ),
            (NI, NJ, NZ),
        ],
        48 * 1024 * 1024,
    )
    sums = lax.all_to_all(sums, ("x", "y", "c"), 0, 0, tiled=True)
    sums = jnp.broadcast_to(jnp.sum(sums, axis=0, keepdims=True), (far, 1, NZ))
    sums = lax.all_to_all(sums, "z", 0, 0, tiled=True)
    adjoint, sensitivity = call(
        final_kernel, (sums, basis, senses), [(3, RX, RY, NZ), (RX, RY, NZ)]
    )
    return adjoint, sensitivity


def solution(mesh):
    size_x, size_y = mesh.shape["gx"], mesh.shape["gy"]
    side = int(round(size_x**0.5))
    whole = Mesh(
        mesh.devices.reshape(side, size_x // side, size_y // 2, 2), ("x", "y", "z", "c")
    )
    field = P(None, ("x", "y"), ("z", "c"), None)
    grid = P(("x", "y"), ("z", "c"), None)
    return jax.shard_map(
        shards,
        mesh=whole,
        in_specs=(field, field, grid, grid, P(), P()),
        out_specs=(field, grid),
        check_vma=False,
    )
```

time: 705 us -> 89.2 us (0.13)
  blocking collectives: 523 us -> 38.5 us
  starting transfers between devices: 63.5 us -> 17 us
  local copies, waits for them, and re-layouts: 48.4 us -> 3.45 us
  other arithmetic: 32.6 us -> 0.05 us
  Pallas kernels: 0 us -> 23.1 us
  matrix products: 9.08 us -> 0 us
  waiting for transfers between devices: 14.5 us -> 5.76 us
  between operations: 8.05 us -> 0.79 us
    psum x5 -> x0, blocking collectives: 523 us -> none  [the longest x3 314 us: precond_sum(): return lax.psum(jnp.sum(residual * scaled), ('gx', 'gy'))]
    ppermute x22 -> x4, starting transfers between devices: 63.5 us -> 17 us  [the longest x1 8.9 us: shards(): first = lax.ppermute(first, 'c', [(0, 1), (1, 0)])]
    all_to_all x0 -> x2, blocking collectives: none -> 38.5 us  [the longest x1 27.1 us: shards(): sums = lax.all_to_all(sums, 'z', 0, 0, tiled=True)]
    pallas_call x0 -> x5, Pallas kernels: none -> 23.1 us  [call(): pl.pallas_call(kernel, out_shape=[jax.ShapeDtypeStruct(s, F32) for s in s...]
    unnamed x59 -> x20, local copies, waits for them, and re-layouts: 23.2 us -> 3.44 us
    unnamed x6 -> x0, other arithmetic: 17.4 us -> none
    reshape x6 -> x0, local copies, waits for them, and re-layouts: 9.82 us -> none  [the longest x3 5.34 us: element_forces(): stacked.reshape(24, -1)]
    dot_general x4 -> x0, matrix products: 9.08 us -> none  [element_forces(): jnp.dot(stiffness, stacked.reshape(24, -1), precision=lax.Precision.HIGHEST)]
  transfers between devices with their start and end apart: 22 -> 4, of which waited for: 10 -> 1; matrix products, arithmetic and copies ran while one was open for 5% -> 0% of each run, Pallas kernels for 0% -> 2%
where the time goes in v1:
time: 89.2 us; the launch traced here: 88.8 us
  blocking collectives  38.5 us (43%)
  Pallas kernels  23.1 us (26%)
  starting transfers between devices  17 us (19%)
  waiting for transfers between devices  5.76 us (6%)
  local copies, waits for them, and re-layouts  3.45 us (4%)
    all_to_all x1, blocking collectives, shards(): sums = lax.all_to_all(sums, 'z', 0, 0, tiled=True)  27.1 us
    pallas_call x5, Pallas kernels, call(): pl.pallas_call(kernel, out_shape=[jax.ShapeDtypeStruct(s, F32) for s in s...  23.1 us
    all_to_all x1, blocking collectives, shards(): sums = lax.all_to_all(sums, ('x', 'y', 'c'), 0, 0, tiled=True)  11.4 us
    ppermute x1, starting transfers between devices, shards(): first = lax.ppermute(first, 'c', [(0, 1), (1, 0)])  8.9 us
    ppermute x1, waiting for transfers between devices, shards(): second = lax.ppermute(second, gy, pairs + [(j, i) for i, j in pairs])  5.75 us
    ppermute x1, starting transfers between devices, shards(): low = lax.ppermute(low, gx, [(i, i + 1) for i in range(count_x - 1)])  4.79 us
    unnamed x20, local copies, waits for them, and re-layouts  3.44 us
    ppermute x1, starting transfers between devices, shards(): second = lax.ppermute(second, gy, pairs + [(j, i) for i, j in pairs])  1.92 us
  transfers between devices with their start and end apart: 4, of which 1 were waited for; matrix products, arithmetic and copies ran while one was open for 0% of the time, Pallas kernels for 2%

profile of v1, /device:TPU:1, one launch (start us, length us, event | category | flops | bytes accessed | tf_op | source)
XLA Modules:
  0.0 88.8 jit_solution(7032884646234651179)
XLA Ops:
  0.6 0.0 copy-start
  0.6 0.9 %copy-done = f32[3,12,8,128]{3,2,1,0:T(8,128)S(1)} copy-done((f32[3,12,8,128]{3,2,1,0:T(8,128)S(1)}, f32[3,12,8,128]{3,2,1,0:T(8,128)}, u32[]{:S(2)}) %copy-start) | copy-done | bytes 147480
  1.5 0.0 copy-start.2
  1.5 0.9 %copy-done.2 = f32[3,12,8,128]{3,2,1,0:T(8,128)S(1)} copy-done((f32[3,12,8,128]{3,2,1,0:T(8,128)S(1)}, f32[3,12,8,128]{3,2,1,0:T(8,128)}, u32[]{:S(2)}) %copy-start.2) | copy-done | bytes 147480
  2.5 0.0 copy-start.4
  2.5 0.8 copy-done.4
  3.3 0.0 copy-start.6
  3.3 0.8 copy-done.6
  4.1 0.0 copy-start.8
  4.1 0.0 copy-start.9
  4.1 0.0 copy-start.5
  4.1 0.0 copy-start.7
  4.1 1.4 %collective-permute-start.1 = (f32[27,8,128]{2,1,0:T(8,128)S(1)}, f32[27,8,128]{2,1,0:T(8,128)S(1)}, u32[]{:S(2)}, u32[]{:S(2)}) collective-permute-start(f32[27,8,128]{2,1,0:T(8,128)S(1)} %get-tuple-element.14), channel_id=1, source_target_pairs={{32,0},{64,32},{96,64},{128,96},{160,128},{192,160},{224,192},{256... | collective-permute-start | bytes 331784 | tf_op jit(solution)/shard_map/ppermute | solution.py:503
  5.5 0.0 copy-start.1
  5.5 0.0 copy-start.3
  5.5 4.8 %collective-permute-start = (f32[20,8,128]{2,1,0:T(8,128)S(1)}, f32[20,8,128]{2,1,0:T(8,128)S(1)}, u32[]{:S(2)}, u32[]{:S(2)}) collective-permute-start(f32[20,8,128]{2,1,0:T(8,128)S(1)} %get-tuple-element.13), channel_id=1, source_target_pairs={{0,32},{32,64},{64,96},{96,128},{128,160},{160,192},{192,224},{224... | collective-permute-start | bytes 245768 | tf_op jit(solution)/shard_map/ppermute | solution.py:502
  10.3 0.0 copy-done.8
  10.4 0.0 copy-done.9
  10.4 1.8 %shard_map.77.placed = f32[3,19,8,128]{3,2,1,0:T(8,128)S(1)} custom-call(s32[3,2048]{1,0:T(4,128)S(1)} %copy-done.8, f32[3,2048]{1,0:T(4,128)S(1)} %copy-done.9), custom_call_target="tpu_custom_call" | custom-call | tf_op jit(solution)/shard_map/pallas_call | solution.py:485
  12.1 0.0 collective-permute-done.low
  12.1 0.0 collective-permute-done.1.up
  12.1 0.0 copy-done.5
  12.2 0.0 copy-done.7
  12.2 0.0 copy-done.1
  12.2 0.0 copy-done.3
  12.2 0.2 shard_map.79
  12.4 8.9 %collective-permute-start.2 = (f32[128,4,128]{2,1,0:T(4,128)S(1)}, f32[128,4,128]{2,1,0:T(4,128)S(1)}, u32[]{:S(2)}, u32[]{:S(2)}) collective-permute-start(f32[128,4,128]{2,1,0:T(4,128)S(1)} %get-tuple-element.19), channel_id=1, source_target_pairs={{0,1},{1,0},{2,3},{3,2},{4,5},{5,4},{6,7},{7,6},{8,9},{9,8},{10,11... | collective-permute-start | bytes 786440 | tf_op jit(solution)/shard_map/ppermute | solution.py:517
  21.3 1.9 %collective-permute-start.3 = (f32[128,4,128]{2,1,0:T(4,128)S(1)}, f32[128,4,128]{2,1,0:T(4,128)S(1)}, u32[]{:S(2)}, u32[]{:S(2)}) collective-permute-start(f32[128,4,128]{2,1,0:T(4,128)S(1)} %get-tuple-element.20), channel_id=1, source_target_pairs={{1,2},{3,4},{5,6},{7,8},{9,10},{11,12},{13,14},{15,16},{17,18},{19... | collective-permute-start | bytes 786440 | tf_op jit(solution)/shard_map/ppermute | solution.py:519
  23.2 0.0 collective-permute-done.2.first
  23.2 5.8 %collective-permute-done.3.second = f32[128,4,128]{2,1,0:T(4,128)S(1)} collective-permute-done((f32[128,4,128]{2,1,0:T(4,128)S(1)}, f32[128,4,128]{2,1,0:T(4,128)S(1)}, u32[]{:S(2)}, u32[]{:S(2)}) %collective-permute-start.3) | collective-permute-done | bytes 262176 | tf_op jit(solution)/shard_map/ppermute | solution.py:519
  29.0 20.4 %shard_map.80 = (f32[3,3,12,8,128]{4,3,2,1,0:T(8,128)S(1)}, f32[3,12,8,128]{3,2,1,0:T(8,128)S(1)}, f32[32,1,128]{2,1,0:T(1,128)S(1)}) custom-call(f32[3,19,8,128]{3,2,1,0:T(8,128)S(1)} %get-tuple-element.15.ld, f32[19,8,128]{2,1,0:T(8,128)S(1)} %get-tuple-element.16.fr, f32[22,8,128]{2,1,0:T(8,128)S(1)} %get-tuple-element.17.dn, ...), custom_call_target="tpu_custom_call" | custom-call | tf_op jit(solution)/shard_map/pallas_call | solution.py:485
  49.4 11.4 %all_to_all.10 = f32[32,1,128]{2,1,0:T(1,128)S(1)} all-to-all(f32[32,1,128]{2,1,0:T(1,128)S(1)} %get-tuple-element.21), channel_id=1, replica_groups=mesh['x'=4,'y'=4,'z'=16,'c'=2] {'x','y','c'}, dimensions={0} | all-to-all | bytes 32768 | tf_op jit(solution)/shard_map/all_to_all | solution.py:543
  60.8 0.1 reduce_sum.9
  60.8 27.1 %all_to_all.11.gathered = f32[16,1,128]{2,1,0:T(1,128)S(1)} all-to-all(f32[16,1,128]{2,1,0:T(1,128)S(1)} %broadcast_in_dim.2), channel_id=1, replica_groups=mesh['x'=4,'y'=4,'z'=16,'c'=2] {'z'}, dimensions={0} | all-to-all | bytes 16384 | tf_op jit(solution)/shard_map/all_to_all | solution.py:545
  88.0 0.8 shard_map.81
  (2 shorter events, 0.0 us)
Async XLA Ops:
  0.6 0.9 %copy-start = (f32[3,12,8,128]{3,2,1,0:T(8,128)S(1)}, f32[3,12,8,128]{3,2,1,0:T(8,128)}, u32[]{:S(2)}) copy-start(f32[3,12,8,128]{3,2,1,0:T(8,128)} %load.3) | copy-start | bytes 442372
  1.5 0.9 %copy-start.2 = (f32[3,12,8,128]{3,2,1,0:T(8,128)S(1)}, f32[3,12,8,128]{3,2,1,0:T(8,128)}, u32[]{:S(2)}) copy-start(f32[3,12,8,128]{3,2,1,0:T(8,128)} %disp.3) | copy-start | bytes 442372
  2.5 0.8 copy-start.4
  3.3 0.8 copy-start.6
  4.1 6.3 %copy-start.8 = (s32[3,2048]{1,0:T(4,128)S(1)}, s32[3,2048]{1,0:T(4,128)}, u32[]{:S(2)}) copy-start(s32[3,2048]{1,0:T(4,128)} %nodes.1) | copy-start | bytes 73732
  4.1 6.3 %copy-start.9 = (f32[3,2048]{1,0:T(4,128)S(1)}, f32[3,2048]{1,0:T(4,128)}, u32[]{:S(2)}) copy-start(f32[3,2048]{1,0:T(4,128)} %forces.1) | copy-start | bytes 73732
  4.1 8.1 %copy-start.5 = (f32[12,8,128]{2,1,0:T(8,128)S(1)}, f32[12,8,128]{2,1,0:T(8,128)}, u32[]{:S(2)}) copy-start(f32[12,8,128]{2,1,0:T(8,128)} %dens.3) | copy-start | bytes 147460
  4.1 8.1 %copy-start.7 = (s32[12,8,128]{2,1,0:T(8,128)S(1)}, s32[12,8,128]{2,1,0:T(8,128)}, u32[]{:S(2)}) copy-start(s32[12,8,128]{2,1,0:T(8,128)} %mask.3) | copy-start | bytes 147460
  4.1 8.0 %collective-permute-start.1 = (f32[27,8,128]{2,1,0:T(8,128)S(1)}, f32[27,8,128]{2,1,0:T(8,128)S(1)}, u32[]{:S(2)}, u32[]{:S(2)}) collective-permute-start(f32[27,8,128]{2,1,0:T(8,128)S(1)} %get-tuple-element.14), channel_id=1, source_target_pairs={{32,0},{64,32},{96,64},{128,96},{160,128},{192,160},{224,192},{256... | collective-permute-start | bytes 331784 | tf_op jit(solution)/shard_map/ppermute | solution.py:503
  5.5 6.6 %copy-start.1 = (f32[3,12,8,128]{3,2,1,0:T(8,128)S(1)}, f32[3,12,8,128]{3,2,1,0:T(8,128)}, u32[]{:S(2)}) copy-start(f32[3,12,8,128]{3,2,1,0:T(8,128)} %load.3) | copy-start | bytes 442372
  5.5 6.6 %copy-start.3 = (f32[3,12,8,128]{3,2,1,0:T(8,128)S(1)}, f32[3,12,8,128]{3,2,1,0:T(8,128)}, u32[]{:S(2)}) copy-start(f32[3,12,8,128]{3,2,1,0:T(8,128)} %disp.3) | copy-start | bytes 442372
  5.5 6.6 %collective-permute-start = (f32[20,8,128]{2,1,0:T(8,128)S(1)}, f32[20,8,128]{2,1,0:T(8,128)S(1)}, u32[]{:S(2)}, u32[]{:S(2)}) collective-permute-start(f32[20,8,128]{2,1,0:T(8,128)S(1)} %get-tuple-element.13), channel_id=1, source_target_pairs={{0,32},{32,64},{64,96},{96,128},{128,160},{160,192},{192,224},{224... | collective-permute-start | bytes 245768 | tf_op jit(solution)/shard_map/ppermute | solution.py:502
  12.4 10.8 %collective-permute-start.2 = (f32[128,4,128]{2,1,0:T(4,128)S(1)}, f32[128,4,128]{2,1,0:T(4,128)S(1)}, u32[]{:S(2)}, u32[]{:S(2)}) collective-permute-start(f32[128,4,128]{2,1,0:T(4,128)S(1)} %get-tuple-element.19), channel_id=1, source_target_pairs={{0,1},{1,0},{2,3},{3,2},{4,5},{5,4},{6,7},{7,6},{8,9},{9,8},{10,11... | collective-permute-start | bytes 786440 | tf_op jit(solution)/shard_map/ppermute | solution.py:517
  21.3 7.7 %collective-permute-start.3 = (f32[128,4,128]{2,1,0:T(4,128)S(1)}, f32[128,4,128]{2,1,0:T(4,128)S(1)}, u32[]{:S(2)}, u32[]{:S(2)}) collective-permute-start(f32[128,4,128]{2,1,0:T(4,128)S(1)} %get-tuple-element.20), channel_id=1, source_target_pairs={{1,2},{3,4},{5,6},{7,8},{9,10},{11,12},{13,14},{15,16},{17,18},{19... | collective-permute-start | bytes 786440 | tf_op jit(solution)/shard_map/ppermute | solution.py:519

commit v2 on v1

v2 whole, which is shorter than its diff:
```python
import functools

import jax
import jax.numpy as jnp
import numpy as np
from jax import lax
from jax.experimental import pallas as pl
from jax.experimental.pallas import tpu as pltpu
from jax.sharding import Mesh, PartitionSpec as P

POISSON = 0.3
PENALTY = 3.0
SOFT = 0.001
CORNERS = [(a, b, c) for c in (0, 1) for b in (0, 1) for a in (0, 1)]
EDGE = float(1.5 - np.sqrt(2.0))

RX, RY, NZ = 12, 8, 128
NI = RX + 8
LOW_X, UP_X = 20, 27
BLOCKS = 128
F32 = jnp.float32


def element_stiffness():
    lame_first = POISSON / ((1.0 + POISSON) * (1.0 - 2.0 * POISSON))
    shear_mod = 1.0 / (2.0 * (1.0 + POISSON))
    elastic = np.zeros((6, 6))
    elastic[:3, :3] = lame_first
    for axis_number in range(3):
        elastic[axis_number, axis_number] = lame_first + 2.0 * shear_mod
        elastic[axis_number + 3, axis_number + 3] = shear_mod
    points = [0.5 - 0.5 / np.sqrt(3.0), 0.5 + 0.5 / np.sqrt(3.0)]
    matrix = np.zeros((24, 24))
    for point_x in points:
        for point_y in points:
            for point_z in points:
                coords = (point_x, point_y, point_z)
                strain = np.zeros((6, 24))
                for number, corner in enumerate(CORNERS):
                    factors = [coords[d] if corner[d] else 1.0 - coords[d] for d in range(3)]
                    slopes = [1.0 if corner[d] else -1.0 for d in range(3)]
                    derivs = [
                        slopes[0] * factors[1] * factors[2],
                        factors[0] * slopes[1] * factors[2],
                        factors[0] * factors[1] * slopes[2],
                    ]
                    column = 3 * number
                    strain[0, column] = derivs[0]
                    strain[1, column + 1] = derivs[1]
                    strain[2, column + 2] = derivs[2]
                    strain[3, column] = derivs[1]
                    strain[3, column + 1] = derivs[0]
                    strain[4, column + 1] = derivs[2]
                    strain[4, column + 2] = derivs[1]
                    strain[5, column] = derivs[2]
                    strain[5, column + 2] = derivs[0]
                matrix += strain.T @ elastic @ strain / 8.0
    return matrix


def modal_stiffness():
    one = np.array([[1.0, 1.0], [-1.0, 1.0]])
    change = np.zeros((8, 8))
    for row, (a, b, c) in enumerate(CORNERS):
        for column, (p, q, r) in enumerate(CORNERS):
            change[row, column] = one[a, p] * one[b, q] * one[c, r]
    inverse = np.linalg.inv(np.kron(change, np.eye(3)))
    modal = inverse.T @ element_stiffness() @ inverse
    modes = [corner + (d,) for corner in CORNERS for d in range(3)]
    return {(modes[i], modes[j]): float(modal[i, j]) for i in range(24) for j in range(24)}


MODAL_VALUE = modal_stiffness()
CORNER_DIAG = float(element_stiffness()[0, 0])


def pack_x_kernel(load, disp, dens, mask, low, up, flags, done):
    copies = [(mask.at[RX - 3 : RX], flags.at[0:3]), (mask.at[0:4], flags.at[3:7])]
    for c in range(3):
        copies.append((load.at[c, RX - 3 : RX], low.at[3 * c : 3 * c + 3]))
        copies.append((load.at[c, 0:4], up.at[4 * c : 4 * c + 4]))
        copies.append((disp.at[c, RX - 1 : RX], low.at[17 + c : 18 + c]))
        copies.append((disp.at[c, 0:2], up.at[21 + 2 * c : 23 + 2 * c]))
    copies.append((dens.at[RX - 5 : RX], low.at[12:17]))
    copies.append((dens.at[0:5], up.at[16:21]))
    copies = [
        pltpu.make_async_copy(source, target, done.at[n])
        for n, (source, target) in enumerate(copies)
    ]
    for copy in copies:
        copy.start()
    for copy in copies:
        copy.wait()
    low[9:12] = (1 - flags[0:3]).astype(F32)
    up[12:16] = (1 - flags[3:7]).astype(F32)


def loads_kernel(nodes, forces, out):
    first_x = (lax.axis_index("x") * lax.axis_size("y") + lax.axis_index("y")) * RX - 3
    first_y = (lax.axis_index("z") * lax.axis_size("c") + lax.axis_index("c")) * RY
    count = (NI - 1) * RY
    chunk = 256
    place = lax.broadcasted_iota(jnp.int32, (count, chunk), 0)
    depth = lax.broadcasted_iota(jnp.int32, (NZ, chunk), 0)
    total = jnp.zeros((9 * count, NZ), F32)
    for start in range(0, nodes.shape[1], chunk):
        cols = slice(start, start + chunk)
        local_x = nodes[0:1, cols] - first_x
        local_y = nodes[1:2, cols] - first_y
        inside = (local_x >= 0) & (local_x < NI - 1) & (local_y >= 0) & (local_y < RY)
        spot = jnp.where(inside, local_x * RY + local_y, -1)
        hit = place == spot
        layer = jnp.where(depth == nodes[2:3, cols], 1.0, 0.0).astype(jnp.bfloat16)
        parts = []
        for c in range(3):
            rest = forces[c : c + 1, cols]
            for _ in range(3):
                head = rest.astype(jnp.bfloat16).astype(F32)
                rest = rest - head
                parts.append(jnp.where(hit, head, 0.0).astype(jnp.bfloat16))
        total = total + lax.dot_general(
            jnp.concatenate(parts, axis=0),
            layer,
            (((1,), (1,)), ((), ())),
            preferred_element_type=F32,
        )
    for c in range(3):
        base = 3 * c * count
        summed = (
            total[base : base + count]
            + total[base + count : base + 2 * count]
            + total[base + 2 * count : base + 3 * count]
        )
        out[c] = summed.reshape(NI - 1, RY, NZ)


def pack_y_kernel(load, disp, dens, mask, placed, low, up, ld, fr, dn, di, first, second):
    for c in range(3):
        ld[c, 0:3] = low[3 * c : 3 * c + 3] + placed[c, 0:3]
        ld[c, 3 : 3 + RX] = load[c] + placed[c, 3 : 3 + RX]
        ld[c, 3 + RX : 7 + RX] = up[4 * c : 4 * c + 4] + placed[c, 3 + RX : 7 + RX]
        di[c, 0] = low[17 + c]
        di[c, 1 : 1 + RX] = disp[c]
        di[c, 1 + RX : 3 + RX] = up[21 + 2 * c : 23 + 2 * c]
    fr[0:3] = low[9:12]
    fr[3 : 3 + RX] = (1 - mask[...]).astype(F32)
    fr[3 + RX : 7 + RX] = up[12:16]
    dn[0:5] = low[12:17]
    dn[5 : 5 + RX] = dens[...]
    dn[5 + RX : 10 + RX] = up[16:21]
    even = lax.axis_index("c") == 0

    def rows_for_upper(out):
        for c in range(3):
            out[19 * c : 19 * c + 19] = ld[c, :, 4:8]
        out[57:76] = fr[:, 4:8]
        out[76:98] = dn[:, 4:8]
        for p in range(22):
            out[98 + p // 4, p % 4 : p % 4 + 1] = dn[p, 3:4]
        for n in range(45):
            out[104 + n // 4, n % 4 : n % 4 + 1] = di[n // 15, n % 15, 7:8]

    def rows_for_lower(out):
        for c in range(3):
            out[19 * c : 19 * c + 19] = ld[c, :, 0:4]
        out[57:76] = fr[:, 0:4]
        out[76:98] = dn[:, 0:4]
        for p in range(22):
            out[98 + p // 4, p % 4 : p % 4 + 1] = dn[p, 4:5]
        for n in range(45):
            out[104 + n // 2, 2 * (n % 2) : 2 * (n % 2) + 2] = di[n // 15, n % 15, 0:2]

    @pl.when(even)
    def _():
        rows_for_upper(first)
        rows_for_lower(second)

    @pl.when(jnp.logical_not(even))
    def _():
        rows_for_lower(first)
        rows_for_upper(second)


def up_z(v, lane):
    return jnp.where(lane < NZ - 1, pltpu.roll(v, NZ - 1, 1), 0.0)


def down_z(v, lane):
    return jnp.where(lane > 0, pltpu.roll(v, 1, 1), 0.0)


def axes(*ones):
    return tuple(int(n in ones) for n in range(3))


K_SHEAR = MODAL_VALUE[axes(1) + (0,), axes(0) + (1,)]
K_NORMAL = MODAL_VALUE[axes(0) + (0,), axes(0) + (0,)]
K_CROSS = MODAL_VALUE[axes(0) + (0,), axes(1) + (1,)]
K_BEND = MODAL_VALUE[axes(0, 1) + (0,), axes(0, 1) + (0,)]
K_BEND_OFF = MODAL_VALUE[axes(0, 1) + (0,), axes(1, 2) + (2,)]
K_TWIST = MODAL_VALUE[axes(0, 1) + (2,), axes(0, 2) + (1,)]
K_LAST = MODAL_VALUE[axes(0, 1, 2) + (0,), axes(0, 1, 2) + (0,)]
PAIRS = [(0, 1), (0, 2), (1, 2)]
BENDS = [(0, 1, 2), (1, 0, 2), (0, 2, 1)]


def combine(h):
    out = {}
    for d, e in PAIRS:
        out["s", d, e] = h[axes(e) + (d,)] + h[axes(d) + (e,)]
    normal = [h[axes(d) + (d,)] for d in range(3)]
    total = normal[0] + normal[1] + normal[2]
    for d in range(3):
        out["n", d] = normal[d] * ((K_NORMAL - K_CROSS) / K_CROSS) + total
    for d, e, f in BENDS:
        one, two = h[axes(d, e) + (d,)], h[axes(e, f) + (f,)]
        out["b", d, e] = one * (K_BEND / K_BEND_OFF) + two
        out["b", f, e] = two * (K_BEND / K_BEND_OFF) + one
    twist = [h[axes(*[n for n in range(3) if n != d]) + (d,)] for d in range(3)]
    total = twist[0] + twist[1] + twist[2]
    for d in range(3):
        out["t", d] = twist[d] + total
        out["l", d] = h[axes(0, 1, 2) + (d,)]
    return out


SCALES = {"s": K_SHEAR, "n": K_CROSS, "b": K_BEND_OFF, "t": K_TWIST, "l": K_LAST}


def mode_of(key):
    kind = key[0]
    if kind == "s":
        return axes(key[2]) + (key[1],)
    if kind == "n":
        return axes(key[1]) + (key[1],)
    if kind == "b":
        return axes(key[1], key[2]) + (key[1],)
    if kind == "t":
        return axes(*[n for n in range(3) if n != key[1]]) + (key[1],)
    return axes(0, 1, 2) + (key[1],)


def modes_of(near, far):
    result = {}
    for key in near:
        c, b, s = key
        result[0, b, s, c] = near[key] + far[key]
        result[1, b, s, c] = far[key] - near[key]
    return result


KEYS = [("s", d, e) for d, e in PAIRS] + [("n", d) for d in range(3)]
KEYS += [("b", d, e) for d, e, f in BENDS] + [("b", f, e) for d, e, f in BENDS]
KEYS += [("t", d) for d in range(3)] + [("l", d) for d in range(3)]
NUMBER = {key: n for n, key in enumerate(KEYS)}
PARTS = [(c, s) for c in range(3) for s in (0, 1)]


def main_kernel(ld, fr, dn, di, first, second, basis, senses, sums, L1, FR1, D1, DN, MOD, SC, HP, W, Z, G, DS, SS, F, DV):
    gx = lax.axis_index("x") * lax.axis_size("y") + lax.axis_index("y")
    gy = lax.axis_index("z") * lax.axis_size("c") + lax.axis_index("c")
    extent_x = RX * lax.axis_size("x") * lax.axis_size("y")
    extent_y = RY * lax.axis_size("z") * lax.axis_size("c")
    lane = lax.broadcasted_iota(jnp.int32, (8, NZ), 1)
    row = lax.broadcasted_iota(jnp.int32, (8, NZ), 0)
    upper_half = row < 4

    DN[:, 16:24] = dn[...]
    D1[...] = jnp.zeros(D1.shape, F32)

    def fill(below, above):
        for c in range(3):
            L1[c, :, 0:4] = above[19 * c : 19 * c + 19]
            L1[c, :, 4:8] = below[19 * c : 19 * c + 19]
        FR1[:, 0:4] = above[57:76]
        FR1[:, 4:8] = below[57:76]
        DN[:, 12:16] = below[76:98]
        DN[:, 24:28] = above[76:98]
        for p in range(22):
            DN[p, 11:12] = below[98 + p // 4, p % 4 : p % 4 + 1]
            DN[p, 28:29] = above[98 + p // 4, p % 4 : p % 4 + 1]
        for n in range(45):
            D1[n // 15, n % 15, 7:8] = below[104 + n // 4, n % 4 : n % 4 + 1]
            D1[n // 15, n % 15, 0:2] = above[104 + n // 2, 2 * (n % 2) : 2 * (n % 2) + 2]

    even = lax.axis_index("c") == 0

    @pl.when(even)
    def _():
        fill(second, first)

    @pl.when(jnp.logical_not(even))
    def _():
        fill(first, second)

    load_of = lambda c, i, t: (L1 if t else ld)[c, i - 1]
    free_of = lambda i, t: (FR1 if t else fr)[i - 1]
    disp_of = lambda c, p, t: (D1 if t else di)[c, p]

    near_z = 2.0 - jnp.where(lane == 0, 1.0, 0.0) - jnp.where(lane == NZ - 1, 1.0, 0.0)
    inside_y, part_a, part_b = [], [], []
    for t in range(2):
        place_y = gy * RY + (row if t == 0 else jnp.where(upper_half, row + 8, row - 8))
        inside_y.append(jnp.where((place_y >= 0) & (place_y < extent_y), 1.0, 0.0))
        near_y = 2.0 - jnp.where(place_y == 0, 1.0, 0.0) - jnp.where(place_y == extent_y - 1, 1.0, 0.0)
        part_a.append(1.5 + 0.5 * (near_y + near_z) + EDGE * near_y * near_z)
        part_b.append(0.5 + EDGE * (near_y + near_z))

    def filter_parts(cells, beside):
        deep = up_z(cells, lane) + down_z(cells, lane)
        deep_beside = up_z(beside, lane) + down_z(beside, lane)
        around = deep + beside
        return (
            1.5 * cells + 0.5 * around + EDGE * deep_beside,
            0.5 * cells + EDGE * around,
        )

    def density_rows(p, t, shift):
        if t == 0:
            return DN[p, 16 + shift : 24 + shift]
        return jnp.where(
            upper_half, DN[p, 24 + shift : 32 + shift], DN[p, 8 + shift : 16 + shift]
        )

    for t in range(2):
        window = []
        for p in range(NI + 2):
            beside = density_rows(p, t, -1) + density_rows(p, t, 1)
            window.append(filter_parts(density_rows(p, t, 0), beside))
            i = p - 2
            if i < 0:
                continue
            place_x = gx * RX - 4 + i
            inside_x = jnp.where((place_x >= 0) & (place_x < extent_x), 1.0, 0.0)
            near_x = 2.0 - jnp.where(place_x == 0, 1.0, 0.0) - jnp.where(place_x == extent_x - 1, 1.0, 0.0)
            inverse = 1.0 / (part_a[t] + near_x * part_b[t])
            physical = (window[-2][0] + window[-3][1] + window[-1][1]) * inverse
            squared = physical * physical
            inside = inside_y[t] * inside_x
            mod = inside * (SOFT + (1.0 - SOFT) * (squared * physical))
            MOD[i, t] = mod
            if 3 <= i <= NI - 4:
                SC[i - 3, t] = (inside * (PENALTY * (1.0 - SOFT))) * (squared * inverse)
            deep = mod + down_z(mod, lane)
            HP[i, 8 + 8 * t : 16 + 8 * t] = deep
            if t == 1:
                HP[i, 0:8] = deep

    zero = jnp.zeros((8, NZ), F32)

    def store_parts(c, i, t, v):
        above = up_z(v, lane)
        for s, part in ((0, v + above), (1, above - v)):
            G[2 * c + s, i, 8 * t : 8 * t + 8] = part
            if t == 0:
                G[2 * c + s, i, 16:24] = part

    def in_block(i, t):
        return t == 0 and 4 <= i < 4 + RX

    bz = zero
    for t in range(2):
        before = None
        for i in range(NI):
            summed = HP[i, 8 + 8 * t : 16 + 8 * t] + HP[i, 7 + 8 * t : 15 + 8 * t]
            if i > 0:
                inverse = jnp.where(free_of(i, t) > 0.5, (1.0 / CORNER_DIAG) / (summed + before), 0.0)
                W[i, t] = inverse
                for c in range(3):
                    load = load_of(c, i, t)
                    z = inverse * load
                    Z[0, c, i, t] = z
                    store_parts(c, i, t, z)
                    if in_block(i, t):
                        bz = bz + z * load
            before = summed

    def yz_modes(i, t):
        result = {}
        for c, s in PARTS:
            part = G[2 * c + s, i, 8 * t : 8 * t + 8]
            higher = G[2 * c + s, i, 8 * t + 1 : 8 * t + 9]
            result[c, 0, s] = part + higher
            result[c, 1, s] = higher - part
        return result

    def apply(k):
        for t in range(2):
            near = yz_modes(1 + k, t)
            passed = None
            for i in range(1 + k, NI - 1 - k):
                far = yz_modes(i + 1, t)
                modes = modes_of(near, far)
                mixed = combine(modes)
                if 3 <= i <= NI - 4:
                    energy = None
                    for key, n in NUMBER.items():
                        factor = mixed[key] if key[0] == "s" else modes[mode_of(key)]
                        term = factor * F[n, i - 3, t]
                        energy = term if energy is None else energy + term
                    value = energy * SC[i - 3, t]
                    DV[k, i - 3, 8 + 8 * t : 16 + 8 * t] = value
                    if t == 1:
                        DV[k, i - 3, 0:8] = value
                young = MOD[i, t]
                scaled = {kind: young * factor for kind, factor in SCALES.items()}
                forces = {}
                for key, value in mixed.items():
                    force = scaled[key[0]] * value
                    forces[mode_of(key)] = force
                    if key[0] == "s":
                        forces[axes(key[1]) + (key[2],)] = force
                following = {}
                for c, s in PARTS:
                    node = {}
                    for b in (0, 1):
                        slope = forces[1, b, s, c]
                        if (0, b, s, c) in forces:
                            level = forces[0, b, s, c]
                            low, following[c, b, s] = level - slope, level + slope
                            node[b] = low if passed is None else passed[c, b, s] + low
                        else:
                            following[c, b, s] = slope
                            node[b] = -slope if passed is None else passed[c, b, s] - slope
                    if i > 1 + k:
                        DS[2 * c + s, i, t] = node[0] - node[1]
                        both = node[0] + node[1]
                        SS[2 * c + s, i, 8 + 8 * t : 16 + 8 * t] = both
                        if t == 1:
                            SS[2 * c + s, i, 0:8] = both
                passed, near = following, far

    def image(c, i, t):
        level, slope = [
            DS[2 * c + s, i, t] + SS[2 * c + s, i, 7 + 8 * t : 15 + 8 * t] for s in (0, 1)
        ]
        return level - slope + down_z(level + slope, lane)

    for p in range(RX + 3):
        for t in range(2):
            for c in range(3):
                v = disp_of(c, p, t)
                above = up_z(v, lane)
                for s, part in ((0, v + above), (1, above - v)):
                    SS[2 * c + s, p, 8 * t : 8 * t + 8] = part
                    if t == 0:
                        SS[2 * c + s, p, 16:24] = part
    for t in range(2):
        near = None
        for p in range(RX + 3):
            far = {}
            for c, s in PARTS:
                part = SS[2 * c + s, p, 8 * t : 8 * t + 8]
                higher = SS[2 * c + s, p, 8 * t + 1 : 8 * t + 9]
                far[c, 0, s] = part + higher
                far[c, 1, s] = higher - part
            if near is not None:
                for key, value in combine(modes_of(near, far)).items():
                    F[NUMBER[key], p - 1, t] = value * SCALES[key[0]]
            near = far

    def add(total, i, t, one, two):
        return total + one * two if in_block(i, t) else total

    h00 = b1 = h01 = h11 = b2 = h12 = h22 = h02 = zero
    apply(0)
    for t in range(2):
        for i in range(2, NI - 1):
            for c in range(3):
                q = image(c, i, t)
                z = Z[0, c, i, t]
                y = W[i, t] * q - z
                Z[1, c, i, t] = y
                store_parts(c, i, t, y)
                h00 = add(h00, i, t, z, q)
                h01 = add(h01, i, t, y, q)
                if in_block(i, t):
                    b1 = b1 + y * load_of(c, i, t)
    apply(1)
    for t in range(2):
        for i in range(3, NI - 2):
            for c in range(3):
                q = image(c, i, t)
                z = Z[1, c, i, t]
                y = W[i, t] * q - z
                Z[2, c, i, t] = y
                store_parts(c, i, t, y)
                h11 = add(h11, i, t, z, q)
                h12 = add(h12, i, t, y, q)
                if in_block(i, t):
                    b2 = b2 + y * load_of(c, i, t)
    apply(2)
    for i in range(4, 4 + RX):
        for c in range(3):
            q = image(c, i, 0)
            h22 = add(h22, i, 0, Z[2, c, i, 0], q)
            h02 = add(h02, i, 0, Z[0, c, i, 0], q)

    lanes = lax.broadcasted_iota(jnp.int32, (1, NZ), 1)
    line = jnp.zeros((1, NZ), F32)
    for n, value in enumerate((bz, b1, b2, h00, h01, h02, h11, h12, h22)):
        whole = jnp.sum(value, axis=0, keepdims=True)
        whole = jnp.sum(whole, axis=1, keepdims=True)
        line = line + jnp.where(lanes == n, whole, 0.0)
    for n in range(sums.shape[0]):
        sums[n] = line

    for k in range(3):
        window = []
        for p in range(RX + 2):
            beside = DV[k, p, 7:15] + DV[k, p, 9:17]
            window.append(filter_parts(DV[k, p, 8:16], beside))
            if p >= 2:
                senses[k, p - 2] = window[-2][0] + window[-3][1] + window[-1][1]
        for c in range(3):
            basis[k, c] = Z[k, c, 4 : 4 + RX, 0]


def final_kernel(gathered, basis, senses, adjoint, sensitivity):
    total = jnp.sum(gathered[...], axis=0)

    def value(n):
        return jnp.broadcast_to(total[:, n : n + 1], (1, NZ))

    b0, b1, b2, h00, h01, h02, h11, h12, h22 = [value(n) for n in range(9)]
    l1, l2 = h01 / h00, h02 / h00
    d1 = h11 - l1 * h01
    e = h12 - l1 * h02
    fine1 = d1 > 0.0
    l3 = jnp.where(fine1, e / d1, 0.0)
    d2 = h22 - l2 * h02 - l3 * e
    t1 = b1 - l1 * b0
    t2 = b2 - l2 * b0 - l3 * t1
    c2 = jnp.where(d2 > 0.0, t2 / d2, 0.0)
    c1 = jnp.where(fine1, t1 / d1, 0.0) - l3 * c2
    c0 = b0 / h00 - l1 * c1 - l2 * c2
    adjoint[...] = c0 * basis[0] + c1 * basis[1] + c2 * basis[2]
    sensitivity[...] = c0 * senses[0] + c1 * senses[1] + c2 * senses[2]


VMEM = pl.BlockSpec(memory_space=pltpu.VMEM)


def call(kernel, inputs, outs, scratch=(), limit=None):
    single = not isinstance(outs, list)
    shapes = [outs] if single else outs
    result = pl.pallas_call(
        kernel,
        out_shape=[jax.ShapeDtypeStruct(s, F32) for s in shapes],
        in_specs=[VMEM] * len(inputs),
        out_specs=[VMEM] * len(shapes),
        scratch_shapes=[pltpu.VMEM(s, F32) for s in scratch],
        compiler_params=pltpu.CompilerParams(vmem_limit_bytes=limit or 32 * 1024 * 1024),
    )(*inputs)
    return result[0] if single else result


MAIN_SCRATCH = [
    (3, NI - 1, 8, NZ),
    (NI - 1, 8, NZ),
    (3, RX + 3, 8, NZ),
    (NI + 2, 40, NZ),
    (NI, 2, 8, NZ),
    (RX + 2, 2, 8, NZ),
    (NI, 24, NZ),
    (NI, 2, 8, NZ),
    (3, 3, NI, 2, 8, NZ),
    (6, NI, 24, NZ),
    (6, NI, 2, 8, NZ),
    (6, NI, 24, NZ),
    (len(KEYS), RX + 2, 2, 8, NZ),
    (3, RX + 2, 24, NZ),
]


def shards(displacement, adjoint_load, density, fixed_mask, load_nodes, load_forces):
    gx, gy = ("x", "y"), ("z", "c")
    count_x = lax.axis_size("x") * lax.axis_size("y")
    count_y = lax.axis_size("z") * lax.axis_size("c")
    own = (adjoint_load, displacement, density, fixed_mask)
    low, up = pl.pallas_call(
        pack_x_kernel,
        out_shape=[
            jax.ShapeDtypeStruct((LOW_X, RY, NZ), F32),
            jax.ShapeDtypeStruct((UP_X, RY, NZ), F32),
        ],
        in_specs=[pl.BlockSpec(memory_space=pl.ANY)] * 4,
        out_specs=[VMEM] * 2,
        scratch_shapes=[
            pltpu.VMEM((7, RY, NZ), jnp.int32),
            pltpu.SemaphoreType.DMA((16,)),
        ],
    )(*own)
    low = lax.ppermute(low, gx, [(i, i + 1) for i in range(count_x - 1)])
    up = lax.ppermute(up, gx, [(i + 1, i) for i in range(count_x - 1)])
    placed = call(loads_kernel, (load_nodes, load_forces), (3, NI - 1, RY, NZ))
    ld, fr, dn, di, first, second = call(
        pack_y_kernel,
        own + (placed, low, up),
        [
            (3, NI - 1, RY, NZ),
            (NI - 1, RY, NZ),
            (NI + 2, RY, NZ),
            (3, RX + 3, RY, NZ),
            (BLOCKS, 4, NZ),
            (BLOCKS, 4, NZ),
        ],
    )
    pairs = [(i, i + 1) for i in range(1, count_y - 1, 2)]
    second = lax.ppermute(second, gy, pairs + [(j, i) for i, j in pairs])
    first = lax.ppermute(first, "c", [(0, 1), (1, 0)])
    near = lax.axis_size("c") * count_x
    far = lax.axis_size("z")
    basis, senses, sums = call(
        main_kernel,
        (ld, fr, dn, di, first, second),
        [(3, 3, RX, RY, NZ), (3, RX, RY, NZ), (near, 1, NZ)],
        MAIN_SCRATCH,
        48 * 1024 * 1024,
    )
    sums = lax.all_to_all(sums, ("x", "y", "c"), 0, 0, tiled=True)
    sums = jnp.broadcast_to(jnp.sum(sums, axis=0, keepdims=True), (far, 1, NZ))
    sums = lax.all_to_all(sums, "z", 0, 0, tiled=True)
    adjoint, sensitivity = call(
        final_kernel, (sums, basis, senses), [(3, RX, RY, NZ), (RX, RY, NZ)]
    )
    return adjoint, sensitivity


def solution(mesh):
    size_x, size_y = mesh.shape["gx"], mesh.shape["gy"]
    side = int(round(size_x**0.5))
    whole = Mesh(
        mesh.devices.reshape(side, size_x // side, size_y // 2, 2), ("x", "y", "z", "c")
    )
    field = P(None, ("x", "y"), ("z", "c"), None)
    grid = P(("x", "y"), ("z", "c"), None)
    return jax.shard_map(
        shards,
        mesh=whole,
        in_specs=(field, field, grid, grid, P(), P()),
        out_specs=(field, grid),
        check_vma=False,
    )
```

time: 89.2 us -> 73.5 us (0.82)
  Pallas kernels: 23.1 us -> 10.9 us
  local copies, waits for them, and re-layouts: 3.45 us -> 0.04 us
    pallas_call x5 -> x4, Pallas kernels: 23.1 us -> 9.13 us  [call(): pl.pallas_call(kernel, out_shape=[jax.ShapeDtypeStruct(s, F32) for s in s...]
    unnamed x20 -> x12, local copies, waits for them, and re-layouts: 3.44 us -> 0.03 us
    pallas_call x0 -> x1, Pallas kernels: none -> 1.73 us  [shards(): pl.pallas_call(pack_x_kernel, out_shape=[jax.ShapeDtypeStruct((LOW_X, RY,...]
where the time goes in v2:
time: 73.5 us; the launch traced here: 73.2 us
  blocking collectives  38.4 us (52%)
  starting transfers between devices  17.2 us (23%)
  Pallas kernels  10.9 us (15%)
  waiting for transfers between devices  5.76 us (8%)
  between operations  0.8 us (1%)
    all_to_all x1, blocking collectives, shards(): sums = lax.all_to_all(sums, 'z', 0, 0, tiled=True)  27.1 us
    all_to_all x1, blocking collectives, shards(): sums = lax.all_to_all(sums, ('x', 'y', 'c'), 0, 0, tiled=True)  11.3 us
    ppermute x1, starting transfers between devices, shards(): first = lax.ppermute(first, 'c', [(0, 1), (1, 0)])  9.22 us
    pallas_call x4, Pallas kernels, call(): pl.pallas_call(kernel, out_shape=[jax.ShapeDtypeStruct(s, F32) for s in s...  9.13 us
    ppermute x1, waiting for transfers between devices, shards(): second = lax.ppermute(second, gy, pairs + [(j, i) for i, j in pairs])  5.75 us
    ppermute x1, starting transfers between devices, shards(): low = lax.ppermute(low, gx, [(i, i + 1) for i in range(count_x - 1)])  4.79 us
    ppermute x1, starting transfers between devices, shards(): second = lax.ppermute(second, gy, pairs + [(j, i) for i, j in pairs])  1.92 us
    pallas_call x1, Pallas kernels, shards(): pl.pallas_call(pack_x_kernel, out_shape=[jax.ShapeDtypeStruct((LOW_X, RY,...  1.73 us
  transfers between devices with their start and end apart: 4, of which 1 were waited for; matrix products, arithmetic and copies ran while one was open for 0% of the time, Pallas kernels for 2%

profile of v2, /device:TPU:1, one launch (start us, length us, event | category | flops | bytes accessed | tf_op | source)
XLA Modules:
  0.0 73.2 jit_solution(14588956479209092262)
XLA Ops:
  0.6 0.0 copy-start.5
  0.6 0.0 copy-start.4
  0.7 0.0 copy-start.2
  0.7 0.0 copy-start.3
  0.7 1.7 %shard_map.78 = (f32[20,8,128]{2,1,0:T(8,128)}, f32[27,8,128]{2,1,0:T(8,128)}) custom-call(f32[3,12,8,128]{3,2,1,0:T(8,128)} %load.3, f32[3,12,8,128]{3,2,1,0:T(8,128)} %disp.3, f32[12,8,128]{2,1,0:T(8,128)} %dens.3, s32[12,8,128]{2,1,0:T(8,128)} %mask.3), custom_call_target="tpu_custom_call" | custom-call | tf_op jit(solution)/shard_map/pallas_call | solution.py:581
  2.4 1.3 %collective-permute-start.1 = (f32[27,8,128]{2,1,0:T(8,128)}, f32[27,8,128]{2,1,0:T(8,128)S(1)}, u32[]{:S(2)}, u32[]{:S(2)}) collective-permute-start(f32[27,8,128]{2,1,0:T(8,128)} %get-tuple-element.14), channel_id=1, source_target_pairs={{32,0},{64,32},{96,64},{128,96},{160,128},{192,160},{224,192},{256... | collective-permute-start | bytes 331784 | tf_op jit(solution)/shard_map/ppermute | solution.py:595
  3.7 0.0 copy-start
  3.7 0.0 copy-start.1
  3.7 4.8 %collective-permute-start = (f32[20,8,128]{2,1,0:T(8,128)}, f32[20,8,128]{2,1,0:T(8,128)S(1)}, u32[]{:S(2)}, u32[]{:S(2)}) collective-permute-start(f32[20,8,128]{2,1,0:T(8,128)} %get-tuple-element.13), channel_id=1, source_target_pairs={{0,32},{32,64},{64,96},{96,128},{128,160},{160,192},{192,224},{224... | collective-permute-start | bytes 245768 | tf_op jit(solution)/shard_map/ppermute | solution.py:594
  8.5 0.0 copy-done.5
  8.5 0.0 copy-done.4
  8.5 1.7 %shard_map.77.placed = f32[3,19,8,128]{3,2,1,0:T(8,128)S(1)} custom-call(s32[3,2048]{1,0:T(4,128)S(1)} %copy-done.4, f32[3,2048]{1,0:T(4,128)S(1)} %copy-done.5), custom_call_target="tpu_custom_call" | custom-call | tf_op jit(solution)/shard_map/pallas_call | solution.py:547
  10.3 0.0 collective-permute-done.low
  10.3 0.0 collective-permute-done.1.up
  10.3 0.0 copy-done.2
  10.3 0.0 copy-done.3
  10.3 0.0 copy-done
  10.4 0.0 copy-done.1
  10.4 0.2 shard_map.79
  10.5 9.2 %collective-permute-start.2 = (f32[128,4,128]{2,1,0:T(4,128)S(1)}, f32[128,4,128]{2,1,0:T(4,128)S(1)}, u32[]{:S(2)}, u32[]{:S(2)}) collective-permute-start(f32[128,4,128]{2,1,0:T(4,128)S(1)} %get-tuple-element.19), channel_id=1, source_target_pairs={{0,1},{1,0},{2,3},{3,2},{4,5},{5,4},{6,7},{7,6},{8,9},{9,8},{10,11... | collective-permute-start | bytes 786440 | tf_op jit(solution)/shard_map/ppermute | solution.py:611
  19.8 1.9 %collective-permute-start.3 = (f32[128,4,128]{2,1,0:T(4,128)S(1)}, f32[128,4,128]{2,1,0:T(4,128)S(1)}, u32[]{:S(2)}, u32[]{:S(2)}) collective-permute-start(f32[128,4,128]{2,1,0:T(4,128)S(1)} %get-tuple-element.20), channel_id=1, source_target_pairs={{1,2},{3,4},{5,6},{7,8},{9,10},{11,12},{13,14},{15,16},{17,18},{19... | collective-permute-start | bytes 786440 | tf_op jit(solution)/shard_map/ppermute | solution.py:610
  21.7 0.0 collective-permute-done.2.first
  21.7 5.8 %collective-permute-done.3.second = f32[128,4,128]{2,1,0:T(4,128)S(1)} collective-permute-done((f32[128,4,128]{2,1,0:T(4,128)S(1)}, f32[128,4,128]{2,1,0:T(4,128)S(1)}, u32[]{:S(2)}, u32[]{:S(2)}) %collective-permute-start.3) | collective-permute-done | bytes 262176 | tf_op jit(solution)/shard_map/ppermute | solution.py:610
  27.5 6.4 %shard_map.80 = (f32[3,3,12,8,128]{4,3,2,1,0:T(8,128)S(1)}, f32[3,12,8,128]{3,2,1,0:T(8,128)S(1)}, f32[32,1,128]{2,1,0:T(1,128)S(1)}) custom-call(f32[3,19,8,128]{3,2,1,0:T(8,128)S(1)} %get-tuple-element.15.ld, f32[19,8,128]{2,1,0:T(8,128)S(1)} %get-tuple-element.16.fr, f32[22,8,128]{2,1,0:T(8,128)S(1)} %get-tuple-element.17.dn, ...), custom_call_target="tpu_custom_call" | custom-call | tf_op jit(solution)/shard_map/pallas_call | solution.py:547
  33.9 11.3 %all_to_all.10 = f32[32,1,128]{2,1,0:T(1,128)S(1)} all-to-all(f32[32,1,128]{2,1,0:T(1,128)S(1)} %get-tuple-element.21), channel_id=1, replica_groups=mesh['x'=4,'y'=4,'z'=16,'c'=2] {'x','y','c'}, dimensions={0} | all-to-all | bytes 32768 | tf_op jit(solution)/shard_map/all_to_all | solution.py:621
  45.2 0.1 reduce_sum.9
  45.2 27.1 %all_to_all.11.gathered = f32[16,1,128]{2,1,0:T(1,128)S(1)} all-to-all(f32[16,1,128]{2,1,0:T(1,128)S(1)} %broadcast_in_dim.2), channel_id=1, replica_groups=mesh['x'=4,'y'=4,'z'=16,'c'=2] {'z'}, dimensions={0} | all-to-all | bytes 16384 | tf_op jit(solution)/shard_map/all_to_all | solution.py:623
  72.4 0.8 %shard_map.81 = (f32[3,12,8,128]{3,2,1,0:T(8,128)}, f32[12,8,128]{2,1,0:T(8,128)}) custom-call(f32[16,1,128]{2,1,0:T(1,128)S(1)} %all_to_all.11.gathered, f32[3,3,12,8,128]{4,3,2,1,0:T(8,128)S(1)} %get-tuple-element.22.basis, f32[3,12,8,128]{3,2,1,0:T(8,128)S(1)} %get-tuple-element.23.senses), custom_call_target="tpu_custom_call" | custom-call | tf_op jit(solution)/shard_map/pallas_call | solution.py:547
  (1 shorter events, 0.0 us)
Async XLA Ops:
  0.6 7.9 %copy-start.5 = (f32[3,2048]{1,0:T(4,128)S(1)}, f32[3,2048]{1,0:T(4,128)}, u32[]{:S(2)}) copy-start(f32[3,2048]{1,0:T(4,128)} %forces.1) | copy-start | bytes 73732
  0.6 7.9 %copy-start.4 = (s32[3,2048]{1,0:T(4,128)S(1)}, s32[3,2048]{1,0:T(4,128)}, u32[]{:S(2)}) copy-start(s32[3,2048]{1,0:T(4,128)} %nodes.1) | copy-start | bytes 73732
  0.7 9.7 %copy-start.2 = (f32[12,8,128]{2,1,0:T(8,128)S(1)}, f32[12,8,128]{2,1,0:T(8,128)}, u32[]{:S(2)}) copy-start(f32[12,8,128]{2,1,0:T(8,128)} %dens.3) | copy-start | bytes 147460
  0.7 9.7 %copy-start.3 = (s32[12,8,128]{2,1,0:T(8,128)S(1)}, s32[12,8,128]{2,1,0:T(8,128)}, u32[]{:S(2)}) copy-start(s32[12,8,128]{2,1,0:T(8,128)} %mask.3) | copy-start | bytes 147460
  2.4 7.9 %collective-permute-start.1 = (f32[27,8,128]{2,1,0:T(8,128)}, f32[27,8,128]{2,1,0:T(8,128)S(1)}, u32[]{:S(2)}, u32[]{:S(2)}) collective-permute-start(f32[27,8,128]{2,1,0:T(8,128)} %get-tuple-element.14), channel_id=1, source_target_pairs={{32,0},{64,32},{96,64},{128,96},{160,128},{192,160},{224,192},{256... | collective-permute-start | bytes 331784 | tf_op jit(solution)/shard_map/ppermute | solution.py:595
  3.7 6.6 %copy-start = (f32[3,12,8,128]{3,2,1,0:T(8,128)S(1)}, f32[3,12,8,128]{3,2,1,0:T(8,128)}, u32[]{:S(2)}) copy-start(f32[3,12,8,128]{3,2,1,0:T(8,128)} %load.3) | copy-start | bytes 442372
  3.7 6.6 %copy-start.1 = (f32[3,12,8,128]{3,2,1,0:T(8,128)S(1)}, f32[3,12,8,128]{3,2,1,0:T(8,128)}, u32[]{:S(2)}) copy-start(f32[3,12,8,128]{3,2,1,0:T(8,128)} %disp.3) | copy-start | bytes 442372
  3.7 6.6 %collective-permute-start = (f32[20,8,128]{2,1,0:T(8,128)}, f32[20,8,128]{2,1,0:T(8,128)S(1)}, u32[]{:S(2)}, u32[]{:S(2)}) collective-permute-start(f32[20,8,128]{2,1,0:T(8,128)} %get-tuple-element.13), channel_id=1, source_target_pairs={{0,32},{32,64},{64,96},{96,128},{128,160},{160,192},{192,224},{224... | collective-permute-start | bytes 245768 | tf_op jit(solution)/shard_map/ppermute | solution.py:594
  10.5 11.2 %collective-permute-start.2 = (f32[128,4,128]{2,1,0:T(4,128)S(1)}, f32[128,4,128]{2,1,0:T(4,128)S(1)}, u32[]{:S(2)}, u32[]{:S(2)}) collective-permute-start(f32[128,4,128]{2,1,0:T(4,128)S(1)} %get-tuple-element.19), channel_id=1, source_target_pairs={{0,1},{1,0},{2,3},{3,2},{4,5},{5,4},{6,7},{7,6},{8,9},{9,8},{10,11... | collective-permute-start | bytes 786440 | tf_op jit(solution)/shard_map/ppermute | solution.py:611
  19.8 7.7 %collective-permute-start.3 = (f32[128,4,128]{2,1,0:T(4,128)S(1)}, f32[128,4,128]{2,1,0:T(4,128)S(1)}, u32[]{:S(2)}, u32[]{:S(2)}) collective-permute-start(f32[128,4,128]{2,1,0:T(4,128)S(1)} %get-tuple-element.20), channel_id=1, source_target_pairs={{1,2},{3,4},{5,6},{7,8},{9,10},{11,12},{13,14},{15,16},{17,18},{19... | collective-permute-start | bytes 786440 | tf_op jit(solution)/shard_map/ppermute | solution.py:610

commit v3 on v2

--- a/solution.py
+++ b/solution.py
@@ -17,7 +17,8 @@
 RX, RY, NZ = 12, 8, 128
 NI = RX + 8
 LOW_X, UP_X = 20, 27
-BLOCKS = 128
+NEAR, CORNER = 81, 46
+CHUNK = 256
 F32 = jnp.float32
 
 
@@ -95,22 +96,23 @@
     up[12:16] = (1 - flags[3:7]).astype(F32)
 
 
-def loads_kernel(nodes, forces, out):
+def loads_kernel(nodes, forces, _, out):
     first_x = (lax.axis_index("x") * lax.axis_size("y") + lax.axis_index("y")) * RX - 3
     first_y = (lax.axis_index("z") * lax.axis_size("c") + lax.axis_index("c")) * RY
     count = (NI - 1) * RY
-    chunk = 256
+    chunk = CHUNK
     place = lax.broadcasted_iota(jnp.int32, (count, chunk), 0)
-    depth = lax.broadcasted_iota(jnp.int32, (NZ, chunk), 0)
-    total = jnp.zeros((9 * count, NZ), F32)
+    depth = lax.broadcasted_iota(jnp.int32, (2 * NZ, chunk), 0)
+    total = jnp.zeros((9 * count, 2 * NZ), F32)
     for start in range(0, nodes.shape[1], chunk):
         cols = slice(start, start + chunk)
         local_x = nodes[0:1, cols] - first_x
         local_y = nodes[1:2, cols] - first_y
-        inside = (local_x >= 0) & (local_x < NI - 1) & (local_y >= 0) & (local_y < RY)
-        spot = jnp.where(inside, local_x * RY + local_y, -1)
+        inside = (local_x >= 0) & (local_x < NI - 1) & (local_y >= -4) & (local_y < RY + 4)
+        spot = jnp.where(inside, local_x * RY + (local_y & (RY - 1)), -1)
         hit = place == spot
-        layer = jnp.where(depth == nodes[2:3, cols], 1.0, 0.0).astype(jnp.bfloat16)
+        outer = jnp.where((local_y < 0) | (local_y >= RY), NZ, 0)
+        layer = jnp.where(depth == nodes[2:3, cols] + outer, 1.0, 0.0).astype(jnp.bfloat16)
         parts = []
         for c in range(3):
             rest = forces[c : c + 1, cols]
@@ -131,54 +133,51 @@
             + total[base + count : base + 2 * count]
             + total[base + 2 * count : base + 3 * count]
         )
-        out[c] = summed.reshape(NI - 1, RY, NZ)
-
-
-def pack_y_kernel(load, disp, dens, mask, placed, low, up, ld, fr, dn, di, first, second):
-    for c in range(3):
-        ld[c, 0:3] = low[3 * c : 3 * c + 3] + placed[c, 0:3]
-        ld[c, 3 : 3 + RX] = load[c] + placed[c, 3 : 3 + RX]
-        ld[c, 3 + RX : 7 + RX] = up[4 * c : 4 * c + 4] + placed[c, 3 + RX : 7 + RX]
-        di[c, 0] = low[17 + c]
-        di[c, 1 : 1 + RX] = disp[c]
-        di[c, 1 + RX : 3 + RX] = up[21 + 2 * c : 23 + 2 * c]
-    fr[0:3] = low[9:12]
-    fr[3 : 3 + RX] = (1 - mask[...]).astype(F32)
-    fr[3 + RX : 7 + RX] = up[12:16]
-    dn[0:5] = low[12:17]
-    dn[5 : 5 + RX] = dens[...]
-    dn[5 + RX : 10 + RX] = up[16:21]
-    even = lax.axis_index("c") == 0
-
-    def rows_for_upper(out):
+        for t in range(2):
+            out[c, :, t] = summed[:, t * NZ : t * NZ + NZ].reshape(NI - 1, RY, NZ)
+
+
+def pack_y_kernel(which, load, disp, dens, mask, low, up, *rest):
+    out = rest[-1]
+
+    def write(rows, extra, count, at):
+        free = lambda part: (1 - part).astype(F32)
         for c in range(3):
-            out[19 * c : 19 * c + 19] = ld[c, :, 4:8]
-        out[57:76] = fr[:, 4:8]
-        out[76:98] = dn[:, 4:8]
-        for p in range(22):
-            out[98 + p // 4, p % 4 : p % 4 + 1] = dn[p, 3:4]
-        for n in range(45):
-            out[104 + n // 4, n % 4 : n % 4 + 1] = di[n // 15, n % 15, 7:8]
-
-    def rows_for_lower(out):
-        for c in range(3):
-            out[19 * c : 19 * c + 19] = ld[c, :, 0:4]
-        out[57:76] = fr[:, 0:4]
-        out[76:98] = dn[:, 0:4]
-        for p in range(22):
-            out[98 + p // 4, p % 4 : p % 4 + 1] = dn[p, 4:5]
-        for n in range(45):
-            out[104 + n // 2, 2 * (n % 2) : 2 * (n % 2) + 2] = di[n // 15, n % 15, 0:2]
-
-    @pl.when(even)
+            out[12 * c : 12 * c + 12] = load[c, :, rows]
+            q = NEAR + 7 * c
+            out[q : q + 3] = low[3 * c : 3 * c + 3, rows]
+            out[q + 3 : q + 7] = up[4 * c : 4 * c + 4, rows]
+        out[36:48] = free(mask[:, rows])
+        out[48:60] = dens[:, rows]
+        q = NEAR + 21
+        out[q : q + 3] = low[9:12, rows]
+        out[q + 3 : q + 7] = up[12:16, rows]
+        out[q + 7 : q + 12] = low[12:17, rows]
+        out[q + 12 : q + 17] = up[16:21, rows]
+        for p in range(12):
+            out[60 + p // 4, p % 4 : p % 4 + 1] = dens[p, extra : extra + 1]
+        for r in range(10):
+            source = low[12 + r, extra : extra + 1] if r < 5 else up[11 + r, extra : extra + 1]
+            out[NEAR + 38 + r // 4, r % 4 : r % 4 + 1] = source
+        per = 4 // count
+        for n in range(36):
+            spot = count * (n % per)
+            out[63 + n // per, spot : spot + count] = disp[n // 12, n % 12, at : at + count]
+        for n in range(9):
+            c, m = n // 3, n % 3
+            source = low[17 + c] if m == 0 else up[20 + 2 * c + m]
+            spot = count * (n % per)
+            out[NEAR + 41 + n // per, spot : spot + count] = source[at : at + count]
+
+    upper = lax.axis_index("c") == which
+
+    @pl.when(upper)
     def _():
-        rows_for_upper(first)
-        rows_for_lower(second)
-
-    @pl.when(jnp.logical_not(even))
+        write(slice(4, 8), 3, 1, 7)
+
+    @pl.when(jnp.logical_not(upper))
     def _():
-        rows_for_lower(first)
-        rows_for_upper(second)
+        write(slice(0, 4), 4, 2, 0)
 
 
 def up_z(v, lane):
@@ -256,7 +255,7 @@
 PARTS = [(c, s) for c in range(3) for s in (0, 1)]
 
 
-def main_kernel(ld, fr, dn, di, first, second, basis, senses, sums, L1, FR1, D1, DN, MOD, SC, HP, W, Z, G, DS, SS, F, DV):
+def main_kernel(load, disp, dens, mask, low, up, placed, first, second, basis, senses, sums, L0, L1, FR1, D1, DN, MOD, SC, HP, W, Z, G, DS, SS, F, DV):
     gx = lax.axis_index("x") * lax.axis_size("y") + lax.axis_index("y")
     gy = lax.axis_index("z") * lax.axis_size("c") + lax.axis_index("c")
     extent_x = RX * lax.axis_size("x") * lax.axis_size("y")
@@ -265,23 +264,47 @@
     row = lax.broadcasted_iota(jnp.int32, (8, NZ), 0)
     upper_half = row < 4
 
-    DN[:, 16:24] = dn[...]
+    DN[0:5, 16:24] = low[12:17]
+    DN[5 : 5 + RX, 16:24] = dens[...]
+    DN[5 + RX : 10 + RX, 16:24] = up[16:21]
     D1[...] = jnp.zeros(D1.shape, F32)
 
     def fill(below, above):
+        below_corner, above_corner = below.at[NEAR : NEAR + CORNER], above.at[NEAR : NEAR + CORNER]
+        for rows, near, corner in (
+            (slice(0, 4), above, above_corner),
+            (slice(4, 8), below, below_corner),
+        ):
+            for c in range(3):
+                L1[c, 0:3, rows] = corner[7 * c : 7 * c + 3]
+                L1[c, 3:15, rows] = near[12 * c : 12 * c + 12]
+                L1[c, 15:19, rows] = corner[7 * c + 3 : 7 * c + 7]
+            FR1[0:3, rows] = corner[21:24]
+            FR1[3:15, rows] = near[36:48]
+            FR1[15:19, rows] = corner[24:28]
+        for rows, extra, near, corner in (
+            (slice(24, 28), 28, above, above_corner),
+            (slice(12, 16), 11, below, below_corner),
+        ):
+            DN[0:5, rows] = corner[28:33]
+            DN[5:17, rows] = near[48:60]
+            DN[17:22, rows] = corner[33:38]
+            for p in range(22):
+                if 5 <= p < 17:
+                    one = near[60 + (p - 5) // 4, (p - 5) % 4 : (p - 5) % 4 + 1]
+                else:
+                    r = p if p < 5 else p - 12
+                    one = corner[38 + r // 4, r % 4 : r % 4 + 1]
+                DN[p, extra : extra + 1] = one
         for c in range(3):
-            L1[c, :, 0:4] = above[19 * c : 19 * c + 19]
-            L1[c, :, 4:8] = below[19 * c : 19 * c + 19]
-        FR1[:, 0:4] = above[57:76]
-        FR1[:, 4:8] = below[57:76]
-        DN[:, 12:16] = below[76:98]
-        DN[:, 24:28] = above[76:98]
-        for p in range(22):
-            DN[p, 11:12] = below[98 + p // 4, p % 4 : p % 4 + 1]
-            DN[p, 28:29] = above[98 + p // 4, p % 4 : p % 4 + 1]
-        for n in range(45):
-            D1[n // 15, n % 15, 7:8] = below[104 + n // 4, n % 4 : n % 4 + 1]
-            D1[n // 15, n % 15, 0:2] = above[104 + n // 2, 2 * (n % 2) : 2 * (n % 2) + 2]
+            for p in range(12):
+                n = 12 * c + p
+                D1[c, p + 1, 7:8] = below[63 + n // 4, n % 4 : n % 4 + 1]
+                D1[c, p + 1, 0:2] = above[63 + n // 2, 2 * (n % 2) : 2 * (n % 2) + 2]
+            for m, p in enumerate((0, 13, 14)):
+                n = 3 * c + m
+                D1[c, p, 7:8] = below_corner[41 + n // 4, n % 4 : n % 4 + 1]
+                D1[c, p, 0:2] = above_corner[41 + n // 2, 2 * (n % 2) : 2 * (n % 2) + 2]
 
     even = lax.axis_index("c") == 0
 
@@ -293,9 +316,32 @@
     def _():
         fill(first, second)
 
-    load_of = lambda c, i, t: (L1 if t else ld)[c, i - 1]
-    free_of = lambda i, t: (FR1 if t else fr)[i - 1]
-    disp_of = lambda c, p, t: (D1 if t else di)[c, p]
+    def load_of(c, i, t):
+        if t == 1:
+            value = L1[c, i - 1]
+        elif i < 4:
+            value = low[3 * c + i - 1]
+        elif i < 4 + RX:
+            value = load[c, i - 4]
+        else:
+            value = up[4 * c + i - 4 - RX]
+        return value + placed[c, i - 1, t]
+
+    def is_free(i, t):
+        if t == 1:
+            return FR1[i - 1] > 0.5
+        if i < 4:
+            return low[9 + i - 1] > 0.5
+        if i < 4 + RX:
+            return mask[i - 4] == 0
+        return up[12 + i - 4 - RX] > 0.5
+
+    def disp_of(c, p, t):
+        if t == 1:
+            return D1[c, p]
+        if p == 0:
+            return low[17 + c]
+        return disp[c, p - 1] if p <= RX else up[21 + 2 * c + p - 1 - RX]
 
     near_z = 2.0 - jnp.where(lane == 0, 1.0, 0.0) - jnp.where(lane == NZ - 1, 1.0, 0.0)
     inside_y, part_a, part_b = [], [], []
@@ -364,15 +410,16 @@
         for i in range(NI):
             summed = HP[i, 8 + 8 * t : 16 + 8 * t] + HP[i, 7 + 8 * t : 15 + 8 * t]
             if i > 0:
-                inverse = jnp.where(free_of(i, t) > 0.5, (1.0 / CORNER_DIAG) / (summed + before), 0.0)
+                inverse = jnp.where(is_free(i, t), (1.0 / CORNER_DIAG) / (summed + before), 0.0)
                 W[i, t] = inverse
                 for c in range(3):
-                    load = load_of(c, i, t)
-                    z = inverse * load
+                    here = load_of(c, i, t)
+                    z = inverse * here
                     Z[0, c, i, t] = z
                     store_parts(c, i, t, z)
                     if in_block(i, t):
-                        bz = bz + z * load
+                        L0[c, i - 4] = here
+                        bz = bz + z * here
             before = summed
 
     def yz_modes(i, t):
@@ -475,7 +522,7 @@
                 h00 = add(h00, i, t, z, q)
                 h01 = add(h01, i, t, y, q)
                 if in_block(i, t):
-                    b1 = b1 + y * load_of(c, i, t)
+                    b1 = b1 + y * L0[c, i - 4]
     apply(1)
     for t in range(2):
         for i in range(3, NI - 2):
@@ -488,7 +535,7 @@
                 h11 = add(h11, i, t, z, q)
                 h12 = add(h12, i, t, y, q)
                 if in_block(i, t):
-                    b2 = b2 + y * load_of(c, i, t)
+                    b2 = b2 + y * L0[c, i - 4]
     apply(2)
     for i in range(4, 4 + RX):
         for c in range(3):
@@ -541,13 +588,13 @@
 VMEM = pl.BlockSpec(memory_space=pltpu.VMEM)
 
 
-def call(kernel, inputs, outs, scratch=(), limit=None):
+def call(kernel, inputs, outs, scratch=(), limit=None, extra=0):
     single = not isinstance(outs, list)
     shapes = [outs] if single else outs
     result = pl.pallas_call(
         kernel,
         out_shape=[jax.ShapeDtypeStruct(s, F32) for s in shapes],
-        in_specs=[VMEM] * len(inputs),
+        in_specs=[VMEM] * (len(inputs) - extra) + [pl.BlockSpec(memory_space=pl.ANY)] * extra,
         out_specs=[VMEM] * len(shapes),
         scratch_shapes=[pltpu.VMEM(s, F32) for s in scratch],
         compiler_params=pltpu.CompilerParams(vmem_limit_bytes=limit or 32 * 1024 * 1024),
@@ -556,6 +603,7 @@
 
 
 MAIN_SCRATCH = [
+    (3, RX, 8, NZ),
     (3, NI - 1, 8, NZ),
     (NI - 1, 8, NZ),
     (3, RX + 3, 8, NZ),
@@ -574,7 +622,7 @@
 
 
 def shards(displacement, adjoint_load, density, fixed_mask, load_nodes, load_forces):
-    gx, gy = ("x", "y"), ("z", "c")
+    gx = ("x", "y")
     count_x = lax.axis_size("x") * lax.axis_size("y")
     count_y = lax.axis_size("z") * lax.axis_size("c")
     own = (adjoint_load, displacement, density, fixed_mask)
@@ -593,28 +641,22 @@
     )(*own)
     low = lax.ppermute(low, gx, [(i, i + 1) for i in range(count_x - 1)])
     up = lax.ppermute(up, gx, [(i + 1, i) for i in range(count_x - 1)])
-    placed = call(loads_kernel, (load_nodes, load_forces), (3, NI - 1, RY, NZ))
-    ld, fr, dn, di, first, second = call(
-        pack_y_kernel,
-        own + (placed, low, up),
-        [
-            (3, NI - 1, RY, NZ),
-            (NI - 1, RY, NZ),
-            (NI + 2, RY, NZ),
-            (3, RX + 3, RY, NZ),
-            (BLOCKS, 4, NZ),
-            (BLOCKS, 4, NZ),
-        ],
+    sizes = (NEAR + CORNER, 4, NZ)
+    second = call(functools.partial(pack_y_kernel, 1), own + (low, up), (NEAR + CORNER + 1, 4, NZ))
+    pairs = [(i, i + 1) for i in range(1, count_y - 1, 2)]
+    pairs = pairs + [(j, i) for i, j in pairs]
+    placed = call(
+        loads_kernel, (load_nodes, load_forces, low), (3, NI - 1, 2, RY, NZ), extra=1
     )
-    pairs = [(i, i + 1) for i in range(1, count_y - 1, 2)]
-    second = lax.ppermute(second, gy, pairs + [(j, i) for i, j in pairs])
+    first = call(functools.partial(pack_y_kernel, 0), own + (low, up, placed), sizes, extra=1)
+    second = lax.ppermute(second, ("z", "c"), pairs)
     first = lax.ppermute(first, "c", [(0, 1), (1, 0)])
-    near = lax.axis_size("c") * count_x
+    close = lax.axis_size("c") * count_x
     far = lax.axis_size("z")
     basis, senses, sums = call(
         main_kernel,
-        (ld, fr, dn, di, first, second),
-        [(3, 3, RX, RY, NZ), (3, RX, RY, NZ), (near, 1, NZ)],
+        own + (low, up, placed, first, second),
+        [(3, 3, RX, RY, NZ), (3, RX, RY, NZ), (close, 1, NZ)],
         MAIN_SCRATCH,
         48 * 1024 * 1024,
     )

time: 73.5 us -> 71.3 us (0.970)
  waiting for transfers between devices: 5.76 us -> 2.92 us
  blocking collectives: 38.4 us -> 40.4 us
  starting transfers between devices: 17.2 us -> 15.9 us
    ppermute x1, waiting for transfers between devices: 5.75 us -> 0.01 us  [shards(): second = lax.ppermute(second, ('z', 'c'), pairs)]
    ppermute x1, starting transfers between devices: 9.22 us -> 4.53 us  [shards(): first = lax.ppermute(first, 'c', [(0, 1), (1, 0)])]
    ppermute x1, starting transfers between devices: 1.92 us -> 5.4 us  [shards(): second = lax.ppermute(second, ('z', 'c'), pairs)]
    all_to_all x1, blocking collectives: 11.3 us -> 14.5 us  [shards(): sums = lax.all_to_all(sums, ('x', 'y', 'c'), 0, 0, tiled=True)]
    ppermute x1, waiting for transfers between devices: 0.01 us -> 1.78 us  [shards(): low = lax.ppermute(low, gx, [(i, i + 1) for i in range(count_x - 1)])]
    all_to_all x1, blocking collectives: 27.1 us -> 26 us  [shards(): sums = lax.all_to_all(sums, 'z', 0, 0, tiled=True)]
    ppermute x1, waiting for transfers between devices: 0.01 us -> 1.14 us  [shards(): first = lax.ppermute(first, 'c', [(0, 1), (1, 0)])]
    pallas_call x4 -> x5, Pallas kernels: 9.13 us -> 9.16 us  [call(): pl.pallas_call(kernel, out_shape=[jax.ShapeDtypeStruct(s, F32) for s in s...]
  transfers between devices with their start and end apart: 4 -> 4, of which waited for: 1 -> 2; matrix products, arithmetic and copies ran while one was open for 0% -> 0% of each run, Pallas kernels for 2% -> 3%
where the time goes in v3:
time: 71.3 us; the launch traced here: 71 us
  blocking collectives  40.4 us (57%)
  starting transfers between devices  15.9 us (22%)
  Pallas kernels  10.9 us (15%)
  waiting for transfers between devices  2.92 us (4%)
  between operations  0.78 us (1%)
    all_to_all x1, blocking collectives, shards(): sums = lax.all_to_all(sums, 'z', 0, 0, tiled=True)  26 us
    all_to_all x1, blocking collectives, shards(): sums = lax.all_to_all(sums, ('x', 'y', 'c'), 0, 0, tiled=True)  14.5 us
    pallas_call x5, Pallas kernels, call(): pl.pallas_call(kernel, out_shape=[jax.ShapeDtypeStruct(s, F32) for s in s...  9.16 us
    ppermute x1, starting transfers between devices, shards(): second = lax.ppermute(second, ('z', 'c'), pairs)  5.4 us
    ppermute x1, starting transfers between devices, shards(): low = lax.ppermute(low, gx, [(i, i + 1) for i in range(count_x - 1)])  4.66 us
    ppermute x1, starting transfers between devices, shards(): first = lax.ppermute(first, 'c', [(0, 1), (1, 0)])  4.53 us
    ppermute x1, waiting for transfers between devices, shards(): low = lax.ppermute(low, gx, [(i, i + 1) for i in range(count_x - 1)])  1.78 us
    pallas_call x1, Pallas kernels, shards(): pl.pallas_call(pack_x_kernel, out_shape=[jax.ShapeDtypeStruct((LOW_X, RY,...  1.74 us
  transfers between devices with their start and end apart: 4, of which 2 were waited for; matrix products, arithmetic and copies ran while one was open for 0% of the time, Pallas kernels for 3%

profile of v3, /device:TPU:1, one launch (start us, length us, event | category | flops | bytes accessed | tf_op | source)
XLA Modules:
  0.0 71.0 jit_solution(13535846447608183461)
XLA Ops:
  0.6 0.0 copy-start.3
  0.6 0.0 copy-start.2
  0.7 0.0 copy-start
  0.7 0.0 copy-start.1
  0.7 1.7 %shard_map.77 = (f32[20,8,128]{2,1,0:T(8,128)}, f32[27,8,128]{2,1,0:T(8,128)}) custom-call(f32[3,12,8,128]{3,2,1,0:T(8,128)} %load.7, f32[3,12,8,128]{3,2,1,0:T(8,128)} %disp.7, f32[12,8,128]{2,1,0:T(8,128)} %dens.7, s32[12,8,128]{2,1,0:T(8,128)} %mask.7), custom_call_target="tpu_custom_call" | custom-call | tf_op jit(solution)/shard_map/pallas_call | solution.py:629
  2.4 1.3 %collective-permute-start.1 = (f32[27,8,128]{2,1,0:T(8,128)}, f32[27,8,128]{2,1,0:T(8,128)S(1)}, u32[]{:S(2)}, u32[]{:S(2)}) collective-permute-start(f32[27,8,128]{2,1,0:T(8,128)} %get-tuple-element.8), channel_id=1, source_target_pairs={{32,0},{64,32},{96,64},{128,96},{160,128},{192,160},{224,192},{256... | collective-permute-start | bytes 331784 | tf_op jit(solution)/shard_map/ppermute | solution.py:643
  3.7 0.0 copy-start.4
  3.7 0.0 copy-start.5
  3.7 4.7 %collective-permute-start = (f32[20,8,128]{2,1,0:T(8,128)}, f32[20,8,128]{2,1,0:T(8,128)S(1)}, u32[]{:S(2)}, u32[]{:S(2)}) collective-permute-start(f32[20,8,128]{2,1,0:T(8,128)} %get-tuple-element.7), channel_id=1, source_target_pairs={{0,32},{32,64},{64,96},{96,128},{128,160},{160,192},{192,224},{224... | collective-permute-start | bytes 245768 | tf_op jit(solution)/shard_map/ppermute | solution.py:642
  8.4 1.8 %collective-permute-done._.low = f32[20,8,128]{2,1,0:T(8,128)S(1)} collective-permute-done((f32[20,8,128]{2,1,0:T(8,128)}, f32[20,8,128]{2,1,0:T(8,128)S(1)}, u32[]{:S(2)}, u32[]{:S(2)}) %collective-permute-start) | collective-permute-done | bytes 81952 | tf_op jit(solution)/shard_map/ppermute | solution.py:642
  10.2 0.0 collective-permute-done.1.up
  10.2 0.0 copy-done.3
  10.2 0.0 copy-done.2
  10.2 0.0 copy-done
  10.2 0.0 copy-done.1
  10.2 0.1 shard_map.80
  10.3 5.4 %collective-permute-start.3 = (f32[128,4,128]{2,1,0:T(4,128)S(1)}, f32[128,4,128]{2,1,0:T(4,128)S(1)}, u32[]{:S(2)}, u32[]{:S(2)}) collective-permute-start(f32[128,4,128]{2,1,0:T(4,128)S(1)} %shard_map.80), channel_id=1, source_target_pairs={{1,2},{3,4},{5,6},{7,8},{9,10},{11,12},{13,14},{15,16},{17,18},{19... | collective-permute-start | bytes 786440 | tf_op jit(solution)/shard_map/ppermute | solution.py:652
  15.7 0.0 copy-done.4
  15.7 0.0 copy-done.5
  15.7 1.8 %shard_map.78.rest_0_.placed = f32[3,19,2,8,128]{4,3,2,1,0:T(8,128)S(1)} custom-call(s32[3,2048]{1,0:T(4,128)S(1)} %copy-done.4, f32[3,2048]{1,0:T(4,128)S(1)} %copy-done.5, f32[20,8,128]{2,1,0:T(8,128)S(1)} %collective-permute-done._.low), custom_call_target="tpu_custom_call" | custom-call | tf_op jit(solution)/shard_map/pallas_call | solution.py:594
  17.6 0.1 shard_map.79
  17.6 4.5 %collective-permute-start.2 = (f32[127,4,128]{2,1,0:T(4,128)S(1)}, f32[127,4,128]{2,1,0:T(4,128)S(1)}, u32[]{:S(2)}, u32[]{:S(2)}) collective-permute-start(f32[127,4,128]{2,1,0:T(4,128)S(1)} %shard_map.79), channel_id=1, source_target_pairs={{0,1},{1,0},{2,3},{3,2},{4,5},{5,4},{6,7},{7,6},{8,9},{9,8},{10,11... | collective-permute-start | bytes 780296 | tf_op jit(solution)/shard_map/ppermute | solution.py:653
  22.2 1.1 %collective-permute-done.2.first = f32[127,4,128]{2,1,0:T(4,128)S(1)} collective-permute-done((f32[127,4,128]{2,1,0:T(4,128)S(1)}, f32[127,4,128]{2,1,0:T(4,128)S(1)}, u32[]{:S(2)}, u32[]{:S(2)}) %collective-permute-start.2) | collective-permute-done | bytes 260128 | tf_op jit(solution)/shard_map/ppermute | solution.py:653
  23.3 0.0 collective-permute-done.3.second
  23.3 6.4 %shard_map.81 = (f32[3,3,12,8,128]{4,3,2,1,0:T(8,128)S(1)}, f32[3,12,8,128]{3,2,1,0:T(8,128)S(1)}, f32[32,1,128]{2,1,0:T(1,128)S(1)}) custom-call(f32[3,12,8,128]{3,2,1,0:T(8,128)S(1)} %copy-done, f32[3,12,8,128]{3,2,1,0:T(8,128)S(1)} %copy-done.1, f32[12,8,128]{2,1,0:T(8,128)S(1)} %copy-done.2, s32[12,8,128]{2,1,0:T(8,128)S(1)} %copy-done.3, ...), custom_call_target="tpu_custom_call" | custom-call | tf_op jit(solution)/shard_map/pallas_call | solution.py:594
  29.7 14.5 %all_to_all.10 = f32[32,1,128]{2,1,0:T(1,128)S(1)} all-to-all(f32[32,1,128]{2,1,0:T(1,128)S(1)} %get-tuple-element.9), channel_id=1, replica_groups=mesh['x'=4,'y'=4,'z'=16,'c'=2] {'x','y','c'}, dimensions={0} | all-to-all | bytes 32768 | tf_op jit(solution)/shard_map/all_to_all | solution.py:663
  44.2 0.1 reduce_sum.9
  44.2 26.0 %all_to_all.11.gathered = f32[16,1,128]{2,1,0:T(1,128)S(1)} all-to-all(f32[16,1,128]{2,1,0:T(1,128)S(1)} %broadcast_in_dim.2), channel_id=1, replica_groups=mesh['x'=4,'y'=4,'z'=16,'c'=2] {'z'}, dimensions={0} | all-to-all | bytes 16384 | tf_op jit(solution)/shard_map/all_to_all | solution.py:665
  70.2 0.8 %shard_map.82 = (f32[3,12,8,128]{3,2,1,0:T(8,128)}, f32[12,8,128]{2,1,0:T(8,128)}) custom-call(f32[16,1,128]{2,1,0:T(1,128)S(1)} %all_to_all.11.gathered, f32[3,3,12,8,128]{4,3,2,1,0:T(8,128)S(1)} %get-tuple-element.10.basis, f32[3,12,8,128]{3,2,1,0:T(8,128)S(1)} %get-tuple-element.11.senses), custom_call_target="tpu_custom_call" | custom-call | tf_op jit(solution)/shard_map/pallas_call | solution.py:594
  (1 shorter events, 0.0 us)
Async XLA Ops:
  0.6 9.6 %copy-start.3 = (s32[12,8,128]{2,1,0:T(8,128)S(1)}, s32[12,8,128]{2,1,0:T(8,128)}, u32[]{:S(2)}) copy-start(s32[12,8,128]{2,1,0:T(8,128)} %mask.7) | copy-start | bytes 147460
  0.6 9.6 %copy-start.2 = (f32[12,8,128]{2,1,0:T(8,128)S(1)}, f32[12,8,128]{2,1,0:T(8,128)}, u32[]{:S(2)}) copy-start(f32[12,8,128]{2,1,0:T(8,128)} %dens.7) | copy-start | bytes 147460
  0.7 9.6 %copy-start = (f32[3,12,8,128]{3,2,1,0:T(8,128)S(1)}, f32[3,12,8,128]{3,2,1,0:T(8,128)}, u32[]{:S(2)}) copy-start(f32[3,12,8,128]{3,2,1,0:T(8,128)} %load.7) | copy-start | bytes 442372
  0.7 9.6 %copy-start.1 = (f32[3,12,8,128]{3,2,1,0:T(8,128)S(1)}, f32[3,12,8,128]{3,2,1,0:T(8,128)}, u32[]{:S(2)}) copy-start(f32[3,12,8,128]{3,2,1,0:T(8,128)} %disp.7) | copy-start | bytes 442372
  2.4 7.8 %collective-permute-start.1 = (f32[27,8,128]{2,1,0:T(8,128)}, f32[27,8,128]{2,1,0:T(8,128)S(1)}, u32[]{:S(2)}, u32[]{:S(2)}) collective-permute-start(f32[27,8,128]{2,1,0:T(8,128)} %get-tuple-element.8), channel_id=1, source_target_pairs={{32,0},{64,32},{96,64},{128,96},{160,128},{192,160},{224,192},{256... | collective-permute-start | bytes 331784 | tf_op jit(solution)/shard_map/ppermute | solution.py:643
  3.7 12.0 %copy-start.4 = (s32[3,2048]{1,0:T(4,128)S(1)}, s32[3,2048]{1,0:T(4,128)}, u32[]{:S(2)}) copy-start(s32[3,2048]{1,0:T(4,128)} %nodes.1) | copy-start | bytes 73732
  3.7 12.0 %copy-start.5 = (f32[3,2048]{1,0:T(4,128)S(1)}, f32[3,2048]{1,0:T(4,128)}, u32[]{:S(2)}) copy-start(f32[3,2048]{1,0:T(4,128)} %forces.1) | copy-start | bytes 73732
  3.7 6.4 %collective-permute-start = (f32[20,8,128]{2,1,0:T(8,128)}, f32[20,8,128]{2,1,0:T(8,128)S(1)}, u32[]{:S(2)}, u32[]{:S(2)}) collective-permute-start(f32[20,8,128]{2,1,0:T(8,128)} %get-tuple-element.7), channel_id=1, source_target_pairs={{0,32},{32,64},{64,96},{96,128},{128,160},{160,192},{192,224},{224... | collective-permute-start | bytes 245768 | tf_op jit(solution)/shard_map/ppermute | solution.py:642
  10.3 13.0 %collective-permute-start.3 = (f32[128,4,128]{2,1,0:T(4,128)S(1)}, f32[128,4,128]{2,1,0:T(4,128)S(1)}, u32[]{:S(2)}, u32[]{:S(2)}) collective-permute-start(f32[128,4,128]{2,1,0:T(4,128)S(1)} %shard_map.80), channel_id=1, source_target_pairs={{1,2},{3,4},{5,6},{7,8},{9,10},{11,12},{13,14},{15,16},{17,18},{19... | collective-permute-start | bytes 786440 | tf_op jit(solution)/shard_map/ppermute | solution.py:652
  17.6 5.7 %collective-permute-start.2 = (f32[127,4,128]{2,1,0:T(4,128)S(1)}, f32[127,4,128]{2,1,0:T(4,128)S(1)}, u32[]{:S(2)}, u32[]{:S(2)}) collective-permute-start(f32[127,4,128]{2,1,0:T(4,128)S(1)} %shard_map.79), channel_id=1, source_target_pairs={{0,1},{1,0},{2,3},{3,2},{4,5},{5,4},{6,7},{7,6},{8,9},{9,8},{10,11... | collective-permute-start | bytes 780296 | tf_op jit(solution)/shard_map/ppermute | solution.py:653

commit v4 on v3

--- a/solution.py
+++ b/solution.py
@@ -352,14 +352,12 @@
         part_a.append(1.5 + 0.5 * (near_y + near_z) + EDGE * near_y * near_z)
         part_b.append(0.5 + EDGE * (near_y + near_z))
 
-    def filter_parts(cells, beside):
-        deep = up_z(cells, lane) + down_z(cells, lane)
-        deep_beside = up_z(beside, lane) + down_z(beside, lane)
-        around = deep + beside
-        return (
-            1.5 * cells + 0.5 * around + EDGE * deep_beside,
-            0.5 * cells + EDGE * around,
-        )
+    def filtered(cells, beside, p):
+        side = cells[p - 1] + cells[p + 1]
+        far = beside[p - 1] + beside[p + 1]
+        deep = 0.5 * cells[p] + EDGE * (beside[p] + side)
+        deep = up_z(deep, lane) + down_z(deep, lane)
+        return 1.5 * cells[p] + 0.5 * (beside[p] + side) + EDGE * far + deep
 
     def density_rows(p, t, shift):
         if t == 0:
@@ -369,10 +367,10 @@
         )
 
     for t in range(2):
-        window = []
+        cells, beside = [], []
         for p in range(NI + 2):
-            beside = density_rows(p, t, -1) + density_rows(p, t, 1)
-            window.append(filter_parts(density_rows(p, t, 0), beside))
+            cells.append(density_rows(p, t, 0))
+            beside.append(density_rows(p, t, -1) + density_rows(p, t, 1))
             i = p - 2
             if i < 0:
                 continue
@@ -380,7 +378,7 @@
             inside_x = jnp.where((place_x >= 0) & (place_x < extent_x), 1.0, 0.0)
             near_x = 2.0 - jnp.where(place_x == 0, 1.0, 0.0) - jnp.where(place_x == extent_x - 1, 1.0, 0.0)
             inverse = 1.0 / (part_a[t] + near_x * part_b[t])
-            physical = (window[-2][0] + window[-3][1] + window[-1][1]) * inverse
+            physical = filtered(cells, beside, p - 1) * inverse
             squared = physical * physical
             inside = inside_y[t] * inside_x
             mod = inside * (SOFT + (1.0 - SOFT) * (squared * physical))
@@ -553,12 +551,12 @@
         sums[n] = line
 
     for k in range(3):
-        window = []
+        cells, beside = [], []
         for p in range(RX + 2):
-            beside = DV[k, p, 7:15] + DV[k, p, 9:17]
-            window.append(filter_parts(DV[k, p, 8:16], beside))
+            cells.append(DV[k, p, 8:16])
+            beside.append(DV[k, p, 7:15] + DV[k, p, 9:17])
             if p >= 2:
-                senses[k, p - 2] = window[-2][0] + window[-3][1] + window[-1][1]
+                senses[k, p - 2] = filtered(cells, beside, p - 1)
         for c in range(3):
             basis[k, c] = Z[k, c, 4 : 4 + RX, 0]
 
@@ -629,10 +627,10 @@
     low, up = pl.pallas_call(
         pack_x_kernel,
         out_shape=[
-            jax.ShapeDtypeStruct((LOW_X, RY, NZ), F32),
-            jax.ShapeDtypeStruct((UP_X, RY, NZ), F32),
+            pltpu.VMEM((LOW_X, RY, NZ), F32),
+            pltpu.VMEM((UP_X, RY, NZ), F32),
         ],
-        in_specs=[pl.BlockSpec(memory_space=pl.ANY)] * 4,
+        in_specs=[pl.BlockSpec(memory_space=pltpu.HBM)] * 4,
         out_specs=[VMEM] * 2,
         scratch_shapes=[
             pltpu.VMEM((7, RY, NZ), jnp.int32),

time: 71.3 us -> 69.6 us (0.976)
  Pallas kernels: 10.9 us -> 9.35 us
    pallas_call x5, Pallas kernels: 9.16 us -> 8.29 us  [call(): pl.pallas_call(kernel, out_shape=[jax.ShapeDtypeStruct(s, F32) for s in s...]
where the time goes in v4:
time: 69.6 us; the launch traced here: 69.2 us
  blocking collectives  40.5 us (58%)
  starting transfers between devices  15.9 us (23%)
  Pallas kernels  9.35 us (13%)
  waiting for transfers between devices  2.61 us (4%)
  between operations  0.78 us (1%)
    all_to_all x1, blocking collectives, shards(): sums = lax.all_to_all(sums, 'z', 0, 0, tiled=True)  26 us
    all_to_all x1, blocking collectives, shards(): sums = lax.all_to_all(sums, ('x', 'y', 'c'), 0, 0, tiled=True)  14.6 us
    pallas_call x5, Pallas kernels, call(): pl.pallas_call(kernel, out_shape=[jax.ShapeDtypeStruct(s, F32) for s in s...  8.29 us
    ppermute x1, starting transfers between devices, shards(): second = lax.ppermute(second, ('z', 'c'), pairs)  5.4 us
    ppermute x1, starting transfers between devices, shards(): low = lax.ppermute(low, gx, [(i, i + 1) for i in range(count_x - 1)])  4.66 us
    ppermute x1, starting transfers between devices, shards(): first = lax.ppermute(first, 'c', [(0, 1), (1, 0)])  4.53 us
    ppermute x1, waiting for transfers between devices, shards(): low = lax.ppermute(low, gx, [(i, i + 1) for i in range(count_x - 1)])  1.46 us
  transfers between devices with their start and end apart: 4, of which 2 were waited for; matrix products, arithmetic and copies ran while one was open for 0% of the time, Pallas kernels for 3%

profile of v4, /device:TPU:1, one launch (start us, length us, event | category | flops | bytes accessed | tf_op | source)
XLA Modules:
  0.0 69.2 jit_solution(2307177083161836605)
XLA Ops:
  0.6 0.0 copy-start.3
  0.6 0.0 copy-start.2
  0.7 0.0 copy-start
  0.7 0.0 copy-start.1
  0.7 1.1 %shard_map.77 = (f32[20,8,128]{2,1,0:T(8,128)S(1)}, f32[27,8,128]{2,1,0:T(8,128)S(1)}) custom-call(f32[3,12,8,128]{3,2,1,0:T(8,128)} %load.7, f32[3,12,8,128]{3,2,1,0:T(8,128)} %disp.7, f32[12,8,128]{2,1,0:T(8,128)} %dens.7, s32[12,8,128]{2,1,0:T(8,128)} %mask.7), custom_call_target="tpu_custom_call" | custom-call | tf_op jit(solution)/shard_map/pallas_call | solution.py:627
  1.7 1.3 %collective-permute-start.1 = (f32[27,8,128]{2,1,0:T(8,128)S(1)}, f32[27,8,128]{2,1,0:T(8,128)S(1)}, u32[]{:S(2)}, u32[]{:S(2)}) collective-permute-start(f32[27,8,128]{2,1,0:T(8,128)S(1)} %get-tuple-element.8), channel_id=1, source_target_pairs={{32,0},{64,32},{96,64},{128,96},{160,128},{192,160},{224,192},{256... | collective-permute-start | bytes 331784 | tf_op jit(solution)/shard_map/ppermute | solution.py:641
  3.0 0.0 copy-start.4
  3.1 0.0 copy-start.5
  3.1 4.7 %collective-permute-start = (f32[20,8,128]{2,1,0:T(8,128)S(1)}, f32[20,8,128]{2,1,0:T(8,128)S(1)}, u32[]{:S(2)}, u32[]{:S(2)}) collective-permute-start(f32[20,8,128]{2,1,0:T(8,128)S(1)} %get-tuple-element.7), channel_id=1, source_target_pairs={{0,32},{32,64},{64,96},{96,128},{128,160},{160,192},{192,224},{224... | collective-permute-start | bytes 245768 | tf_op jit(solution)/shard_map/ppermute | solution.py:640
  7.7 1.5 %collective-permute-done._.low = f32[20,8,128]{2,1,0:T(8,128)S(1)} collective-permute-done((f32[20,8,128]{2,1,0:T(8,128)S(1)}, f32[20,8,128]{2,1,0:T(8,128)S(1)}, u32[]{:S(2)}, u32[]{:S(2)}) %collective-permute-start) | collective-permute-done | bytes 81952 | tf_op jit(solution)/shard_map/ppermute | solution.py:640
  9.2 0.0 collective-permute-done.1.up
  9.2 0.0 copy-done.3
  9.2 0.0 copy-done.2
  9.2 0.0 copy-done
  9.2 0.0 copy-done.1
  9.2 0.1 shard_map.80
  9.3 5.4 %collective-permute-start.3 = (f32[128,4,128]{2,1,0:T(4,128)S(1)}, f32[128,4,128]{2,1,0:T(4,128)S(1)}, u32[]{:S(2)}, u32[]{:S(2)}) collective-permute-start(f32[128,4,128]{2,1,0:T(4,128)S(1)} %shard_map.80), channel_id=1, source_target_pairs={{1,2},{3,4},{5,6},{7,8},{9,10},{11,12},{13,14},{15,16},{17,18},{19... | collective-permute-start | bytes 786440 | tf_op jit(solution)/shard_map/ppermute | solution.py:650
  14.7 0.0 copy-done.4
  14.7 0.0 copy-done.5
  14.7 1.8 %shard_map.78.rest_0_.placed = f32[3,19,2,8,128]{4,3,2,1,0:T(8,128)S(1)} custom-call(s32[3,2048]{1,0:T(4,128)S(1)} %copy-done.4, f32[3,2048]{1,0:T(4,128)S(1)} %copy-done.5, f32[20,8,128]{2,1,0:T(8,128)S(1)} %collective-permute-done._.low), custom_call_target="tpu_custom_call" | custom-call | tf_op jit(solution)/shard_map/pallas_call | solution.py:592
  16.6 0.1 shard_map.79
  16.6 4.5 %collective-permute-start.2 = (f32[127,4,128]{2,1,0:T(4,128)S(1)}, f32[127,4,128]{2,1,0:T(4,128)S(1)}, u32[]{:S(2)}, u32[]{:S(2)}) collective-permute-start(f32[127,4,128]{2,1,0:T(4,128)S(1)} %shard_map.79), channel_id=1, source_target_pairs={{0,1},{1,0},{2,3},{3,2},{4,5},{5,4},{6,7},{7,6},{8,9},{9,8},{10,11... | collective-permute-start | bytes 780296 | tf_op jit(solution)/shard_map/ppermute | solution.py:651
  21.2 1.1 %collective-permute-done.2.first = f32[127,4,128]{2,1,0:T(4,128)S(1)} collective-permute-done((f32[127,4,128]{2,1,0:T(4,128)S(1)}, f32[127,4,128]{2,1,0:T(4,128)S(1)}, u32[]{:S(2)}, u32[]{:S(2)}) %collective-permute-start.2) | collective-permute-done | bytes 260128 | tf_op jit(solution)/shard_map/ppermute | solution.py:651
  22.3 0.0 collective-permute-done.3.second
  22.3 5.5 %shard_map.81 = (f32[3,3,12,8,128]{4,3,2,1,0:T(8,128)S(1)}, f32[3,12,8,128]{3,2,1,0:T(8,128)S(1)}, f32[32,1,128]{2,1,0:T(1,128)S(1)}) custom-call(f32[3,12,8,128]{3,2,1,0:T(8,128)S(1)} %copy-done, f32[3,12,8,128]{3,2,1,0:T(8,128)S(1)} %copy-done.1, f32[12,8,128]{2,1,0:T(8,128)S(1)} %copy-done.2, s32[12,8,128]{2,1,0:T(8,128)S(1)} %copy-done.3, ...), custom_call_target="tpu_custom_call" | custom-call | tf_op jit(solution)/shard_map/pallas_call | solution.py:592
  27.8 14.6 %all_to_all.10 = f32[32,1,128]{2,1,0:T(1,128)S(1)} all-to-all(f32[32,1,128]{2,1,0:T(1,128)S(1)} %get-tuple-element.9), channel_id=1, replica_groups=mesh['x'=4,'y'=4,'z'=16,'c'=2] {'x','y','c'}, dimensions={0} | all-to-all | bytes 32768 | tf_op jit(solution)/shard_map/all_to_all | solution.py:661
  42.4 0.1 reduce_sum.9
  42.5 26.0 %all_to_all.11.gathered = f32[16,1,128]{2,1,0:T(1,128)S(1)} all-to-all(f32[16,1,128]{2,1,0:T(1,128)S(1)} %broadcast_in_dim.2), channel_id=1, replica_groups=mesh['x'=4,'y'=4,'z'=16,'c'=2] {'z'}, dimensions={0} | all-to-all | bytes 16384 | tf_op jit(solution)/shard_map/all_to_all | solution.py:663
  68.4 0.8 %shard_map.82 = (f32[3,12,8,128]{3,2,1,0:T(8,128)}, f32[12,8,128]{2,1,0:T(8,128)}) custom-call(f32[16,1,128]{2,1,0:T(1,128)S(1)} %all_to_all.11.gathered, f32[3,3,12,8,128]{4,3,2,1,0:T(8,128)S(1)} %get-tuple-element.10.basis, f32[3,12,8,128]{3,2,1,0:T(8,128)S(1)} %get-tuple-element.11.senses), custom_call_target="tpu_custom_call" | custom-call | tf_op jit(solution)/shard_map/pallas_call | solution.py:592
  (1 shorter events, 0.0 us)
Async XLA Ops:
  0.6 8.6 %copy-start.3 = (s32[12,8,128]{2,1,0:T(8,128)S(1)}, s32[12,8,128]{2,1,0:T(8,128)}, u32[]{:S(2)}) copy-start(s32[12,8,128]{2,1,0:T(8,128)} %mask.7) | copy-start | bytes 147460
  0.6 8.6 %copy-start.2 = (f32[12,8,128]{2,1,0:T(8,128)S(1)}, f32[12,8,128]{2,1,0:T(8,128)}, u32[]{:S(2)}) copy-start(f32[12,8,128]{2,1,0:T(8,128)} %dens.7) | copy-start | bytes 147460
  0.7 8.6 %copy-start = (f32[3,12,8,128]{3,2,1,0:T(8,128)S(1)}, f32[3,12,8,128]{3,2,1,0:T(8,128)}, u32[]{:S(2)}) copy-start(f32[3,12,8,128]{3,2,1,0:T(8,128)} %load.7) | copy-start | bytes 442372
  0.7 8.6 %copy-start.1 = (f32[3,12,8,128]{3,2,1,0:T(8,128)S(1)}, f32[3,12,8,128]{3,2,1,0:T(8,128)}, u32[]{:S(2)}) copy-start(f32[3,12,8,128]{3,2,1,0:T(8,128)} %disp.7) | copy-start | bytes 442372
  1.7 7.5 %collective-permute-start.1 = (f32[27,8,128]{2,1,0:T(8,128)S(1)}, f32[27,8,128]{2,1,0:T(8,128)S(1)}, u32[]{:S(2)}, u32[]{:S(2)}) collective-permute-start(f32[27,8,128]{2,1,0:T(8,128)S(1)} %get-tuple-element.8), channel_id=1, source_target_pairs={{32,0},{64,32},{96,64},{128,96},{160,128},{192,160},{224,192},{256... | collective-permute-start | bytes 331784 | tf_op jit(solution)/shard_map/ppermute | solution.py:641
  3.0 11.7 %copy-start.4 = (s32[3,2048]{1,0:T(4,128)S(1)}, s32[3,2048]{1,0:T(4,128)}, u32[]{:S(2)}) copy-start(s32[3,2048]{1,0:T(4,128)} %nodes.1) | copy-start | bytes 73732
  3.1 11.7 %copy-start.5 = (f32[3,2048]{1,0:T(4,128)S(1)}, f32[3,2048]{1,0:T(4,128)}, u32[]{:S(2)}) copy-start(f32[3,2048]{1,0:T(4,128)} %forces.1) | copy-start | bytes 73732
  3.1 6.1 %collective-permute-start = (f32[20,8,128]{2,1,0:T(8,128)S(1)}, f32[20,8,128]{2,1,0:T(8,128)S(1)}, u32[]{:S(2)}, u32[]{:S(2)}) collective-permute-start(f32[20,8,128]{2,1,0:T(8,128)S(1)} %get-tuple-element.7), channel_id=1, source_target_pairs={{0,32},{32,64},{64,96},{96,128},{128,160},{160,192},{192,224},{224... | collective-permute-start | bytes 245768 | tf_op jit(solution)/shard_map/ppermute | solution.py:640
  9.3 13.0 %collective-permute-start.3 = (f32[128,4,128]{2,1,0:T(4,128)S(1)}, f32[128,4,128]{2,1,0:T(4,128)S(1)}, u32[]{:S(2)}, u32[]{:S(2)}) collective-permute-start(f32[128,4,128]{2,1,0:T(4,128)S(1)} %shard_map.80), channel_id=1, source_target_pairs={{1,2},{3,4},{5,6},{7,8},{9,10},{11,12},{13,14},{15,16},{17,18},{19... | collective-permute-start | bytes 786440 | tf_op jit(solution)/shard_map/ppermute | solution.py:650
  16.6 5.7 %collective-permute-start.2 = (f32[127,4,128]{2,1,0:T(4,128)S(1)}, f32[127,4,128]{2,1,0:T(4,128)S(1)}, u32[]{:S(2)}, u32[]{:S(2)}) collective-permute-start(f32[127,4,128]{2,1,0:T(4,128)S(1)} %shard_map.79), channel_id=1, source_target_pairs={{0,1},{1,0},{2,3},{3,2},{4,5},{5,4},{6,7},{7,6},{8,9},{9,8},{10,11... | collective-permute-start | bytes 780296 | tf_op jit(solution)/shard_map/ppermute | solution.py:651

commit v5 on v4

--- a/solution.py
+++ b/solution.py
@@ -75,7 +75,7 @@
 CORNER_DIAG = float(element_stiffness()[0, 0])
 
 
-def pack_x_kernel(load, disp, dens, mask, low, up, flags, done):
+def pack_x_kernel(load, disp, dens, mask, first, second, low, up, flags, done):
     copies = [(mask.at[RX - 3 : RX], flags.at[0:3]), (mask.at[0:4], flags.at[3:7])]
     for c in range(3):
         copies.append((load.at[c, RX - 3 : RX], low.at[3 * c : 3 * c + 3]))
@@ -94,6 +94,17 @@
         copy.wait()
     low[9:12] = (1 - flags[0:3]).astype(F32)
     up[12:16] = (1 - flags[3:7]).astype(F32)
+    even = lax.rem(lax.axis_index("y"), 2) == 0
+
+    @pl.when(even)
+    def _():
+        first[0:LOW_X] = low[...]
+        second[0:UP_X] = up[...]
+
+    @pl.when(jnp.logical_not(even))
+    def _():
+        first[0:UP_X] = up[...]
+        second[0:LOW_X] = low[...]
 
 
 def loads_kernel(nodes, forces, _, out):
@@ -135,6 +146,22 @@
         )
         for t in range(2):
             out[c, :, t] = summed[:, t * NZ : t * NZ + NZ].reshape(NI - 1, RY, NZ)
+
+
+def pack_second_kernel(load, disp, dens, mask, first, second, out, low, up):
+    even = lax.rem(lax.axis_index("y"), 2) == 0
+
+    @pl.when(even)
+    def _():
+        up[...] = first[0:UP_X]
+        low[...] = second[0:LOW_X]
+
+    @pl.when(jnp.logical_not(even))
+    def _():
+        up[...] = second[0:UP_X]
+        low[...] = first[0:LOW_X]
+
+    pack_y_kernel(1, load, disp, dens, mask, low, up, out)
 
 
 def pack_y_kernel(which, load, disp, dens, mask, low, up, *rest):
@@ -619,36 +646,41 @@
 ]
 
 
+def swaps(start, count):
+    pairs = [(i, i + 1) for i in range(start, count - 1, 2)]
+    return pairs + [(j, i) for i, j in pairs]
+
+
 def shards(displacement, adjoint_load, density, fixed_mask, load_nodes, load_forces):
-    gx = ("x", "y")
     count_x = lax.axis_size("x") * lax.axis_size("y")
     count_y = lax.axis_size("z") * lax.axis_size("c")
     own = (adjoint_load, displacement, density, fixed_mask)
-    low, up = pl.pallas_call(
+    first, second = pl.pallas_call(
         pack_x_kernel,
-        out_shape=[
-            pltpu.VMEM((LOW_X, RY, NZ), F32),
-            pltpu.VMEM((UP_X, RY, NZ), F32),
-        ],
+        out_shape=[pltpu.VMEM((UP_X, RY, NZ), F32), pltpu.VMEM((UP_X + 1, RY, NZ), F32)],
         in_specs=[pl.BlockSpec(memory_space=pltpu.HBM)] * 4,
         out_specs=[VMEM] * 2,
         scratch_shapes=[
+            pltpu.VMEM((LOW_X, RY, NZ), F32),
+            pltpu.VMEM((UP_X, RY, NZ), F32),
             pltpu.VMEM((7, RY, NZ), jnp.int32),
             pltpu.SemaphoreType.DMA((16,)),
         ],
     )(*own)
-    low = lax.ppermute(low, gx, [(i, i + 1) for i in range(count_x - 1)])
-    up = lax.ppermute(up, gx, [(i + 1, i) for i in range(count_x - 1)])
+    second = lax.ppermute(second, ("x", "y"), swaps(1, count_x))
+    first = lax.ppermute(first, ("x", "y"), swaps(0, count_x))
     sizes = (NEAR + CORNER, 4, NZ)
-    second = call(functools.partial(pack_y_kernel, 1), own + (low, up), (NEAR + CORNER + 1, 4, NZ))
-    pairs = [(i, i + 1) for i in range(1, count_y - 1, 2)]
-    pairs = pairs + [(j, i) for i, j in pairs]
+    second, low, up = call(
+        pack_second_kernel,
+        own + (first, second),
+        [(NEAR + CORNER + 1, 4, NZ), (LOW_X, RY, NZ), (UP_X, RY, NZ)],
+    )
     placed = call(
         loads_kernel, (load_nodes, load_forces, low), (3, NI - 1, 2, RY, NZ), extra=1
     )
     first = call(functools.partial(pack_y_kernel, 0), own + (low, up, placed), sizes, extra=1)
-    second = lax.ppermute(second, ("z", "c"), pairs)
-    first = lax.ppermute(first, "c", [(0, 1), (1, 0)])
+    second = lax.ppermute(second, ("z", "c"), swaps(1, count_y))
+    first = lax.ppermute(first, "c", swaps(0, 2))
     close = lax.axis_size("c") * count_x
     far = lax.axis_size("z")
     basis, senses, sums = call(

time: 69.6 us -> 68.1 us (0.978)
  starting transfers between devices: 15.9 us -> 14.6 us
  blocking collectives: 40.5 us -> 39.4 us
  waiting for transfers between devices: 2.61 us -> 3.45 us
    ppermute x4, starting transfers between devices: 15.9 us -> 14.6 us  [the longest x1 6.57 us: shards(): first = lax.ppermute(first, ('x', 'y'), swaps(0, count_x))]
    all_to_all x1, blocking collectives: 14.6 us -> 13.5 us  [shards(): sums = lax.all_to_all(sums, ('x', 'y', 'c'), 0, 0, tiled=True)]
    ppermute x4, waiting for transfers between devices: 2.61 us -> 3.45 us  [the longest x1 2.12 us: shards(): first = lax.ppermute(first, ('x', 'y'), swaps(0, count_x))]
where the time goes in v5:
time: 68.1 us; the launch traced here: 67.8 us
  blocking collectives  39.4 us (58%)
  starting transfers between devices  14.6 us (21%)
  Pallas kernels  9.41 us (14%)
  waiting for transfers between devices  3.45 us (5%)
  between operations  0.78 us (1%)
    all_to_all x1, blocking collectives, shards(): sums = lax.all_to_all(sums, 'z', 0, 0, tiled=True)  26 us
    all_to_all x1, blocking collectives, shards(): sums = lax.all_to_all(sums, ('x', 'y', 'c'), 0, 0, tiled=True)  13.5 us
    pallas_call x5, Pallas kernels, call(): pl.pallas_call(kernel, out_shape=[jax.ShapeDtypeStruct(s, F32) for s in s...  8.32 us
    ppermute x1, starting transfers between devices, shards(): first = lax.ppermute(first, ('x', 'y'), swaps(0, count_x))  6.57 us
    ppermute x1, starting transfers between devices, shards(): second = lax.ppermute(second, ('z', 'c'), swaps(1, count_y))  5.31 us
    ppermute x1, waiting for transfers between devices, shards(): first = lax.ppermute(first, ('x', 'y'), swaps(0, count_x))  2.12 us
    ppermute x1, starting transfers between devices, shards(): first = lax.ppermute(first, 'c', swaps(0, 2))  2.1 us
  transfers between devices with their start and end apart: 4, of which 2 were waited for; matrix products, arithmetic and copies ran while one was open for 0% of the time, Pallas kernels for 3%

profile of v5, /device:TPU:1, one launch (start us, length us, event | category | flops | bytes accessed | tf_op | source)
XLA Modules:
  0.0 67.8 jit_solution(1598130966869029752)
XLA Ops:
  0.6 0.0 copy-start.3
  0.6 0.0 copy-start.2
  0.7 0.0 copy-start
  0.7 0.0 copy-start.1
  0.7 1.1 %shard_map.77 = (f32[27,8,128]{2,1,0:T(8,128)S(1)}, f32[28,8,128]{2,1,0:T(8,128)S(1)}) custom-call(f32[3,12,8,128]{3,2,1,0:T(8,128)} %load.7, f32[3,12,8,128]{3,2,1,0:T(8,128)} %disp.7, f32[12,8,128]{2,1,0:T(8,128)} %dens.7, s32[12,8,128]{2,1,0:T(8,128)} %mask.7), custom_call_target="tpu_custom_call" | custom-call | tf_op jit(solution)/shard_map/pallas_call | solution.py:658
  1.8 0.7 collective-permute-start.1
  2.4 0.0 copy-start.4
  2.5 0.0 copy-start.5
  2.5 6.6 %collective-permute-start = (f32[27,8,128]{2,1,0:T(8,128)S(1)}, f32[27,8,128]{2,1,0:T(8,128)S(1)}, u32[]{:S(2)}, u32[]{:S(2)}) collective-permute-start(f32[27,8,128]{2,1,0:T(8,128)S(1)} %get-tuple-element.10), channel_id=1, source_target_pairs={{0,32},{64,96},{128,160},{192,224},{256,288},{320,352},{384,416},{... | collective-permute-start | bytes 331784 | tf_op jit(solution)/shard_map/ppermute | solution.py:671
  9.0 2.1 %collective-permute-done.first = f32[27,8,128]{2,1,0:T(8,128)S(1)} collective-permute-done((f32[27,8,128]{2,1,0:T(8,128)S(1)}, f32[27,8,128]{2,1,0:T(8,128)S(1)}, u32[]{:S(2)}, u32[]{:S(2)}) %collective-permute-start) | collective-permute-done | bytes 110624 | tf_op jit(solution)/shard_map/ppermute | solution.py:671
  11.2 0.0 collective-permute-done.1.second
  11.2 0.0 copy-done.3
  11.2 0.0 copy-done.2
  11.2 0.0 copy-done
  11.2 0.0 copy-done.1
  11.2 0.1 shard_map.78
  11.3 5.3 %collective-permute-start.3 = (f32[128,4,128]{2,1,0:T(4,128)S(1)}, f32[128,4,128]{2,1,0:T(4,128)S(1)}, u32[]{:S(2)}, u32[]{:S(2)}) collective-permute-start(f32[128,4,128]{2,1,0:T(4,128)S(1)} %get-tuple-element.14), channel_id=1, source_target_pairs={{1,2},{3,4},{5,6},{7,8},{9,10},{11,12},{13,14},{15,16},{17,18},{19... | collective-permute-start | bytes 786440 | tf_op jit(solution)/shard_map/ppermute | solution.py:682
  16.6 0.0 copy-done.4
  16.6 0.0 copy-done.5
  16.6 1.8 %shard_map.79.rest_0_.placed = f32[3,19,2,8,128]{4,3,2,1,0:T(8,128)S(1)} custom-call(s32[3,2048]{1,0:T(4,128)S(1)} %copy-done.4, f32[3,2048]{1,0:T(4,128)S(1)} %copy-done.5, f32[20,8,128]{2,1,0:T(8,128)S(1)} %get-tuple-element.12._.low), custom_call_target="tpu_custom_call" | custom-call | tf_op jit(solution)/shard_map/pallas_call | solution.py:619
  18.5 0.1 shard_map.80
  18.6 2.1 %collective-permute-start.2 = (f32[127,4,128]{2,1,0:T(4,128)S(1)}, f32[127,4,128]{2,1,0:T(4,128)S(1)}, u32[]{:S(2)}, u32[]{:S(2)}) collective-permute-start(f32[127,4,128]{2,1,0:T(4,128)S(1)} %shard_map.80), channel_id=1, source_target_pairs={{0,1},{1,0},{2,3},{3,2},{4,5},{5,4},{6,7},{7,6},{8,9},{9,8},{10,11... | collective-permute-start | bytes 780296 | tf_op jit(solution)/shard_map/ppermute | solution.py:683
  20.7 1.3 %collective-permute-done.2.first = f32[127,4,128]{2,1,0:T(4,128)S(1)} collective-permute-done((f32[127,4,128]{2,1,0:T(4,128)S(1)}, f32[127,4,128]{2,1,0:T(4,128)S(1)}, u32[]{:S(2)}, u32[]{:S(2)}) %collective-permute-start.2) | collective-permute-done | bytes 260128 | tf_op jit(solution)/shard_map/ppermute | solution.py:683
  22.0 0.0 collective-permute-done.3.second
  22.0 5.5 %shard_map.81 = (f32[3,3,12,8,128]{4,3,2,1,0:T(8,128)S(1)}, f32[3,12,8,128]{3,2,1,0:T(8,128)S(1)}, f32[32,1,128]{2,1,0:T(1,128)S(1)}) custom-call(f32[3,12,8,128]{3,2,1,0:T(8,128)S(1)} %copy-done, f32[3,12,8,128]{3,2,1,0:T(8,128)S(1)} %copy-done.1, f32[12,8,128]{2,1,0:T(8,128)S(1)} %copy-done.2, s32[12,8,128]{2,1,0:T(8,128)S(1)} %copy-done.3, ...), custom_call_target="tpu_custom_call" | custom-call | tf_op jit(solution)/shard_map/pallas_call | solution.py:619
  27.5 13.5 %all_to_all.10 = f32[32,1,128]{2,1,0:T(1,128)S(1)} all-to-all(f32[32,1,128]{2,1,0:T(1,128)S(1)} %get-tuple-element.15), channel_id=1, replica_groups=mesh['x'=4,'y'=4,'z'=16,'c'=2] {'x','y','c'}, dimensions={0} | all-to-all | bytes 32768 | tf_op jit(solution)/shard_map/all_to_all | solution.py:693
  41.0 0.1 reduce_sum.9
  41.0 26.0 %all_to_all.11.gathered = f32[16,1,128]{2,1,0:T(1,128)S(1)} all-to-all(f32[16,1,128]{2,1,0:T(1,128)S(1)} %broadcast_in_dim.2), channel_id=1, replica_groups=mesh['x'=4,'y'=4,'z'=16,'c'=2] {'z'}, dimensions={0} | all-to-all | bytes 16384 | tf_op jit(solution)/shard_map/all_to_all | solution.py:695
  67.0 0.8 %shard_map.82 = (f32[3,12,8,128]{3,2,1,0:T(8,128)}, f32[12,8,128]{2,1,0:T(8,128)}) custom-call(f32[16,1,128]{2,1,0:T(1,128)S(1)} %all_to_all.11.gathered, f32[3,3,12,8,128]{4,3,2,1,0:T(8,128)S(1)} %get-tuple-element.16.basis, f32[3,12,8,128]{3,2,1,0:T(8,128)S(1)} %get-tuple-element.17.senses), custom_call_target="tpu_custom_call" | custom-call | tf_op jit(solution)/shard_map/pallas_call | solution.py:619
  (1 shorter events, 0.0 us)
Async XLA Ops:
  0.6 10.5 %copy-start.3 = (s32[12,8,128]{2,1,0:T(8,128)S(1)}, s32[12,8,128]{2,1,0:T(8,128)}, u32[]{:S(2)}) copy-start(s32[12,8,128]{2,1,0:T(8,128)} %mask.7) | copy-start | bytes 147460
  0.6 10.5 %copy-start.2 = (f32[12,8,128]{2,1,0:T(8,128)S(1)}, f32[12,8,128]{2,1,0:T(8,128)}, u32[]{:S(2)}) copy-start(f32[12,8,128]{2,1,0:T(8,128)} %dens.7) | copy-start | bytes 147460
  0.7 10.5 %copy-start = (f32[3,12,8,128]{3,2,1,0:T(8,128)S(1)}, f32[3,12,8,128]{3,2,1,0:T(8,128)}, u32[]{:S(2)}) copy-start(f32[3,12,8,128]{3,2,1,0:T(8,128)} %load.7) | copy-start | bytes 442372
  0.7 10.5 %copy-start.1 = (f32[3,12,8,128]{3,2,1,0:T(8,128)S(1)}, f32[3,12,8,128]{3,2,1,0:T(8,128)}, u32[]{:S(2)}) copy-start(f32[3,12,8,128]{3,2,1,0:T(8,128)} %disp.7) | copy-start | bytes 442372
  1.8 9.4 %collective-permute-start.1 = (f32[28,8,128]{2,1,0:T(8,128)S(1)}, f32[28,8,128]{2,1,0:T(8,128)S(1)}, u32[]{:S(2)}, u32[]{:S(2)}) collective-permute-start(f32[28,8,128]{2,1,0:T(8,128)S(1)} %get-tuple-element.11), channel_id=1, source_target_pairs={{32,64},{96,128},{160,192},{224,256},{288,320},{352,384},{416,448}... | collective-permute-start | bytes 344072 | tf_op jit(solution)/shard_map/ppermute | solution.py:670
  2.4 14.2 %copy-start.4 = (s32[3,2048]{1,0:T(4,128)S(1)}, s32[3,2048]{1,0:T(4,128)}, u32[]{:S(2)}) copy-start(s32[3,2048]{1,0:T(4,128)} %nodes.1) | copy-start | bytes 73732
  2.5 14.2 %copy-start.5 = (f32[3,2048]{1,0:T(4,128)S(1)}, f32[3,2048]{1,0:T(4,128)}, u32[]{:S(2)}) copy-start(f32[3,2048]{1,0:T(4,128)} %forces.1) | copy-start | bytes 73732
  2.5 8.7 %collective-permute-start = (f32[27,8,128]{2,1,0:T(8,128)S(1)}, f32[27,8,128]{2,1,0:T(8,128)S(1)}, u32[]{:S(2)}, u32[]{:S(2)}) collective-permute-start(f32[27,8,128]{2,1,0:T(8,128)S(1)} %get-tuple-element.10), channel_id=1, source_target_pairs={{0,32},{64,96},{128,160},{192,224},{256,288},{320,352},{384,416},{... | collective-permute-start | bytes 331784 | tf_op jit(solution)/shard_map/ppermute | solution.py:671
  11.3 10.7 %collective-permute-start.3 = (f32[128,4,128]{2,1,0:T(4,128)S(1)}, f32[128,4,128]{2,1,0:T(4,128)S(1)}, u32[]{:S(2)}, u32[]{:S(2)}) collective-permute-start(f32[128,4,128]{2,1,0:T(4,128)S(1)} %get-tuple-element.14), channel_id=1, source_target_pairs={{1,2},{3,4},{5,6},{7,8},{9,10},{11,12},{13,14},{15,16},{17,18},{19... | collective-permute-start | bytes 786440 | tf_op jit(solution)/shard_map/ppermute | solution.py:682
  18.6 3.4 %collective-permute-start.2 = (f32[127,4,128]{2,1,0:T(4,128)S(1)}, f32[127,4,128]{2,1,0:T(4,128)S(1)}, u32[]{:S(2)}, u32[]{:S(2)}) collective-permute-start(f32[127,4,128]{2,1,0:T(4,128)S(1)} %shard_map.80), channel_id=1, source_target_pairs={{0,1},{1,0},{2,3},{3,2},{4,5},{5,4},{6,7},{7,6},{8,9},{9,8},{10,11... | collective-permute-start | bytes 780296 | tf_op jit(solution)/shard_map/ppermute | solution.py:683

commit v6 on v5

--- a/solution.py
+++ b/solution.py
@@ -75,39 +75,46 @@
 CORNER_DIAG = float(element_stiffness()[0, 0])
 
 
-def pack_x_kernel(load, disp, dens, mask, first, second, low, up, flags, done):
-    copies = [(mask.at[RX - 3 : RX], flags.at[0:3]), (mask.at[0:4], flags.at[3:7])]
-    for c in range(3):
-        copies.append((load.at[c, RX - 3 : RX], low.at[3 * c : 3 * c + 3]))
-        copies.append((load.at[c, 0:4], up.at[4 * c : 4 * c + 4]))
-        copies.append((disp.at[c, RX - 1 : RX], low.at[17 + c : 18 + c]))
-        copies.append((disp.at[c, 0:2], up.at[21 + 2 * c : 23 + 2 * c]))
-    copies.append((dens.at[RX - 5 : RX], low.at[12:17]))
-    copies.append((dens.at[0:5], up.at[16:21]))
+def pack_x_kernel(*refs):
+    sources, (first, second), targets, done = refs[:6], refs[6:8], refs[8:14], refs[14]
     copies = [
         pltpu.make_async_copy(source, target, done.at[n])
-        for n, (source, target) in enumerate(copies)
+        for n, (source, target) in enumerate(zip(sources, targets))
     ]
     for copy in copies:
         copy.start()
     for copy in copies:
         copy.wait()
-    low[9:12] = (1 - flags[0:3]).astype(F32)
-    up[12:16] = (1 - flags[3:7]).astype(F32)
+    load, disp, dens, mask = targets[:4]
+
+    def put_low(out):
+        for c in range(3):
+            out[3 * c : 3 * c + 3] = load[c, RX - 3 : RX]
+            out[17 + c] = disp[c, RX - 1]
+        out[9:12] = (1 - mask[RX - 3 : RX]).astype(F32)
+        out[12:17] = dens[RX - 5 : RX]
+
+    def put_up(out):
+        for c in range(3):
+            out[4 * c : 4 * c + 4] = load[c, 0:4]
+            out[21 + 2 * c : 23 + 2 * c] = disp[c, 0:2]
+        out[12:16] = (1 - mask[0:4]).astype(F32)
+        out[16:21] = dens[0:5]
+
     even = lax.rem(lax.axis_index("y"), 2) == 0
 
     @pl.when(even)
     def _():
-        first[0:LOW_X] = low[...]
-        second[0:UP_X] = up[...]
+        put_low(first)
+        put_up(second)
 
     @pl.when(jnp.logical_not(even))
     def _():
-        first[0:UP_X] = up[...]
-        second[0:LOW_X] = low[...]
-
-
-def loads_kernel(nodes, forces, _, out):
+        put_up(first)
+        put_low(second)
+
+
+def loads_kernel(nodes, forces, out):
     first_x = (lax.axis_index("x") * lax.axis_size("y") + lax.axis_index("y")) * RX - 3
     first_y = (lax.axis_index("z") * lax.axis_size("c") + lax.axis_index("c")) * RY
     count = (NI - 1) * RY
@@ -148,7 +155,7 @@
             out[c, :, t] = summed[:, t * NZ : t * NZ + NZ].reshape(NI - 1, RY, NZ)
 
 
-def pack_second_kernel(load, disp, dens, mask, first, second, out, low, up):
+def pack_second_kernel(load, disp, dens, mask, first, second, _, out, low, up):
     even = lax.rem(lax.axis_index("y"), 2) == 0
 
     @pl.when(even)
@@ -275,6 +282,14 @@
     return result
 
 
+def filtered(cells, beside, p, lane):
+    side = cells[p - 1] + cells[p + 1]
+    far = beside[p - 1] + beside[p + 1]
+    deep = 0.5 * cells[p] + EDGE * (beside[p] + side)
+    deep = up_z(deep, lane) + down_z(deep, lane)
+    return 1.5 * cells[p] + 0.5 * (beside[p] + side) + EDGE * far + deep
+
+
 KEYS = [("s", d, e) for d, e in PAIRS] + [("n", d) for d in range(3)]
 KEYS += [("b", d, e) for d, e, f in BENDS] + [("b", f, e) for d, e, f in BENDS]
 KEYS += [("t", d) for d in range(3)] + [("l", d) for d in range(3)]
@@ -282,7 +297,25 @@
 PARTS = [(c, s) for c in range(3) for s in (0, 1)]
 
 
-def main_kernel(load, disp, dens, mask, low, up, placed, first, second, basis, senses, sums, L0, L1, FR1, D1, DN, MOD, SC, HP, W, Z, G, DS, SS, F, DV):
+def store_parts(parts, c, i, t, v, lane):
+    above = up_z(v, lane)
+    for s, part in ((0, v + above), (1, above - v)):
+        parts[2 * c + s, i, 8 * t : 8 * t + 8] = part
+        if t == 0:
+            parts[2 * c + s, i, 16:24] = part
+
+
+def yz_modes(parts, i, t):
+    result = {}
+    for c, s in PARTS:
+        part = parts[2 * c + s, i, 8 * t : 8 * t + 8]
+        higher = parts[2 * c + s, i, 8 * t + 1 : 8 * t + 9]
+        result[c, 0, s] = part + higher
+        result[c, 1, s] = higher - part
+    return result
+
+
+def main_kernel(load, disp, dens, mask, low, up, placed, first, second, Z, SC, D1, sums, G, L0, L1, FR1, DN, MOD, HP, W, DS, SS):
     gx = lax.axis_index("x") * lax.axis_size("y") + lax.axis_index("y")
     gy = lax.axis_index("z") * lax.axis_size("c") + lax.axis_index("c")
     extent_x = RX * lax.axis_size("x") * lax.axis_size("y")
@@ -363,13 +396,6 @@
             return mask[i - 4] == 0
         return up[12 + i - 4 - RX] > 0.5
 
-    def disp_of(c, p, t):
-        if t == 1:
-            return D1[c, p]
-        if p == 0:
-            return low[17 + c]
-        return disp[c, p - 1] if p <= RX else up[21 + 2 * c + p - 1 - RX]
-
     near_z = 2.0 - jnp.where(lane == 0, 1.0, 0.0) - jnp.where(lane == NZ - 1, 1.0, 0.0)
     inside_y, part_a, part_b = [], [], []
     for t in range(2):
@@ -378,13 +404,6 @@
         near_y = 2.0 - jnp.where(place_y == 0, 1.0, 0.0) - jnp.where(place_y == extent_y - 1, 1.0, 0.0)
         part_a.append(1.5 + 0.5 * (near_y + near_z) + EDGE * near_y * near_z)
         part_b.append(0.5 + EDGE * (near_y + near_z))
-
-    def filtered(cells, beside, p):
-        side = cells[p - 1] + cells[p + 1]
-        far = beside[p - 1] + beside[p + 1]
-        deep = 0.5 * cells[p] + EDGE * (beside[p] + side)
-        deep = up_z(deep, lane) + down_z(deep, lane)
-        return 1.5 * cells[p] + 0.5 * (beside[p] + side) + EDGE * far + deep
 
     def density_rows(p, t, shift):
         if t == 0:
@@ -405,7 +424,7 @@
             inside_x = jnp.where((place_x >= 0) & (place_x < extent_x), 1.0, 0.0)
             near_x = 2.0 - jnp.where(place_x == 0, 1.0, 0.0) - jnp.where(place_x == extent_x - 1, 1.0, 0.0)
             inverse = 1.0 / (part_a[t] + near_x * part_b[t])
-            physical = filtered(cells, beside, p - 1) * inverse
+            physical = filtered(cells, beside, p - 1, lane) * inverse
             squared = physical * physical
             inside = inside_y[t] * inside_x
             mod = inside * (SOFT + (1.0 - SOFT) * (squared * physical))
@@ -418,13 +437,6 @@
                 HP[i, 0:8] = deep
 
     zero = jnp.zeros((8, NZ), F32)
-
-    def store_parts(c, i, t, v):
-        above = up_z(v, lane)
-        for s, part in ((0, v + above), (1, above - v)):
-            G[2 * c + s, i, 8 * t : 8 * t + 8] = part
-            if t == 0:
-                G[2 * c + s, i, 16:24] = part
 
     def in_block(i, t):
         return t == 0 and 4 <= i < 4 + RX
@@ -441,39 +453,20 @@
                     here = load_of(c, i, t)
                     z = inverse * here
                     Z[0, c, i, t] = z
-                    store_parts(c, i, t, z)
+                    store_parts(G, c, i, t, z, lane)
                     if in_block(i, t):
                         L0[c, i - 4] = here
                         bz = bz + z * here
             before = summed
 
-    def yz_modes(i, t):
-        result = {}
-        for c, s in PARTS:
-            part = G[2 * c + s, i, 8 * t : 8 * t + 8]
-            higher = G[2 * c + s, i, 8 * t + 1 : 8 * t + 9]
-            result[c, 0, s] = part + higher
-            result[c, 1, s] = higher - part
-        return result
-
     def apply(k):
         for t in range(2):
-            near = yz_modes(1 + k, t)
+            near = yz_modes(G, 1 + k, t)
             passed = None
             for i in range(1 + k, NI - 1 - k):
-                far = yz_modes(i + 1, t)
+                far = yz_modes(G, i + 1, t)
                 modes = modes_of(near, far)
                 mixed = combine(modes)
-                if 3 <= i <= NI - 4:
-                    energy = None
-                    for key, n in NUMBER.items():
-                        factor = mixed[key] if key[0] == "s" else modes[mode_of(key)]
-                        term = factor * F[n, i - 3, t]
-                        energy = term if energy is None else energy + term
-                    value = energy * SC[i - 3, t]
-                    DV[k, i - 3, 8 + 8 * t : 16 + 8 * t] = value
-                    if t == 1:
-                        DV[k, i - 3, 0:8] = value
                 young = MOD[i, t]
                 scaled = {kind: young * factor for kind, factor in SCALES.items()}
                 forces = {}
@@ -508,29 +501,6 @@
         ]
         return level - slope + down_z(level + slope, lane)
 
-    for p in range(RX + 3):
-        for t in range(2):
-            for c in range(3):
-                v = disp_of(c, p, t)
-                above = up_z(v, lane)
-                for s, part in ((0, v + above), (1, above - v)):
-                    SS[2 * c + s, p, 8 * t : 8 * t + 8] = part
-                    if t == 0:
-                        SS[2 * c + s, p, 16:24] = part
-    for t in range(2):
-        near = None
-        for p in range(RX + 3):
-            far = {}
-            for c, s in PARTS:
-                part = SS[2 * c + s, p, 8 * t : 8 * t + 8]
-                higher = SS[2 * c + s, p, 8 * t + 1 : 8 * t + 9]
-                far[c, 0, s] = part + higher
-                far[c, 1, s] = higher - part
-            if near is not None:
-                for key, value in combine(modes_of(near, far)).items():
-                    F[NUMBER[key], p - 1, t] = value * SCALES[key[0]]
-            near = far
-
     def add(total, i, t, one, two):
         return total + one * two if in_block(i, t) else total
 
@@ -543,7 +513,7 @@
                 z = Z[0, c, i, t]
                 y = W[i, t] * q - z
                 Z[1, c, i, t] = y
-                store_parts(c, i, t, y)
+                store_parts(G, c, i, t, y, lane)
                 h00 = add(h00, i, t, z, q)
                 h01 = add(h01, i, t, y, q)
                 if in_block(i, t):
@@ -556,7 +526,7 @@
                 z = Z[1, c, i, t]
                 y = W[i, t] * q - z
                 Z[2, c, i, t] = y
-                store_parts(c, i, t, y)
+                store_parts(G, c, i, t, y, lane)
                 h11 = add(h11, i, t, z, q)
                 h12 = add(h12, i, t, y, q)
                 if in_block(i, t):
@@ -577,15 +547,55 @@
     for n in range(sums.shape[0]):
         sums[n] = line
 
+
+def sense_kernel(disp, low, up, D1, Z, SC, senses, U, F, DV):
+    lane = lax.broadcasted_iota(jnp.int32, (8, NZ), 1)
+
+    def disp_of(c, p, t):
+        if t == 1:
+            return D1[c, p]
+        if p == 0:
+            return low[17 + c]
+        return disp[c, p - 1] if p <= RX else up[21 + 2 * c + p - 1 - RX]
+
+    for p in range(RX + 3):
+        for t in range(2):
+            for c in range(3):
+                store_parts(U.at[3], c, p, t, disp_of(c, p, t), lane)
+                for k in range(3):
+                    store_parts(U.at[k], c, p, t, Z[k, c, p + 3, t], lane)
+    for t in range(2):
+        near = yz_modes(U.at[3], 0, t)
+        for p in range(RX + 2):
+            far = yz_modes(U.at[3], p + 1, t)
+            for key, value in combine(modes_of(near, far)).items():
+                F[NUMBER[key], p, t] = value * SCALES[key[0]]
+            near = far
+
     for k in range(3):
+        for t in range(2):
+            near = yz_modes(U.at[k], 0, t)
+            for p in range(RX + 2):
+                far = yz_modes(U.at[k], p + 1, t)
+                modes = modes_of(near, far)
+                energy = None
+                for key, n in NUMBER.items():
+                    factor = modes[mode_of(key)]
+                    if key[0] == "s":
+                        factor = factor + modes[axes(key[1]) + (key[2],)]
+                    term = factor * F[n, p, t]
+                    energy = term if energy is None else energy + term
+                value = energy * SC[p, t]
+                DV[k, p, 8 + 8 * t : 16 + 8 * t] = value
+                if t == 1:
+                    DV[k, p, 0:8] = value
+                near = far
         cells, beside = [], []
         for p in range(RX + 2):
             cells.append(DV[k, p, 8:16])
             beside.append(DV[k, p, 7:15] + DV[k, p, 9:17])
             if p >= 2:
-                senses[k, p - 2] = filtered(cells, beside, p - 1)
-        for c in range(3):
-            basis[k, c] = Z[k, c, 4 : 4 + RX, 0]
+                senses[k, p - 2] = filtered(cells, beside, p - 1, lane)
 
 
 def final_kernel(gathered, basis, senses, adjoint, sensitivity):
@@ -606,14 +616,17 @@
     c2 = jnp.where(d2 > 0.0, t2 / d2, 0.0)
     c1 = jnp.where(fine1, t1 / d1, 0.0) - l3 * c2
     c0 = b0 / h00 - l1 * c1 - l2 * c2
-    adjoint[...] = c0 * basis[0] + c1 * basis[1] + c2 * basis[2]
+    own = slice(4, 4 + RX)
+    for c in range(3):
+        one, two, three = [basis[k, c, own, 0] for k in range(3)]
+        adjoint[c] = c0 * one + c1 * two + c2 * three
     sensitivity[...] = c0 * senses[0] + c1 * senses[1] + c2 * senses[2]
 
 
 VMEM = pl.BlockSpec(memory_space=pltpu.VMEM)
 
 
-def call(kernel, inputs, outs, scratch=(), limit=None, extra=0):
+def call(kernel, inputs, outs, scratch=(), limit=None, extra=0, cost=None):
     single = not isinstance(outs, list)
     shapes = [outs] if single else outs
     result = pl.pallas_call(
@@ -622,25 +635,26 @@
         in_specs=[VMEM] * (len(inputs) - extra) + [pl.BlockSpec(memory_space=pl.ANY)] * extra,
         out_specs=[VMEM] * len(shapes),
         scratch_shapes=[pltpu.VMEM(s, F32) for s in scratch],
+        cost_estimate=cost and pl.CostEstimate(flops=0, bytes_accessed=cost, transcendentals=0),
         compiler_params=pltpu.CompilerParams(vmem_limit_bytes=limit or 32 * 1024 * 1024),
     )(*inputs)
     return result[0] if single else result
 
 
 MAIN_SCRATCH = [
+    (6, NI, 24, NZ),
     (3, RX, 8, NZ),
     (3, NI - 1, 8, NZ),
     (NI - 1, 8, NZ),
-    (3, RX + 3, 8, NZ),
     (NI + 2, 40, NZ),
     (NI, 2, 8, NZ),
-    (RX + 2, 2, 8, NZ),
     (NI, 24, NZ),
     (NI, 2, 8, NZ),
-    (3, 3, NI, 2, 8, NZ),
-    (6, NI, 24, NZ),
     (6, NI, 2, 8, NZ),
     (6, NI, 24, NZ),
+]
+SENSE_SCRATCH = [
+    (4, 6, RX + 3, 24, NZ),
     (len(KEYS), RX + 2, 2, 8, NZ),
     (3, RX + 2, 24, NZ),
 ]
@@ -654,41 +668,49 @@
 def shards(displacement, adjoint_load, density, fixed_mask, load_nodes, load_forces):
     count_x = lax.axis_size("x") * lax.axis_size("y")
     count_y = lax.axis_size("z") * lax.axis_size("c")
-    own = (adjoint_load, displacement, density, fixed_mask)
-    first, second = pl.pallas_call(
+    given = (adjoint_load, displacement, density, fixed_mask, load_nodes, load_forces)
+    first, second, *given = pl.pallas_call(
         pack_x_kernel,
-        out_shape=[pltpu.VMEM((UP_X, RY, NZ), F32), pltpu.VMEM((UP_X + 1, RY, NZ), F32)],
-        in_specs=[pl.BlockSpec(memory_space=pltpu.HBM)] * 4,
-        out_specs=[VMEM] * 2,
-        scratch_shapes=[
-            pltpu.VMEM((LOW_X, RY, NZ), F32),
-            pltpu.VMEM((UP_X, RY, NZ), F32),
-            pltpu.VMEM((7, RY, NZ), jnp.int32),
-            pltpu.SemaphoreType.DMA((16,)),
-        ],
-    )(*own)
+        out_shape=[pltpu.VMEM((UP_X, RY, NZ), F32), pltpu.VMEM((UP_X + 1, RY, NZ), F32)]
+        + [pltpu.VMEM(value.shape, value.dtype) for value in given],
+        in_specs=[pl.BlockSpec(memory_space=pltpu.HBM)] * 6,
+        out_specs=[VMEM] * 8,
+        scratch_shapes=[pltpu.SemaphoreType.DMA((6,))],
+    )(*given)
+    own, loads = tuple(given[:4]), tuple(given[4:])
     second = lax.ppermute(second, ("x", "y"), swaps(1, count_x))
     first = lax.ppermute(first, ("x", "y"), swaps(0, count_x))
+    placed = call(loads_kernel, loads, (3, NI - 1, 2, RY, NZ))
     sizes = (NEAR + CORNER, 4, NZ)
     second, low, up = call(
         pack_second_kernel,
-        own + (first, second),
+        own + (first, second, placed),
         [(NEAR + CORNER + 1, 4, NZ), (LOW_X, RY, NZ), (UP_X, RY, NZ)],
+        extra=1,
     )
-    placed = call(
-        loads_kernel, (load_nodes, load_forces, low), (3, NI - 1, 2, RY, NZ), extra=1
-    )
-    first = call(functools.partial(pack_y_kernel, 0), own + (low, up, placed), sizes, extra=1)
+    first = call(functools.partial(pack_y_kernel, 0), own + (low, up, second), sizes, extra=1)
     second = lax.ppermute(second, ("z", "c"), swaps(1, count_y))
     first = lax.ppermute(first, "c", swaps(0, 2))
     close = lax.axis_size("c") * count_x
     far = lax.axis_size("z")
-    basis, senses, sums = call(
+    basis, scale, outer, sums = call(
         main_kernel,
         own + (low, up, placed, first, second),
-        [(3, 3, RX, RY, NZ), (3, RX, RY, NZ), (close, 1, NZ)],
+        [
+            (3, 3, NI, 2, 8, NZ),
+            (RX + 2, 2, 8, NZ),
+            (3, RX + 3, 8, NZ),
+            (close, 1, NZ),
+        ],
         MAIN_SCRATCH,
         48 * 1024 * 1024,
+    )
+    senses = call(
+        sense_kernel,
+        (own[1], low, up, outer, basis, scale),
+        (3, RX, RY, NZ),
+        SENSE_SCRATCH,
+        cost=6_000_000,
     )
     sums = lax.all_to_all(sums, ("x", "y", "c"), 0, 0, tiled=True)
     sums = jnp.broadcast_to(jnp.sum(sums, axis=0, keepdims=True), (far, 1, NZ))

time: 68.1 us -> 67.6 us (level)
  blocking collectives: 39.4 us -> 13.4 us
  starting transfers between devices: 14.6 us -> 30.9 us
  waiting for transfers between devices: 3.45 us -> 11.4 us
  Pallas kernels: 9.41 us -> 10.2 us
    all_to_all x1 -> x0, blocking collectives: 26 us -> none  [shards(): sums = lax.all_to_all(sums, 'z', 0, 0, tiled=True)]
    all_to_all x0 -> x1, starting transfers between devices: none -> 16.2 us  [shards(): sums = lax.all_to_all(sums, 'z', 0, 0, tiled=True)]
    all_to_all x0 -> x1, waiting for transfers between devices: none -> 9.29 us  [shards(): sums = lax.all_to_all(sums, 'z', 0, 0, tiled=True)]
    ppermute x1, waiting for transfers between devices: 2.12 us -> 0.29 us  [shards(): first = lax.ppermute(first, ('x', 'y'), swaps(0, count_x))]
    pallas_call x5 -> x6, Pallas kernels: 8.32 us -> 9.12 us  [call(): pl.pallas_call(kernel, out_shape=[jax.ShapeDtypeStruct(s, F32) for s in s...]
  transfers between devices with their start and end apart: 4 -> 5, of which waited for: 2 -> 4; matrix products, arithmetic and copies ran while one was open for 0% -> 0% of each run, Pallas kernels for 3% -> 6%
where the time goes in v6:
time: 67.6 us; the launch traced here: 67.3 us
  starting transfers between devices  30.9 us (46%)
  blocking collectives  13.4 us (20%)
  waiting for transfers between devices  11.4 us (17%)
  Pallas kernels  10.2 us (15%)
  between operations  0.72 us (1%)
    all_to_all x1, starting transfers between devices, shards(): sums = lax.all_to_all(sums, 'z', 0, 0, tiled=True)  16.2 us
    all_to_all x1, blocking collectives, shards(): sums = lax.all_to_all(sums, ('x', 'y', 'c'), 0, 0, tiled=True)  13.4 us
    all_to_all x1, waiting for transfers between devices, shards(): sums = lax.all_to_all(sums, 'z', 0, 0, tiled=True)  9.29 us
    pallas_call x6, Pallas kernels, call(): pl.pallas_call(kernel, out_shape=[jax.ShapeDtypeStruct(s, F32) for s in s...  9.12 us
    ppermute x1, starting transfers between devices, shards(): first = lax.ppermute(first, ('x', 'y'), swaps(0, count_x))  6.57 us
    ppermute x1, starting transfers between devices, shards(): second = lax.ppermute(second, ('z', 'c'), swaps(1, count_y))  5.31 us
    ppermute x1, starting transfers between devices, shards(): first = lax.ppermute(first, 'c', swaps(0, 2))  2.1 us
  transfers between devices with their start and end apart: 5, of which 4 were waited for; matrix products, arithmetic and copies ran while one was open for 0% of the time, Pallas kernels for 6%

profile of v6, /device:TPU:1, one launch (start us, length us, event | category | flops | bytes accessed | tf_op | source)
XLA Modules:
  0.0 67.3 jit_solution(11274250576831860137)
XLA Ops:
  0.6 1.1 %shard_map.77 = (f32[27,8,128]{2,1,0:T(8,128)S(1)}, f32[28,8,128]{2,1,0:T(8,128)S(1)}, f32[3,12,8,128]{3,2,1,0:T(8,128)S(1)}, f32[3,12,8,128]{3,2,1,0:T(8,128)S(...) custom-call(f32[3,12,8,128]{3,2,1,0:T(8,128)} %refs_0_.1, ...), custom_call_target="tpu_custom_call" | custom-call | tf_op jit(solution)/shard_map/pallas_call | solution.py:672
  1.7 0.7 collective-permute-start.1
  2.4 6.6 %collective-permute-start = (f32[27,8,128]{2,1,0:T(8,128)S(1)}, f32[27,8,128]{2,1,0:T(8,128)S(1)}, u32[]{:S(2)}, u32[]{:S(2)}) collective-permute-start(f32[27,8,128]{2,1,0:T(8,128)S(1)} %get-tuple-element.21), channel_id=1, source_target_pairs={{0,32},{64,96},{128,160},{192,224},{256,288},{320,352},{384,416},{... | collective-permute-start | bytes 331784 | tf_op jit(solution)/shard_map/ppermute | solution.py:682
  9.0 1.8 %shard_map.78._.placed = f32[3,19,2,8,128]{4,3,2,1,0:T(8,128)S(1)} custom-call(s32[3,2048]{1,0:T(4,128)S(1)} %get-tuple-element.23.nodes, f32[3,2048]{1,0:T(4,128)S(1)} %get-tuple-element.24.forces), custom_call_target="tpu_custom_call" | custom-call | tf_op jit(solution)/shard_map/pallas_call | solution.py:632
  10.8 0.3 collective-permute-done.first
  11.1 0.0 collective-permute-done.1.second
  11.1 0.1 shard_map.79
  11.2 5.3 %collective-permute-start.3 = (f32[128,4,128]{2,1,0:T(4,128)S(1)}, f32[128,4,128]{2,1,0:T(4,128)S(1)}, u32[]{:S(2)}, u32[]{:S(2)}) collective-permute-start(f32[128,4,128]{2,1,0:T(4,128)S(1)} %get-tuple-element.27.rest_0_), channel_id=1, source_target_pairs={{1,2},{3,4},{5,6},{7,8},{9,10},{11,12},{13,14},{15,16},{17,18},{19... | collective-permute-start | bytes 786440 | tf_op jit(solution)/shard_map/ppermute | solution.py:692
  16.5 0.1 shard_map.80
  16.6 2.1 %collective-permute-start.2 = (f32[127,4,128]{2,1,0:T(4,128)S(1)}, f32[127,4,128]{2,1,0:T(4,128)S(1)}, u32[]{:S(2)}, u32[]{:S(2)}) collective-permute-start(f32[127,4,128]{2,1,0:T(4,128)S(1)} %shard_map.80), channel_id=1, source_target_pairs={{0,1},{1,0},{2,3},{3,2},{4,5},{5,4},{6,7},{7,6},{8,9},{9,8},{10,11... | collective-permute-start | bytes 780296 | tf_op jit(solution)/shard_map/ppermute | solution.py:693
  18.7 1.3 %collective-permute-done.2.first = f32[127,4,128]{2,1,0:T(4,128)S(1)} collective-permute-done((f32[127,4,128]{2,1,0:T(4,128)S(1)}, f32[127,4,128]{2,1,0:T(4,128)S(1)}, u32[]{:S(2)}, u32[]{:S(2)}) %collective-permute-start.2) | collective-permute-done | bytes 260128 | tf_op jit(solution)/shard_map/ppermute | solution.py:693
  20.0 0.5 collective-permute-done.3.second
  20.5 4.4 %shard_map.81 = (f32[3,3,20,2,8,128]{5,4,3,2,1,0:T(8,128)S(1)}, f32[14,2,8,128]{3,2,1,0:T(8,128)S(1)}, f32[3,15,8,128]{3,2,1,0:T(8,128)S(1)}, f32[32,1,128]{2,1,0:T(1,128)S(1)}) custom-call(f32[3,12,8,128]{3,2,1,0:T(8,128)S(1)} %get-tuple-element.17.load, f32[3,12,8,128]{3,2,1,0:T(8,128)S(1)} %get-tuple-element.18.disp, ...), custom_call_target="tpu_custom_call" | custom-call | tf_op jit(solution)/shard_map/pallas_call | solution.py:632
  24.9 13.4 %all_to_all.10 = f32[32,1,128]{2,1,0:T(1,128)S(1)} all-to-all(f32[32,1,128]{2,1,0:T(1,128)S(1)} %get-tuple-element.28), channel_id=1, replica_groups=mesh['x'=4,'y'=4,'z'=16,'c'=2] {'x','y','c'}, dimensions={0} | all-to-all | bytes 32768 | tf_op jit(solution)/shard_map/all_to_all | solution.py:715
  38.4 0.1 reduce_sum.9
  38.4 0.6 broadcast_in_dim.2
  39.0 16.2 %all-to-all-start.1 = ((f32[16,1,128]{2,1,0:T(1,128)}), f32[16,1,128]{2,1,0:T(1,128)S(1)}, u32[]{:S(2)}, u32[]{:S(2)}) async-start(f32[16,1,128]{2,1,0:T(1,128)} %broadcast_in_dim.2), calls=%async_computation.1 | async-start | bytes 16384 | tf_op jit(solution)/shard_map/all_to_all | solution.py:717
  55.2 1.9 %shard_map.82.senses = f32[3,12,8,128]{3,2,1,0:T(8,128)S(1)} custom-call(f32[3,12,8,128]{3,2,1,0:T(8,128)S(1)} %get-tuple-element.18.disp, f32[20,8,128]{2,1,0:T(8,128)S(1)} %get-tuple-element.25.low, f32[27,8,128]{2,1,0:T(8,128)S(1)} %get-tuple-element.26.up, f32[3,15,8,128]{3,2,1,0:T(8,128)S(1)} %get-tuple-element.30.D1, ...), custom_call_target="tpu_custom_call" | custom-call | bytes 6000000 | tf_op jit(solution)/shard_map/pallas_call | solution.py:632
  57.2 9.3 %all-to-all-done.1.gathered = f32[16,1,128]{2,1,0:T(1,128)S(1)} async-done(((f32[16,1,128]{2,1,0:T(1,128)}), f32[16,1,128]{2,1,0:T(1,128)S(1)}, u32[]{:S(2)}, u32[]{:S(2)}) %all-to-all-start.1) | async-done | bytes 8224 | tf_op jit(solution)/shard_map/all_to_all | solution.py:717
  66.5 0.8 %shard_map.83 = (f32[3,12,8,128]{3,2,1,0:T(8,128)}, f32[12,8,128]{2,1,0:T(8,128)}) custom-call(f32[16,1,128]{2,1,0:T(1,128)S(1)} %all-to-all-done.1.gathered, f32[3,3,20,2,8,128]{5,4,3,2,1,0:T(8,128)S(1)} %get-tuple-element.29.Z.basis, f32[3,12,8,128]{3,2,1,0:T(8,128)S(1)} %shard_map.82.senses), custom_call_target="tpu_custom_call" | custom-call | tf_op jit(solution)/shard_map/pallas_call | solution.py:632
Async XLA Ops:
  1.7 9.4 %collective-permute-start.1 = (f32[28,8,128]{2,1,0:T(8,128)S(1)}, f32[28,8,128]{2,1,0:T(8,128)S(1)}, u32[]{:S(2)}, u32[]{:S(2)}) collective-permute-start(f32[28,8,128]{2,1,0:T(8,128)S(1)} %get-tuple-element.22), channel_id=1, source_target_pairs={{32,64},{96,128},{160,192},{224,256},{288,320},{352,384},{416,448}... | collective-permute-start | bytes 344072 | tf_op jit(solution)/shard_map/ppermute | solution.py:681
  2.4 8.7 %collective-permute-start = (f32[27,8,128]{2,1,0:T(8,128)S(1)}, f32[27,8,128]{2,1,0:T(8,128)S(1)}, u32[]{:S(2)}, u32[]{:S(2)}) collective-permute-start(f32[27,8,128]{2,1,0:T(8,128)S(1)} %get-tuple-element.21), channel_id=1, source_target_pairs={{0,32},{64,96},{128,160},{192,224},{256,288},{320,352},{384,416},{... | collective-permute-start | bytes 331784 | tf_op jit(solution)/shard_map/ppermute | solution.py:682
  11.2 9.4 %collective-permute-start.3 = (f32[128,4,128]{2,1,0:T(4,128)S(1)}, f32[128,4,128]{2,1,0:T(4,128)S(1)}, u32[]{:S(2)}, u32[]{:S(2)}) collective-permute-start(f32[128,4,128]{2,1,0:T(4,128)S(1)} %get-tuple-element.27.rest_0_), channel_id=1, source_target_pairs={{1,2},{3,4},{5,6},{7,8},{9,10},{11,12},{13,14},{15,16},{17,18},{19... | collective-permute-start | bytes 786440 | tf_op jit(solution)/shard_map/ppermute | solution.py:692
  16.6 3.4 %collective-permute-start.2 = (f32[127,4,128]{2,1,0:T(4,128)S(1)}, f32[127,4,128]{2,1,0:T(4,128)S(1)}, u32[]{:S(2)}, u32[]{:S(2)}) collective-permute-start(f32[127,4,128]{2,1,0:T(4,128)S(1)} %shard_map.80), channel_id=1, source_target_pairs={{0,1},{1,0},{2,3},{3,2},{4,5},{5,4},{6,7},{7,6},{8,9},{9,8},{10,11... | collective-permute-start | bytes 780296 | tf_op jit(solution)/shard_map/ppermute | solution.py:693
  39.0 27.5 %all-to-all-start.1 = ((f32[16,1,128]{2,1,0:T(1,128)}), f32[16,1,128]{2,1,0:T(1,128)S(1)}, u32[]{:S(2)}, u32[]{:S(2)}) async-start(f32[16,1,128]{2,1,0:T(1,128)} %broadcast_in_dim.2), calls=%async_computation.1 | async-start | bytes 16384 | tf_op jit(solution)/shard_map/all_to_all | solution.py:717

commit v7 on v6

--- a/solution.py
+++ b/solution.py
@@ -137,9 +137,9 @@
             for _ in range(3):
                 head = rest.astype(jnp.bfloat16).astype(F32)
                 rest = rest - head
-                parts.append(jnp.where(hit, head, 0.0).astype(jnp.bfloat16))
+                parts.append(jnp.where(hit, head, 0.0))
         total = total + lax.dot_general(
-            jnp.concatenate(parts, axis=0),
+            jnp.concatenate(parts, axis=0).astype(jnp.bfloat16),
             layer,
             (((1,), (1,)), ((), ())),
             preferred_element_type=F32,

time: 67.6 us -> 67.6 us (level)
  no operation moved by 1% of the time
where the time goes in v7:
time: 67.6 us; the launch traced here: 67.3 us
  starting transfers between devices  30.9 us (46%)
  blocking collectives  13.4 us (20%)
  waiting for transfers between devices  11.5 us (17%)
  Pallas kernels  10.1 us (15%)
  between operations  0.72 us (1%)
    all_to_all x1, starting transfers between devices, shards(): sums = lax.all_to_all(sums, 'z', 0, 0, tiled=True)  16.2 us
    all_to_all x1, blocking collectives, shards(): sums = lax.all_to_all(sums, ('x', 'y', 'c'), 0, 0, tiled=True)  13.4 us
    all_to_all x1, waiting for transfers between devices, shards(): sums = lax.all_to_all(sums, 'z', 0, 0, tiled=True)  9.29 us
    pallas_call x6, Pallas kernels, call(): pl.pallas_call(kernel, out_shape=[jax.ShapeDtypeStruct(s, F32) for s in s...  9.02 us
    ppermute x1, starting transfers between devices, shards(): first = lax.ppermute(first, ('x', 'y'), swaps(0, count_x))  6.57 us
    ppermute x1, starting transfers between devices, shards(): second = lax.ppermute(second, ('z', 'c'), swaps(1, count_y))  5.31 us
    ppermute x1, starting transfers between devices, shards(): first = lax.ppermute(first, 'c', swaps(0, 2))  2.1 us
  transfers between devices with their start and end apart: 5, of which 4 were waited for; matrix products, arithmetic and copies ran while one was open for 0% of the time, Pallas kernels for 6%

profile of v7, /device:TPU:1, one launch (start us, length us, event | category | flops | bytes accessed | tf_op | source)
XLA Modules:
  0.0 67.3 jit_solution(5228116256030672055)
XLA Ops:
  0.6 1.1 %shard_map.77 = (f32[27,8,128]{2,1,0:T(8,128)S(1)}, f32[28,8,128]{2,1,0:T(8,128)S(1)}, f32[3,12,8,128]{3,2,1,0:T(8,128)S(1)}, f32[3,12,8,128]{3,2,1,0:T(8,128)S(...) custom-call(f32[3,12,8,128]{3,2,1,0:T(8,128)} %refs_0_.1, ...), custom_call_target="tpu_custom_call" | custom-call | tf_op jit(solution)/shard_map/pallas_call | solution.py:672
  1.7 0.7 collective-permute-start.1
  2.4 6.6 %collective-permute-start = (f32[27,8,128]{2,1,0:T(8,128)S(1)}, f32[27,8,128]{2,1,0:T(8,128)S(1)}, u32[]{:S(2)}, u32[]{:S(2)}) collective-permute-start(f32[27,8,128]{2,1,0:T(8,128)S(1)} %get-tuple-element.21), channel_id=1, source_target_pairs={{0,32},{64,96},{128,160},{192,224},{256,288},{320,352},{384,416},{... | collective-permute-start | bytes 331784 | tf_op jit(solution)/shard_map/ppermute | solution.py:682
  9.0 1.7 %shard_map.78._.placed = f32[3,19,2,8,128]{4,3,2,1,0:T(8,128)S(1)} custom-call(s32[3,2048]{1,0:T(4,128)S(1)} %get-tuple-element.23.nodes, f32[3,2048]{1,0:T(4,128)S(1)} %get-tuple-element.24.forces), custom_call_target="tpu_custom_call" | custom-call | tf_op jit(solution)/shard_map/pallas_call | solution.py:632
  10.7 0.4 collective-permute-done.first
  11.1 0.0 collective-permute-done.1.second
  11.1 0.1 shard_map.79
  11.2 5.3 %collective-permute-start.3 = (f32[128,4,128]{2,1,0:T(4,128)S(1)}, f32[128,4,128]{2,1,0:T(4,128)S(1)}, u32[]{:S(2)}, u32[]{:S(2)}) collective-permute-start(f32[128,4,128]{2,1,0:T(4,128)S(1)} %get-tuple-element.27.rest_0_), channel_id=1, source_target_pairs={{1,2},{3,4},{5,6},{7,8},{9,10},{11,12},{13,14},{15,16},{17,18},{19... | collective-permute-start | bytes 786440 | tf_op jit(solution)/shard_map/ppermute | solution.py:692
  16.5 0.1 shard_map.80
  16.6 2.1 %collective-permute-start.2 = (f32[127,4,128]{2,1,0:T(4,128)S(1)}, f32[127,4,128]{2,1,0:T(4,128)S(1)}, u32[]{:S(2)}, u32[]{:S(2)}) collective-permute-start(f32[127,4,128]{2,1,0:T(4,128)S(1)} %shard_map.80), channel_id=1, source_target_pairs={{0,1},{1,0},{2,3},{3,2},{4,5},{5,4},{6,7},{7,6},{8,9},{9,8},{10,11... | collective-permute-start | bytes 780296 | tf_op jit(solution)/shard_map/ppermute | solution.py:693
  18.7 1.3 %collective-permute-done.2.first = f32[127,4,128]{2,1,0:T(4,128)S(1)} collective-permute-done((f32[127,4,128]{2,1,0:T(4,128)S(1)}, f32[127,4,128]{2,1,0:T(4,128)S(1)}, u32[]{:S(2)}, u32[]{:S(2)}) %collective-permute-start.2) | collective-permute-done | bytes 260128 | tf_op jit(solution)/shard_map/ppermute | solution.py:693
  20.0 0.5 collective-permute-done.3.second
  20.5 4.4 %shard_map.81 = (f32[3,3,20,2,8,128]{5,4,3,2,1,0:T(8,128)S(1)}, f32[14,2,8,128]{3,2,1,0:T(8,128)S(1)}, f32[3,15,8,128]{3,2,1,0:T(8,128)S(1)}, f32[32,1,128]{2,1,0:T(1,128)S(1)}) custom-call(f32[3,12,8,128]{3,2,1,0:T(8,128)S(1)} %get-tuple-element.17.load, f32[3,12,8,128]{3,2,1,0:T(8,128)S(1)} %get-tuple-element.18.disp, ...), custom_call_target="tpu_custom_call" | custom-call | tf_op jit(solution)/shard_map/pallas_call | solution.py:632
  24.9 13.4 %all_to_all.10 = f32[32,1,128]{2,1,0:T(1,128)S(1)} all-to-all(f32[32,1,128]{2,1,0:T(1,128)S(1)} %get-tuple-element.28), channel_id=1, replica_groups=mesh['x'=4,'y'=4,'z'=16,'c'=2] {'x','y','c'}, dimensions={0} | all-to-all | bytes 32768 | tf_op jit(solution)/shard_map/all_to_all | solution.py:715
  38.4 0.1 reduce_sum.9
  38.4 0.6 broadcast_in_dim.2
  39.0 16.2 %all-to-all-start.1 = ((f32[16,1,128]{2,1,0:T(1,128)}), f32[16,1,128]{2,1,0:T(1,128)S(1)}, u32[]{:S(2)}, u32[]{:S(2)}) async-start(f32[16,1,128]{2,1,0:T(1,128)} %broadcast_in_dim.2), calls=%async_computation.1 | async-start | bytes 16384 | tf_op jit(solution)/shard_map/all_to_all | solution.py:717
  55.2 1.9 %shard_map.82.senses = f32[3,12,8,128]{3,2,1,0:T(8,128)S(1)} custom-call(f32[3,12,8,128]{3,2,1,0:T(8,128)S(1)} %get-tuple-element.18.disp, f32[20,8,128]{2,1,0:T(8,128)S(1)} %get-tuple-element.25.low, f32[27,8,128]{2,1,0:T(8,128)S(1)} %get-tuple-element.26.up, f32[3,15,8,128]{3,2,1,0:T(8,128)S(1)} %get-tuple-element.30.D1, ...), custom_call_target="tpu_custom_call" | custom-call | bytes 6000000 | tf_op jit(solution)/shard_map/pallas_call | solution.py:632
  57.2 9.3 %all-to-all-done.1.gathered = f32[16,1,128]{2,1,0:T(1,128)S(1)} async-done(((f32[16,1,128]{2,1,0:T(1,128)}), f32[16,1,128]{2,1,0:T(1,128)S(1)}, u32[]{:S(2)}, u32[]{:S(2)}) %all-to-all-start.1) | async-done | bytes 8224 | tf_op jit(solution)/shard_map/all_to_all | solution.py:717
  66.5 0.8 %shard_map.83 = (f32[3,12,8,128]{3,2,1,0:T(8,128)}, f32[12,8,128]{2,1,0:T(8,128)}) custom-call(f32[16,1,128]{2,1,0:T(1,128)S(1)} %all-to-all-done.1.gathered, f32[3,3,20,2,8,128]{5,4,3,2,1,0:T(8,128)S(1)} %get-tuple-element.29.Z.basis, f32[3,12,8,128]{3,2,1,0:T(8,128)S(1)} %shard_map.82.senses), custom_call_target="tpu_custom_call" | custom-call | tf_op jit(solution)/shard_map/pallas_call | solution.py:632
Async XLA Ops:
  1.7 9.4 %collective-permute-start.1 = (f32[28,8,128]{2,1,0:T(8,128)S(1)}, f32[28,8,128]{2,1,0:T(8,128)S(1)}, u32[]{:S(2)}, u32[]{:S(2)}) collective-permute-start(f32[28,8,128]{2,1,0:T(8,128)S(1)} %get-tuple-element.22), channel_id=1, source_target_pairs={{32,64},{96,128},{160,192},{224,256},{288,320},{352,384},{416,448}... | collective-permute-start | bytes 344072 | tf_op jit(solution)/shard_map/ppermute | solution.py:681
  2.4 8.7 %collective-permute-start = (f32[27,8,128]{2,1,0:T(8,128)S(1)}, f32[27,8,128]{2,1,0:T(8,128)S(1)}, u32[]{:S(2)}, u32[]{:S(2)}) collective-permute-start(f32[27,8,128]{2,1,0:T(8,128)S(1)} %get-tuple-element.21), channel_id=1, source_target_pairs={{0,32},{64,96},{128,160},{192,224},{256,288},{320,352},{384,416},{... | collective-permute-start | bytes 331784 | tf_op jit(solution)/shard_map/ppermute | solution.py:682
  11.2 9.4 %collective-permute-start.3 = (f32[128,4,128]{2,1,0:T(4,128)S(1)}, f32[128,4,128]{2,1,0:T(4,128)S(1)}, u32[]{:S(2)}, u32[]{:S(2)}) collective-permute-start(f32[128,4,128]{2,1,0:T(4,128)S(1)} %get-tuple-element.27.rest_0_), channel_id=1, source_target_pairs={{1,2},{3,4},{5,6},{7,8},{9,10},{11,12},{13,14},{15,16},{17,18},{19... | collective-permute-start | bytes 786440 | tf_op jit(solution)/shard_map/ppermute | solution.py:692
  16.6 3.4 %collective-permute-start.2 = (f32[127,4,128]{2,1,0:T(4,128)S(1)}, f32[127,4,128]{2,1,0:T(4,128)S(1)}, u32[]{:S(2)}, u32[]{:S(2)}) collective-permute-start(f32[127,4,128]{2,1,0:T(4,128)S(1)} %shard_map.80), channel_id=1, source_target_pairs={{0,1},{1,0},{2,3},{3,2},{4,5},{5,4},{6,7},{7,6},{8,9},{9,8},{10,11... | collective-permute-start | bytes 780296 | tf_op jit(solution)/shard_map/ppermute | solution.py:693
  39.0 27.5 %all-to-all-start.1 = ((f32[16,1,128]{2,1,0:T(1,128)}), f32[16,1,128]{2,1,0:T(1,128)S(1)}, u32[]{:S(2)}, u32[]{:S(2)}) async-start(f32[16,1,128]{2,1,0:T(1,128)} %broadcast_in_dim.2), calls=%async_computation.1 | async-start | bytes 16384 | tf_op jit(solution)/shard_map/all_to_all | solution.py:717

commit v8 on v7

--- a/solution.py
+++ b/solution.py
@@ -315,7 +315,7 @@
     return result
 
 
-def main_kernel(load, disp, dens, mask, low, up, placed, first, second, Z, SC, D1, sums, G, L0, L1, FR1, DN, MOD, HP, W, DS, SS):
+def main_kernel(load, disp, dens, mask, low, up, placed, first, second, Z, SC, sums, G, L0, L1, FR1, DN, MOD, HP, W, DS, SS):
     gx = lax.axis_index("x") * lax.axis_size("y") + lax.axis_index("y")
     gy = lax.axis_index("z") * lax.axis_size("c") + lax.axis_index("c")
     extent_x = RX * lax.axis_size("x") * lax.axis_size("y")
@@ -327,7 +327,6 @@
     DN[0:5, 16:24] = low[12:17]
     DN[5 : 5 + RX, 16:24] = dens[...]
     DN[5 + RX : 10 + RX, 16:24] = up[16:21]
-    D1[...] = jnp.zeros(D1.shape, F32)
 
     def fill(below, above):
         below_corner, above_corner = below.at[NEAR : NEAR + CORNER], above.at[NEAR : NEAR + CORNER]
@@ -356,15 +355,6 @@
                     r = p if p < 5 else p - 12
                     one = corner[38 + r // 4, r % 4 : r % 4 + 1]
                 DN[p, extra : extra + 1] = one
-        for c in range(3):
-            for p in range(12):
-                n = 12 * c + p
-                D1[c, p + 1, 7:8] = below[63 + n // 4, n % 4 : n % 4 + 1]
-                D1[c, p + 1, 0:2] = above[63 + n // 2, 2 * (n % 2) : 2 * (n % 2) + 2]
-            for m, p in enumerate((0, 13, 14)):
-                n = 3 * c + m
-                D1[c, p, 7:8] = below_corner[41 + n // 4, n % 4 : n % 4 + 1]
-                D1[c, p, 0:2] = above_corner[41 + n // 2, 2 * (n % 2) : 2 * (n % 2) + 2]
 
     even = lax.axis_index("c") == 0
 
@@ -548,7 +538,32 @@
         sums[n] = line
 
 
-def sense_kernel(disp, low, up, D1, Z, SC, senses, U, F, DV):
+def sense_kernel(disp, low, up, first, second, Z, SC, senses, D1, U, F, DV):
+    D1[...] = jnp.zeros(D1.shape, F32)
+
+    def fill(below, below_corner, above, above_corner):
+        for c in range(3):
+            for p in range(12):
+                n = 12 * c + p
+                D1[c, p + 1, 7:8] = below[63 + n // 4, n % 4 : n % 4 + 1]
+                D1[c, p + 1, 0:2] = above[63 + n // 2, 2 * (n % 2) : 2 * (n % 2) + 2]
+            for m, p in enumerate((0, 13, 14)):
+                n = 3 * c + m
+                D1[c, p, 7:8] = below_corner[41 + n // 4, n % 4 : n % 4 + 1]
+                D1[c, p, 0:2] = above_corner[41 + n // 2, 2 * (n % 2) : 2 * (n % 2) + 2]
+
+    even = lax.axis_index("c") == 0
+
+    @pl.when(even)
+    def _():
+        near, corner = second.at[0:NEAR], second.at[NEAR : NEAR + CORNER]
+        fill(near, corner, first.at[0:NEAR], first.at[NEAR : NEAR + CORNER])
+
+    @pl.when(jnp.logical_not(even))
+    def _():
+        near, corner = second.at[0:NEAR], second.at[NEAR : NEAR + CORNER]
+        fill(first.at[0:NEAR], first.at[NEAR : NEAR + CORNER], near, corner)
+
     lane = lax.broadcasted_iota(jnp.int32, (8, NZ), 1)
 
     def disp_of(c, p, t):
@@ -654,6 +669,7 @@
     (6, NI, 24, NZ),
 ]
 SENSE_SCRATCH = [
+    (3, RX + 3, 8, NZ),
     (4, 6, RX + 3, 24, NZ),
     (len(KEYS), RX + 2, 2, 8, NZ),
     (3, RX + 2, 24, NZ),
@@ -693,13 +709,12 @@
     first = lax.ppermute(first, "c", swaps(0, 2))
     close = lax.axis_size("c") * count_x
     far = lax.axis_size("z")
-    basis, scale, outer, sums = call(
+    basis, scale, sums = call(
         main_kernel,
         own + (low, up, placed, first, second),
         [
             (3, 3, NI, 2, 8, NZ),
             (RX + 2, 2, 8, NZ),
-            (3, RX + 3, 8, NZ),
             (close, 1, NZ),
         ],
         MAIN_SCRATCH,
@@ -707,7 +722,7 @@
     )
     senses = call(
         sense_kernel,
-        (own[1], low, up, outer, basis, scale),
+        (own[1], low, up, first, second, basis, scale),
         (3, RX, RY, NZ),
         SENSE_SCRATCH,
         cost=6_000_000,

time: 67.6 us -> 67.5 us (level)
  no operation moved by 1% of the time
where the time goes in v8:
time: 67.5 us; the launch traced here: 67.2 us
  starting transfers between devices  30.9 us (46%)
  blocking collectives  13.4 us (20%)
  waiting for transfers between devices  11.5 us (17%)
  Pallas kernels  10.1 us (15%)
  between operations  0.72 us (1%)
    all_to_all x1, starting transfers between devices, shards(): sums = lax.all_to_all(sums, 'z', 0, 0, tiled=True)  16.2 us
    all_to_all x1, blocking collectives, shards(): sums = lax.all_to_all(sums, ('x', 'y', 'c'), 0, 0, tiled=True)  13.4 us
    all_to_all x1, waiting for transfers between devices, shards(): sums = lax.all_to_all(sums, 'z', 0, 0, tiled=True)  9.25 us
    pallas_call x6, Pallas kernels, call(): pl.pallas_call(kernel, out_shape=[jax.ShapeDtypeStruct(s, F32) for s in s...  9.01 us
    ppermute x1, starting transfers between devices, shards(): first = lax.ppermute(first, ('x', 'y'), swaps(0, count_x))  6.57 us
    ppermute x1, starting transfers between devices, shards(): second = lax.ppermute(second, ('z', 'c'), swaps(1, count_y))  5.31 us
    ppermute x1, starting transfers between devices, shards(): first = lax.ppermute(first, 'c', swaps(0, 2))  2.1 us
  transfers between devices with their start and end apart: 5, of which 4 were waited for; matrix products, arithmetic and copies ran while one was open for 0% of the time, Pallas kernels for 6%

profile of v8, /device:TPU:1, one launch (start us, length us, event | category | flops | bytes accessed | tf_op | source)
XLA Modules:
  0.0 67.2 jit_solution(11866991079332567507)
XLA Ops:
  0.6 1.1 %shard_map.77 = (f32[27,8,128]{2,1,0:T(8,128)S(1)}, f32[28,8,128]{2,1,0:T(8,128)S(1)}, f32[3,12,8,128]{3,2,1,0:T(8,128)S(1)}, f32[3,12,8,128]{3,2,1,0:T(8,128)S(...) custom-call(f32[3,12,8,128]{3,2,1,0:T(8,128)} %refs_0_.1, ...), custom_call_target="tpu_custom_call" | custom-call | tf_op jit(solution)/shard_map/pallas_call | solution.py:688
  1.7 0.7 collective-permute-start.1
  2.4 6.6 %collective-permute-start = (f32[27,8,128]{2,1,0:T(8,128)S(1)}, f32[27,8,128]{2,1,0:T(8,128)S(1)}, u32[]{:S(2)}, u32[]{:S(2)}) collective-permute-start(f32[27,8,128]{2,1,0:T(8,128)S(1)} %get-tuple-element.20), channel_id=1, source_target_pairs={{0,32},{64,96},{128,160},{192,224},{256,288},{320,352},{384,416},{... | collective-permute-start | bytes 331784 | tf_op jit(solution)/shard_map/ppermute | solution.py:698
  9.0 1.7 %shard_map.78._.placed = f32[3,19,2,8,128]{4,3,2,1,0:T(8,128)S(1)} custom-call(s32[3,2048]{1,0:T(4,128)S(1)} %get-tuple-element.22.nodes, f32[3,2048]{1,0:T(4,128)S(1)} %get-tuple-element.23.forces), custom_call_target="tpu_custom_call" | custom-call | tf_op jit(solution)/shard_map/pallas_call | solution.py:647
  10.7 0.4 collective-permute-done.first
  11.1 0.0 collective-permute-done.1.second
  11.1 0.1 shard_map.79
  11.2 5.3 %collective-permute-start.3 = (f32[128,4,128]{2,1,0:T(4,128)S(1)}, f32[128,4,128]{2,1,0:T(4,128)S(1)}, u32[]{:S(2)}, u32[]{:S(2)}) collective-permute-start(f32[128,4,128]{2,1,0:T(4,128)S(1)} %get-tuple-element.26.rest_0_), channel_id=1, source_target_pairs={{1,2},{3,4},{5,6},{7,8},{9,10},{11,12},{13,14},{15,16},{17,18},{19... | collective-permute-start | bytes 786440 | tf_op jit(solution)/shard_map/ppermute | solution.py:708
  16.5 0.1 shard_map.80
  16.6 2.1 %collective-permute-start.2 = (f32[127,4,128]{2,1,0:T(4,128)S(1)}, f32[127,4,128]{2,1,0:T(4,128)S(1)}, u32[]{:S(2)}, u32[]{:S(2)}) collective-permute-start(f32[127,4,128]{2,1,0:T(4,128)S(1)} %shard_map.80), channel_id=1, source_target_pairs={{0,1},{1,0},{2,3},{3,2},{4,5},{5,4},{6,7},{7,6},{8,9},{9,8},{10,11... | collective-permute-start | bytes 780296 | tf_op jit(solution)/shard_map/ppermute | solution.py:709
  18.7 1.3 %collective-permute-done.2.first = f32[127,4,128]{2,1,0:T(4,128)S(1)} collective-permute-done((f32[127,4,128]{2,1,0:T(4,128)S(1)}, f32[127,4,128]{2,1,0:T(4,128)S(1)}, u32[]{:S(2)}, u32[]{:S(2)}) %collective-permute-start.2) | collective-permute-done | bytes 260128 | tf_op jit(solution)/shard_map/ppermute | solution.py:709
  20.0 0.5 collective-permute-done.3.second
  20.5 4.4 %shard_map.81 = (f32[3,3,20,2,8,128]{5,4,3,2,1,0:T(8,128)S(1)}, f32[14,2,8,128]{3,2,1,0:T(8,128)S(1)}, f32[32,1,128]{2,1,0:T(1,128)S(1)}) custom-call(f32[3,12,8,128]{3,2,1,0:T(8,128)S(1)} %get-tuple-element.16.load, f32[3,12,8,128]{3,2,1,0:T(8,128)S(1)} %get-tuple-element.17.disp, f32[12,8,128]{2,1,0:T(8,128)S(1)} %get-tuple-element.18.dens, ...), custom_call_target="tpu_custom_call" | custom-call | tf_op jit(solution)/shard_map/pallas_call | solution.py:647
  24.9 13.4 %all_to_all.10 = f32[32,1,128]{2,1,0:T(1,128)S(1)} all-to-all(f32[32,1,128]{2,1,0:T(1,128)S(1)} %get-tuple-element.27), channel_id=1, replica_groups=mesh['x'=4,'y'=4,'z'=16,'c'=2] {'x','y','c'}, dimensions={0} | all-to-all | bytes 32768 | tf_op jit(solution)/shard_map/all_to_all | solution.py:730
  38.3 0.1 reduce_sum.9
  38.4 0.6 broadcast_in_dim.2
  39.0 16.2 %all-to-all-start.1 = ((f32[16,1,128]{2,1,0:T(1,128)}), f32[16,1,128]{2,1,0:T(1,128)S(1)}, u32[]{:S(2)}, u32[]{:S(2)}) async-start(f32[16,1,128]{2,1,0:T(1,128)} %broadcast_in_dim.2), calls=%async_computation.1 | async-start | bytes 16384 | tf_op jit(solution)/shard_map/all_to_all | solution.py:732
  55.2 2.0 %shard_map.82.senses = f32[3,12,8,128]{3,2,1,0:T(8,128)S(1)} custom-call(f32[3,12,8,128]{3,2,1,0:T(8,128)S(1)} %get-tuple-element.17.disp, f32[20,8,128]{2,1,0:T(8,128)S(1)} %get-tuple-element.24.low, f32[27,8,128]{2,1,0:T(8,128)S(1)} %get-tuple-element.25.up, f32[127,4,128]{2,1,0:T(4,128)S(1)} %collective-permute-done.2.first, ...), custom_call_target="tpu_custom_call" | custom-call | bytes 6000000 | tf_op jit(solution)/shard_map/pallas_call | solution.py:647
  57.2 9.2 %all-to-all-done.1.gathered = f32[16,1,128]{2,1,0:T(1,128)S(1)} async-done(((f32[16,1,128]{2,1,0:T(1,128)}), f32[16,1,128]{2,1,0:T(1,128)S(1)}, u32[]{:S(2)}, u32[]{:S(2)}) %all-to-all-start.1) | async-done | bytes 8224 | tf_op jit(solution)/shard_map/all_to_all | solution.py:732
  66.4 0.8 %shard_map.83 = (f32[3,12,8,128]{3,2,1,0:T(8,128)}, f32[12,8,128]{2,1,0:T(8,128)}) custom-call(f32[16,1,128]{2,1,0:T(1,128)S(1)} %all-to-all-done.1.gathered, f32[3,3,20,2,8,128]{5,4,3,2,1,0:T(8,128)S(1)} %get-tuple-element.28.Z.basis, f32[3,12,8,128]{3,2,1,0:T(8,128)S(1)} %shard_map.82.senses), custom_call_target="tpu_custom_call" | custom-call | tf_op jit(solution)/shard_map/pallas_call | solution.py:647
Async XLA Ops:
  1.7 9.4 %collective-permute-start.1 = (f32[28,8,128]{2,1,0:T(8,128)S(1)}, f32[28,8,128]{2,1,0:T(8,128)S(1)}, u32[]{:S(2)}, u32[]{:S(2)}) collective-permute-start(f32[28,8,128]{2,1,0:T(8,128)S(1)} %get-tuple-element.21), channel_id=1, source_target_pairs={{32,64},{96,128},{160,192},{224,256},{288,320},{352,384},{416,448}... | collective-permute-start | bytes 344072 | tf_op jit(solution)/shard_map/ppermute | solution.py:697
  2.4 8.7 %collective-permute-start = (f32[27,8,128]{2,1,0:T(8,128)S(1)}, f32[27,8,128]{2,1,0:T(8,128)S(1)}, u32[]{:S(2)}, u32[]{:S(2)}) collective-permute-start(f32[27,8,128]{2,1,0:T(8,128)S(1)} %get-tuple-element.20), channel_id=1, source_target_pairs={{0,32},{64,96},{128,160},{192,224},{256,288},{320,352},{384,416},{... | collective-permute-start | bytes 331784 | tf_op jit(solution)/shard_map/ppermute | solution.py:698
  11.2 9.4 %collective-permute-start.3 = (f32[128,4,128]{2,1,0:T(4,128)S(1)}, f32[128,4,128]{2,1,0:T(4,128)S(1)}, u32[]{:S(2)}, u32[]{:S(2)}) collective-permute-start(f32[128,4,128]{2,1,0:T(4,128)S(1)} %get-tuple-element.26.rest_0_), channel_id=1, source_target_pairs={{1,2},{3,4},{5,6},{7,8},{9,10},{11,12},{13,14},{15,16},{17,18},{19... | collective-permute-start | bytes 786440 | tf_op jit(solution)/shard_map/ppermute | solution.py:708
  16.6 3.4 %collective-permute-start.2 = (f32[127,4,128]{2,1,0:T(4,128)S(1)}, f32[127,4,128]{2,1,0:T(4,128)S(1)}, u32[]{:S(2)}, u32[]{:S(2)}) collective-permute-start(f32[127,4,128]{2,1,0:T(4,128)S(1)} %shard_map.80), channel_id=1, source_target_pairs={{0,1},{1,0},{2,3},{3,2},{4,5},{5,4},{6,7},{7,6},{8,9},{9,8},{10,11... | collective-permute-start | bytes 780296 | tf_op jit(solution)/shard_map/ppermute | solution.py:709
  39.0 27.5 %all-to-all-start.1 = ((f32[16,1,128]{2,1,0:T(1,128)}), f32[16,1,128]{2,1,0:T(1,128)S(1)}, u32[]{:S(2)}, u32[]{:S(2)}) async-start(f32[16,1,128]{2,1,0:T(1,128)} %broadcast_in_dim.2), calls=%async_computation.1 | async-start | bytes 16384 | tf_op jit(solution)/shard_map/all_to_all | solution.py:732
